TPU v7x, 128 devices: a whole 4x4x4 slice. The times are simulated.
128 devices in a mesh: dp: 8 (over z_lo, x), frame: 16 (over y, z_hi, core).
Axes of the slice: x: 4, y: 4, z: 4 (z_hi: 2, z_lo: 2; z = z_hi * 2 + z_lo), core: 2. Of those that a mesh axis runs over, the one named last changes fastest.
Arguments:
- frames_in: bfloat16 [8, 16, 128, 1024], P('dp', 'frame'), may hold values from -6 to 6
- bottleneck: bfloat16 [8, 4, 1024], P('dp'), may hold values from -6 to 6
- spatial_entry: bfloat16 [1024, 1536], replicated, may hold values from -2 to 2
- spatial_exit: bfloat16 [1024, 512], replicated, may hold values from -0.25 to 0.25
- temporal_entry: bfloat16 [1024, 1536], replicated, may hold values from -2 to 2
- temporal_exit: bfloat16 [1024, 512], replicated, may hold values from -0.25 to 0.25
- output_grad: bfloat16 [8, 16, 128, 1024], P('dp', 'frame'), may hold values from -6 to 6
- joined_grad: bfloat16 [8, 4, 1024], P('dp'), may hold values from -6 to 6
Outputs:
- frames_delta: bfloat16 [8, 16, 128, 1024], P('dp', 'frame')
- bottleneck_delta: bfloat16 [8, 4, 1024], P('dp')
- spatialin_grad: bfloat16 [1024, 1536], P(('dp', 'frame'))
- spatialout_grad: bfloat16 [1024, 512], P(('dp', 'frame'))
- temporalin_grad: bfloat16 [1024, 1536], P(('dp', 'frame'))
- temporalout_grad: bfloat16 [1024, 512], P(('dp', 'frame'))
All inputs are finite; a program needn't handle non-finite values.
Results may differ from a plain program's by a relative error of at most 0.024.
Values may be sent and summed in bfloat16 or wider, within the bound.
No kernel may reach another device: no remote copies, remote signals or barrier semaphores. Data moves between devices by JAX's collectives and lax.ppermute only.
A program may use at most 64 MiB of HBM per device.

v0:
```python
import math

import jax
import jax.numpy as jnp
from jax import lax
from jax.sharding import Mesh
from jax.sharding import PartitionSpec as P

HEADS = 8
FRAME = ("frame_0", "frame_1", "frame_2")
DP_FRAME = ("dp", "frame_0", "frame_1", "frame_2")


EPSILON = 1e-05


def in_one_piece(arrays, axis, split_dim, concat_dim, along):
    ends, at = ([], 0)
    for a in arrays[:-1]:
        at += a.shape[along]
        ends.append(at)
    both = jnp.concatenate(arrays, axis=along)
    return tuple(
        jnp.split(
            lax.all_to_all(both, axis, split_axis=split_dim, concat_axis=concat_dim, tiled=True),
            ends,
            axis=along,
        )
    )


def in_blocks(array, dim, count):
    before, after = (array.shape[:dim], array.shape[dim + 1 :])
    return jnp.moveaxis(array.reshape(*before, count, -1, *after), dim, 0)


def laid_out(parts, dim):
    shape = list(parts.shape[1:])
    shape[dim] *= parts.shape[0]
    return jnp.moveaxis(parts, 0, dim).reshape(shape)


def exchange_in_order(parts, axes, turns):
    inside = parts.shape[1:]
    out = parts.reshape(*(lax.axis_size(a) for a in axes), *inside)
    for k in turns:
        out = lax.all_to_all(out, axes[k], k, k, tiled=True)
    return out.reshape(-1, *inside)


def core_and_chips(array, groups, turns, split_dim, concat_dim):
    count = lax.axis_size(groups[0]) * lax.axis_size(groups[1])
    parts = in_blocks(array, split_dim, count)
    return laid_out(exchange_in_order(parts, groups, turns), concat_dim)


def copy_for_each(array, axis):
    count = lax.axis_size(axis)
    return lax.all_to_all(
        jnp.broadcast_to(array[None], (count, *array.shape)), axis, 0, 0, tiled=True
    )


def taken_together(array, axis):
    return copy_for_each(array, axis).sum(axis=0)


def side_by_side(arrays, axis, dim, along):
    widths = [a.shape[along] for a in arrays]
    both = jnp.concatenate(arrays, axis=along)
    out = lax.psum_scatter(both, axis, scatter_dimension=dim, tiled=True)
    return tuple(jnp.split(out, [sum(widths[:k]) for k in range(1, len(widths))], axis=along))


def sum_at_owner(array, axis, dim):
    count = lax.axis_size(axis)
    parts = lax.all_to_all(in_blocks(array, dim, count), axis, 0, 0, tiled=True)
    return jnp.sum(parts.astype(jnp.float32), axis=0)


def sent_together(arrays, axis, dim, along):
    both = jnp.concatenate(arrays, axis=along)
    out, at, finished = (sum_at_owner(both, axis, dim), 0, [])
    for a in arrays:
        finished.append(lax.slice_in_dim(out, at, at + a.shape[along], axis=along))
        at += a.shape[along]
    return tuple(finished)


def normalize(inputs):
    widened = inputs.astype(jnp.float32)
    centred = widened - jnp.mean(widened, axis=-1, keepdims=True)
    inverse = lax.rsqrt(jnp.mean(centred * centred, axis=-1, keepdims=True) + EPSILON)
    return (centred * inverse, inverse)


def attend(inputs, entry_weight, head_count):
    normed, inverse = normalize(inputs)
    normed_low = normed.astype(jnp.bfloat16)
    mixture = jnp.dot(normed_low, entry_weight, preferred_element_type=jnp.float32).astype(
        jnp.bfloat16
    )
    lead_count, seq_length, side_count = (inputs.shape[0], inputs.shape[1], inputs.shape[2])
    head_width = entry_weight.shape[1] // 3
    head_size = head_width // head_count
    pieces = mixture.reshape(lead_count, seq_length, side_count, 3, head_count, head_size)
    queries = pieces[:, :, :, 0]
    key_heads = pieces[:, :, :, 1]
    values = pieces[:, :, :, 2]
    factor = 1.0 / math.sqrt(head_size)
    scores = (
        jnp.einsum("albhe,ambhe->abhlm", queries, key_heads, preferred_element_type=jnp.float32)
        * factor
    )
    scores = scores - jnp.max(scores, axis=-1, keepdims=True)
    expon = jnp.exp(scores)
    softmax_weights = expon / jnp.sum(expon, axis=-1, keepdims=True)
    softmax_low = softmax_weights.astype(jnp.bfloat16)
    attended = jnp.einsum(
        "abhlm,ambhe->albhe", softmax_low, values, preferred_element_type=jnp.float32
    ).astype(jnp.bfloat16)
    attended = attended.reshape(lead_count, seq_length, side_count, head_width)
    return (
        normed,
        inverse,
        normed_low,
        queries,
        key_heads,
        values,
        softmax_weights,
        softmax_low,
        attended,
    )


def project_out(inputs, attended, exit_weight):
    return inputs.astype(jnp.float32) + lax.dot_general(
        attended, exit_weight, (((3,), (1,)), ((), ())), preferred_element_type=jnp.float32
    )


def backward(cotangent, saved, entry_weight, exit_weight, head_count):
    (
        normed,
        inverse,
        normed_low,
        queries,
        key_heads,
        values,
        softmax_weights,
        softmax_low,
        attended,
    ) = saved
    lead_count, seq_length, side_count = (
        cotangent.shape[0],
        cotangent.shape[1],
        cotangent.shape[2],
    )
    head_width = exit_weight.shape[1]
    head_size = head_width // head_count
    factor = 1.0 / math.sqrt(head_size)
    rows_dims = (((0, 1, 2), (0, 1, 2)), ((), ()))
    exit_grad = lax.dot_general(cotangent, attended, rows_dims, preferred_element_type=jnp.float32)
    attended_grad = lax.dot_general(
        cotangent, exit_weight, (((3,), (0,)), ((), ())), preferred_element_type=jnp.float32
    ).astype(jnp.bfloat16)
    attended_grad = attended_grad.reshape(lead_count, seq_length, side_count, head_count, head_size)
    softmax_grad = jnp.einsum(
        "albhe,ambhe->abhlm", attended_grad, values, preferred_element_type=jnp.float32
    )
    values_grad = jnp.einsum(
        "abhlm,albhe->ambhe", softmax_low, attended_grad, preferred_element_type=jnp.float32
    )
    centre = jnp.sum(softmax_weights * softmax_grad, axis=-1, keepdims=True)
    scores_grad = (softmax_weights * (softmax_grad - centre) * factor).astype(jnp.bfloat16)
    queries_grad = jnp.einsum(
        "abhlm,ambhe->albhe", scores_grad, key_heads, preferred_element_type=jnp.float32
    )
    keys_grad = jnp.einsum(
        "abhlm,albhe->ambhe", scores_grad, queries, preferred_element_type=jnp.float32
    )
    mixture_grad = jnp.stack([queries_grad, keys_grad, values_grad], axis=3).astype(jnp.bfloat16)
    mixture_grad = mixture_grad.reshape(lead_count, seq_length, side_count, 3 * head_width)
    entry_grad = lax.dot_general(
        normed_low, mixture_grad, rows_dims, preferred_element_type=jnp.float32
    )
    normed_grad = lax.dot_general(
        mixture_grad, entry_weight, (((3,), (1,)), ((), ())), preferred_element_type=jnp.float32
    )
    inner_term = (
        normed_grad
        - jnp.mean(normed_grad, axis=-1, keepdims=True)
        - normed * jnp.mean(normed_grad * normed, axis=-1, keepdims=True)
    )
    inputs_grad = cotangent.astype(jnp.float32) + inverse * inner_term
    return (inputs_grad, entry_grad, exit_grad)


def per_device(
    frames_in,
    bottleneck,
    spatial_entry,
    spatial_exit,
    temporal_entry,
    temporal_exit,
    output_grad,
    joined_grad,
):
    clip_count, frames_local, patch_count, model_width = frames_in.shape
    bottle_rows = bottleneck.shape[1]
    frame_groups = lax.axis_size(FRAME)
    data_groups = lax.axis_size("dp")
    seq_rows = patch_count + bottle_rows
    tokens_in = jnp.concatenate([frames_in, bottleneck[:, None]], axis=2)
    sequences = tokens_in.reshape(clip_count * frames_local, seq_rows, 1, model_width)
    spatial_saved = attend(sequences, spatial_entry, HEADS)
    block_out = project_out(sequences, spatial_saved[8], spatial_exit)
    states = block_out.reshape(clip_count, frames_local, seq_rows, model_width)[
        :, :, :patch_count
    ].astype(jnp.bfloat16)
    states_moved, output_moved = in_one_piece((states, output_grad), FRAME, 2, 1, 0)
    temporal_saved = attend(states_moved, temporal_entry, HEADS)
    states_grad, temporal_in, temporal_out = backward(
        output_moved, temporal_saved, temporal_entry, temporal_exit, HEADS
    )
    state_grads = states_grad.astype(jnp.bfloat16)
    grad_factor = 1.0 / math.sqrt(
        clip_count * frames_local * patch_count * data_groups * frame_groups
    )
    state_grads_back = core_and_chips(
        state_grads, (("frame_0", "frame_1"), "frame_2"), (1, 0), 1, 2
    )
    frames_total = frames_local * frame_groups
    joined_rows = (joined_grad.astype(jnp.float32) / frames_total).astype(jnp.bfloat16)
    cotangent = jnp.concatenate([state_grads_back, joined_rows[:, None]], axis=2)
    cotangent = cotangent.reshape(clip_count * frames_local, seq_rows, 1, model_width)
    tokens_grad, spatial_in, spatial_out = backward(
        cotangent, spatial_saved, spatial_entry, spatial_exit, HEADS
    )
    tokens_grad = tokens_grad.reshape(clip_count, frames_local, seq_rows, model_width)
    frames_delta = tokens_grad[:, :, :patch_count].astype(jnp.bfloat16)
    local_bottle = jnp.sum(tokens_grad[:, :, patch_count:], axis=1)
    bottleneck_delta = taken_together(local_bottle, FRAME).astype(jnp.bfloat16)
    partial_sums = tuple(
        (
            part.astype(jnp.float32)
            for part in side_by_side(
                (
                    spatial_in.astype(jnp.bfloat16),
                    spatial_out.astype(jnp.bfloat16),
                    temporal_in.astype(jnp.bfloat16),
                    temporal_out.astype(jnp.bfloat16),
                ),
                "dp",
                0,
                1,
            )
        )
    )
    summed = sent_together(
        (
            partial_sums[0].astype(jnp.bfloat16),
            partial_sums[1].astype(jnp.bfloat16),
            partial_sums[2].astype(jnp.bfloat16),
            partial_sums[3].astype(jnp.bfloat16),
        ),
        FRAME,
        0,
        1,
    )
    spatialin_grad = (summed[0] * grad_factor).astype(jnp.bfloat16)
    spatialout_grad = (summed[1] * grad_factor).astype(jnp.bfloat16)
    temporalin_grad = (summed[2] * grad_factor).astype(jnp.bfloat16)
    temporalout_grad = (summed[3] * grad_factor).astype(jnp.bfloat16)
    return (
        frames_delta,
        bottleneck_delta,
        spatialin_grad,
        spatialout_grad,
        temporalin_grad,
        temporalout_grad,
    )


def solution(mesh):
    finer = Mesh(
        mesh.devices.reshape(mesh.shape["dp"], 4, 2, 2), ("dp", "frame_0", "frame_1", "frame_2")
    )
    in_specs = (
        P("dp", FRAME, None, None),
        P("dp", None, None),
        P(),
        P(),
        P(),
        P(),
        P("dp", FRAME, None, None),
        P("dp", None, None),
    )
    out_specs = (
        P("dp", FRAME, None, None),
        P("dp", None, None),
        P(DP_FRAME, None),
        P(DP_FRAME, None),
        P(DP_FRAME, None),
        P(DP_FRAME, None),
    )
    return jax.shard_map(
        per_device, mesh=finer, in_specs=in_specs, out_specs=out_specs, check_vma=False
    )
```

profile of v0, /device:TPU:0, one launch (start us, length us, event | category | flops | bytes accessed | tf_op | source)
XLA Modules:
  0.0 255.9 jit_solution(6899677484041469461)
XLA Ops:
  7.2 1.2 convert_reduce_fusion.1
  8.4 1.2 fusion.50
  9.7 2.4 convolution_convert_fusion.1
  12.0 2.2 copy.192
  14.2 2.6 %fusion.115 = (f32[8,132]{1,0:T(8,128)S(1)}, f32[8,132,132]{1,2,0:T(8,128)}) fusion(bf16[1,132,1,3,8,64]{1,5,4,3,2,0:T(8,128)(2,1)} %bitcast.231), kind=kOutput, calls=%fused_computation.162 | convolution fusion | flops 18260484 | bytes 1086080 | tf_op jit(solution)/shard_map/sub | solution.py:115
  16.8 1.7 convolution_convert_fusion.4
  18.5 0.5 fusion.24
  19.2 0.4 copy-done.17
  19.6 1.3 copy.161
  21.0 8.0 %all-to-all-start = ((bf16[2,1,128,1024]{3,0,1,2:T(2,128)(2,1)}), bf16[2,1,128,1024]{3,0,1,2:T(2,128)(2,1)}, u32[]{:S(2)}, u32[]{:S(2)}) async-start(bf16[2,1,128,1024]{3,0,1,2:T(2,128)(2,1)} %copy.161), calls=%async_computation | async-start | bytes 1048576 | tf_op jit(solution)/shard_map/all_to_all | solution.py:25
  29.0 0.6 fusion.96
  29.6 11.8 %all-to-all-done = bf16[2,1,128,1024]{3,0,1,2:T(2,128)(2,1)} async-done(((bf16[2,1,128,1024]{3,0,1,2:T(2,128)(2,1)}), bf16[2,1,128,1024]{3,0,1,2:T(2,128)(2,1)}, u32[]{:S(2)}, u32[]{:S(2)}) %all-to-all-start) | async-done | bytes 524320 | tf_op jit(solution)/shard_map/all_to_all | solution.py:25
  41.4 3.0 %fusion.114 = (bf16[1,1,128,1024]{3,0,1,2:T(2,128)(2,1)}, bf16[1,1,128,1024]{3,0,1,2:T(2,128)(2,1)S(1)}) fusion(bf16[2,1,128,1024]{3,0,1,2:T(2,128)(2,1)} %all-to-all-done), kind=kLoop, calls=%fused_computation.161 | loop fusion | bytes 1048576 | tf_op jit(solution)/shard_map/split | solution.py:24
  44.4 0.8 convert_reduce_fusion.2
  45.3 1.2 fusion.56
  46.5 0.7 rsqrt.22
  47.2 1.7 convolution_convert_fusion.6
  48.9 0.9 reshape.627
  49.8 3.4 %fusion.8 = bf16[16,8,1536]{2,1,0:T(8,128)(2,1)} fusion(bf16[1024,1536]{1,0:T(8,128)(2,1)} %param.12, bf16[1,1,128,1024]{3,2,1,0:T(8,128)(2,1)} %get-tuple-element.11, f32[16,8]{1,0:T(8,128)S(1)} %div.56, f32[16,8]{1,0:T(8,128)} %rsqrt.22), kind=kOutput, calls=%fused_computation.12 | convolution fusion | flops 403374080 | bytes 3802112 | tf_op jit(solution)/shard_map/dot_general | solution.py:100
  53.2 2.3 reshape.624
  55.5 2.0 fusion.113
  57.5 1.2 fusion.86
  58.7 2.3 fusion.116
  61.1 2.1 convolution_bitcast_fusion
  63.2 2.8 %convolution_bitcast_fusion.1 = bf16[1,16,8,1,8,64]{5,1,4,2,3,0:T(8,128)(2,1)} fusion(f32[8,8,16,16]{2,3,1,0:T(8,128)} %fusion.86, bf16[1,16,8,1,8,64]{5,4,3,2,1,0:T(8,128)(2,1)} %get-tuple-element.13, f32[8,8,16,16]{2,3,1,0:T(8,128)} %get-tuple-element.24, f32[8,8,16]{2,1,0:T(8,128)S(1)} %get-tuple-element.23), kind=kOutput, calls=%fused_computation.29 | convolution fusion | flops 2212879 | bytes 397312 | tf_op jit(solution)/shard_map/abhlm,albhe->ambhe/dot_general | solution.py:179
  66.0 2.7 %convolution_bitcast_fusion.5 = bf16[1,16,8,1,8,64]{5,1,4,2,3,0:T(8,128)(2,1)} fusion(f32[8,8,16,16]{2,3,1,0:T(8,128)} %fusion.86, bf16[1,16,8,1,8,64]{5,4,3,2,1,0:T(8,128)(2,1)} %get-tuple-element.14, f32[8,8,16,16]{2,3,1,0:T(8,128)} %get-tuple-element.24, f32[8,8,16]{2,1,0:T(8,128)S(1)} %get-tuple-element.23), kind=kOutput, calls=%fused_computation.33 | convolution fusion | flops 2212879 | bytes 397312 | tf_op jit(solution)/shard_map/abhlm,ambhe->albhe/dot_general | solution.py:176
  68.8 2.2 fusion.25
  71.0 0.2 maximum_convert_fusion
  71.2 1.1 copy.170
  72.3 2.4 convert_element_type.285
  74.7 4.0 %fusion.112 = (f32[16,8]{1,0:T(8,128)S(1)}, f32[16,8]{1,0:T(8,128)S(1)}, f32[16,8,1024]{2,1,0:T(8,128)}) fusion(f32[16,8]{1,0:T(8,128)S(1)} %copy-done.21, f32[16,8]{1,0:T(8,128)S(1)} %div.56, bf16[1,1,128,1024]{3,2,1,0:T(8,128)(2,1)} %get-tuple-element.11, bf16[16,8,1536]{2,1,0:T(8,128)(2,1)} %convert_element_type.285, bf16[1024,1536]{1,0:T(8,128)(2,1)} %param.12), kind=kOutput, calls=%fused_computation.159 | convolution fusion | flops 403439360 | bytes 4327424 | tf_op jit(solution)/shard_map/dot_general | solution.py:187
  78.8 2.8 %bitcast_convert_fusion = bf16[1024,1536]{1,0:T(8,128)(2,1)} fusion(bf16[16,8,1536]{2,1,0:T(8,128)(2,1)S(1)} %copy-done.7, bf16[1,1,128,1024]{3,2,1,0:T(8,128)(2,1)S(1)} %copy-done.2, f32[128]{0:T(128)S(1)} %copy-done.33, f32[128]{0:T(128)S(1)} %copy-done.31), kind=kOutput, calls=%fused_computation.5 | convolution fusion | flops 404750336 | bytes 3802112 | tf_op jit(solution)/shard_map/dot_general | solution.py:184
  81.5 0.8 copy.181
  82.3 1.8 reshape.632
  84.1 1.5 fusion.67
  85.7 4.1 %all_to_all.29 = bf16[8,2,1,1,8,1024]{5,4,0,3,2,1:T(8,128)(2,1)S(1)} all-to-all(bf16[8,2,1,1,8,1024]{5,4,0,3,2,1:T(8,128)(2,1)S(1)} %copy.171), channel_id=1, replica_groups=mesh['dp'=8,'frame_0'=4,'frame_1'=2,'frame_2'=2] {'frame_2'}, dimensions={1} | all-to-all | bytes 524288 | tf_op jit(solution)/shard_map/all_to_all | solution.py:47
  89.8 0.7 copy.172
  90.5 4.0 %all-to-all-start.2 = ((bf16[8,2,1,1,8,1024]{5,4,1,3,2,0:T(8,128)(2,1)}), bf16[8,2,1,1,8,1024]{5,4,1,3,2,0:T(8,128)(2,1)}, u32[]{:S(2)}, u32[]{:S(2)}) async-start(bf16[8,2,1,1,8,1024]{5,4,1,3,2,0:T(8,128)(2,1)} %copy.172), calls=%async_computation.2 | async-start | bytes 524288 | tf_op jit(solution)/shard_map/all_to_all | solution.py:47
  94.5 0.2 reduce-scatter.2.cloned.1.call-start
  94.8 2.5 bitcast_convert_fusion.1
  97.3 6.3 %all-to-all-done.2 = bf16[8,2,1,1,8,1024]{5,4,1,3,2,0:T(8,128)(2,1)} async-done(((bf16[8,2,1,1,8,1024]{5,4,1,3,2,0:T(8,128)(2,1)}), bf16[8,2,1,1,8,1024]{5,4,1,3,2,0:T(8,128)(2,1)}, u32[]{:S(2)}, u32[]{:S(2)}) %all-to-all-start.2) | async-done | bytes 262176 | tf_op jit(solution)/shard_map/all_to_all | solution.py:47
  103.6 1.7 convolution_convert_fusion.5
  105.3 2.5 convolution_convert_fusion.2
  107.7 0.8 copy.193
  108.6 2.4 convolution_bitcast_fusion.2
  111.0 2.3 fusion.87
  113.3 3.7 %convolution_bitcast_fusion.4 = bf16[1,132,1,1,8,64]{1,5,4,3,2,0:T(8,128)(2,1)} fusion(f32[8,132,132]{1,2,0:T(8,128)} %fusion.87, bf16[1,132,1,3,8,64]{1,5,4,3,2,0:T(8,128)(2,1)} %bitcast.234, f32[8,132,132]{1,2,0:T(8,128)} %get-tuple-element.22, f32[8,132]{1,0:T(8,128)S(1)} %copy-done.35), kind=kOutput, calls=%fused_computation.32 | convolution fusion | flops 18819108 | bytes 4870144 | tf_op jit(solution)/shard_map/abhlm,ambhe->albhe/dot_general | solution.py:176
  117.0 3.7 %convolution_bitcast_fusion.3 = bf16[1,132,1,1,8,64]{1,5,4,3,2,0:T(8,128)(2,1)} fusion(f32[8,132,132]{1,2,0:T(8,128)} %fusion.87, bf16[1,132,1,3,8,64]{1,5,4,3,2,0:T(8,128)(2,1)} %bitcast.235, f32[8,132,132]{1,2,0:T(8,128)} %get-tuple-element.22, f32[8,132]{1,0:T(8,128)S(1)} %copy-done.35), kind=kOutput, calls=%fused_computation.31 | convolution fusion | flops 18819108 | bytes 4870144 | tf_op jit(solution)/shard_map/abhlm,albhe->ambhe/dot_general | solution.py:179
  120.6 1.4 maximum_convert_fusion.1
  122.0 0.9 copy-done.6
  122.9 1.2 convolution_convert_fusion
  124.1 1.0 copy-done.5
  125.1 3.8 %pad_maximum_fusion = bf16[1024,4096]{1,0:T(8,128)(2,1)} fusion(bf16[1024,512]{1,0:T(8,128)(2,1)S(1)} %copy-done.9, bf16[1024,1536]{1,0:T(8,128)(2,1)S(1)} %copy-done.5, bf16[1024,512]{1,0:T(8,128)(2,1)S(1)} %copy-done.3, bf16[1024,1536]{1,0:T(8,128)(2,1)S(1)} %convolution_convert_fusion), kind=kLoop, calls=%fused_computation.4 | loop fusion | flops 33554432 | bytes 16777216 | tf_op jit(solution)/shard_map/concatenate | solution.py:70
  129.0 2.5 fusion.111
  131.5 1.2 fusion.47
  132.7 0.8 copy-done.8
  133.6 88.9 %all_to_all.30 = f32[16,1,4,1024]{3,2,1,0:T(4,128)S(1)} all-to-all(f32[16,1,4,1024]{3,2,1,0:T(4,128)S(1)} %broadcast_in_dim.11), channel_id=1, replica_groups=mesh['dp'=8,'frame_0'=4,'frame_1'=2,'frame_2'=2] {'frame_0','frame_1','f..., dimensions={0} | all-to-all | bytes 524288 | tf_op jit(solution)/shard_map/all_to_all | solution.py:59
  222.5 6.0 %all-to-all-start.4 = ((bf16[16,8,4096]{2,1,0:T(8,128)(2,1)}), bf16[16,8,4096]{2,1,0:T(8,128)(2,1)}, u32[]{:S(2)}, u32[]{:S(2)}) async-start(bf16[16,8,4096]{2,1,0:T(8,128)(2,1)} %bitcast.239), calls=%async_computation.5 | async-start | bytes 2097152 | tf_op jit(solution)/shard_map/all_to_all | solution.py:77
  228.4 1.8 slice.102
  230.2 0.7 reduce_sum.142
  230.8 15.6 %all-to-all-done.4 = bf16[16,8,4096]{2,1,0:T(8,128)(2,1)} async-done(((bf16[16,8,4096]{2,1,0:T(8,128)(2,1)}), bf16[16,8,4096]{2,1,0:T(8,128)(2,1)}, u32[]{:S(2)}, u32[]{:S(2)}) %all-to-all-start.4) | async-done | bytes 1048608 | tf_op jit(solution)/shard_map/all_to_all | solution.py:77
  246.4 1.4 convert_reduce_fusion
  247.8 0.6 fusion.94
  248.4 0.6 fusion.92
  (83 shorter events, 0.5 us)
Async XLA Ops:
  7.2 2.5 copy-start
  8.4 3.6 %copy-start.25 = (f32[132]{0:T(256)}, f32[132]{0:T(256)S(1)}, u32[]{:S(2)}) copy-start(f32[132]{0:T(256)S(1)} %broadcast_multiply_fusion.4) | copy-start | bytes 1588
  9.7 2.4 copy-start.27
  16.8 1.7 copy-start.34
  16.8 1.7 copy-start.1
  16.8 1.7 copy-start.4
  16.8 1.7 copy-start.15
  18.5 0.7 copy-start.11
  18.5 1.0 copy-start.17
  19.6 9.4 %copy-start.29 = (bf16[1,4,1024]{2,1,0:T(4,128)(2,1)S(1)}, bf16[1,4,1024]{2,1,0:T(4,128)(2,1)}, u32[]{:S(2)}) copy-start(bf16[1,4,1024]{2,1,0:T(4,128)(2,1)} %param.15) | copy-start | bytes 24580
  21.0 20.4 %all-to-all-start = ((bf16[2,1,128,1024]{3,0,1,2:T(2,128)(2,1)}), bf16[2,1,128,1024]{3,0,1,2:T(2,128)(2,1)}, u32[]{:S(2)}, u32[]{:S(2)}) async-start(bf16[2,1,128,1024]{3,0,1,2:T(2,128)(2,1)} %copy.161), calls=%async_computation | async-start | bytes 1048576 | tf_op jit(solution)/shard_map/all_to_all | solution.py:25
  45.2 2.0 copy-start.30
  46.5 0.7 copy-start.32
  55.5 2.0 copy-start.13
  57.5 1.2 copy-start.14
  68.8 2.2 copy-start.18
  68.8 2.2 copy-start.19
  68.8 2.2 copy-start.20
  71.2 3.5 %copy-start.21 = (f32[16,8]{1,0:T(8,128)S(1)}, f32[16,8]{1,0:T(8,128)}, u32[]{:S(2)}) copy-start(f32[16,8]{1,0:T(8,128)} %rsqrt.22) | copy-start | bytes 1540
  74.7 4.1 %copy-start.2 = (bf16[1,1,128,1024]{3,2,1,0:T(8,128)(2,1)S(1)}, bf16[1,1,128,1024]{3,2,1,0:T(8,128)(2,1)}, u32[]{:S(2)}) copy-start(bf16[1,1,128,1024]{3,2,1,0:T(8,128)(2,1)} %get-tuple-element.11) | copy-start | bytes 786436
  74.7 4.1 %copy-start.7 = (bf16[16,8,1536]{2,1,0:T(8,128)(2,1)S(1)}, bf16[16,8,1536]{2,1,0:T(8,128)(2,1)}, u32[]{:S(2)}) copy-start(bf16[16,8,1536]{2,1,0:T(8,128)(2,1)} %convert_element_type.285) | copy-start | bytes 1179652
  74.7 4.1 %copy-start.31 = (f32[128]{0:T(128)S(1)}, f32[128]{0:T(128)}, u32[]{:S(2)}) copy-start(f32[128]{0:T(128)} %copy-done.30) | copy-start | bytes 1540
  74.7 4.1 %copy-start.33 = (f32[128]{0:T(128)S(1)}, f32[128]{0:T(128)}, u32[]{:S(2)}) copy-start(f32[128]{0:T(128)} %copy-done.32) | copy-start | bytes 1540
  78.8 2.8 %copy-start.16 = (bf16[1,16,8,8,64]{4,1,3,2,0:T(8,128)(2,1)S(1)}, bf16[1,16,8,8,64]{4,1,3,2,0:T(8,128)(2,1)}, u32[]{:S(2)}) copy-start(bf16[1,16,8,8,64]{4,1,3,2,0:T(8,128)(2,1)} %fusion.25) | copy-start | bytes 393220
  85.7 9.1 %copy-start.24 = (bf16[16,8,512]{2,1,0:T(8,128)(2,1)S(1)}, bf16[16,8,512]{2,1,0:T(8,128)(2,1)}, u32[]{:S(2)}) copy-start(bf16[16,8,512]{2,1,0:T(8,128)(2,1)} %reshape.632) | copy-start | bytes 393220
  90.5 13.1 %all-to-all-start.2 = ((bf16[8,2,1,1,8,1024]{5,4,1,3,2,0:T(8,128)(2,1)}), bf16[8,2,1,1,8,1024]{5,4,1,3,2,0:T(8,128)(2,1)}, u32[]{:S(2)}, u32[]{:S(2)}) async-start(bf16[8,2,1,1,8,1024]{5,4,1,3,2,0:T(8,128)(2,1)} %copy.172), calls=%async_computation.2 | async-start | bytes 524288 | tf_op jit(solution)/shard_map/all_to_all | solution.py:47
  94.5 127.9 %reduce-scatter.2.cloned.1.call-start = ((), (), s32[]{:S(2)}) async-start(), calls=%async_computation.6 | async-start | bytes 9437184 | tf_op jit(solution)/shard_map/reduce_scatter | solution.py:71
  103.6 1.7 copy-start.12
  103.6 1.7 copy-start.22
  108.6 2.4 copy-start.10
  111.0 2.3 copy-start.35
  120.6 2.3 copy-start.26
  120.6 2.3 copy-start.28
  120.6 3.5 %copy-start.9 = (bf16[1024,512]{1,0:T(8,128)(2,1)S(1)}, bf16[1024,512]{1,0:T(8,128)(2,1)}, u32[]{:S(2)}) copy-start(bf16[1024,512]{1,0:T(8,128)(2,1)} %bitcast_convert_fusion.1) | copy-start | bytes 3145732
  122.0 0.9 copy-start.6
  122.9 1.2 copy-start.3
  122.9 2.2 copy-start.5
  129.0 2.5 copy-start.23
  132.7 0.8 copy-start.8
  222.5 24.0 %all-to-all-start.4 = ((bf16[16,8,4096]{2,1,0:T(8,128)(2,1)}), bf16[16,8,4096]{2,1,0:T(8,128)(2,1)}, u32[]{:S(2)}, u32[]{:S(2)}) async-start(bf16[16,8,4096]{2,1,0:T(8,128)(2,1)} %bitcast.239), calls=%async_computation.5 | async-start | bytes 2097152 | tf_op jit(solution)/shard_map/all_to_all | solution.py:77
Sparse Core Ops, SparseCore 0:
  129.1 92.5 reduce-scatter.1
where the time goes:
time: 258 us; the launch traced here: 256 us
  blocking collectives  93 us (36%)
  matrix products  54.8 us (21%)
  waiting for transfers between devices  33.7 us (13%)
  local copies, waits for them, and re-layouts  25.3 us (10%)
  starting transfers between devices  18.2 us (7%)
  other arithmetic  16.5 us (6%)
  between operations  14.4 us (6%)
    all_to_all x1, blocking collectives, copy_for_each(): lax.all_to_all(jnp.broadcast_to(array[None], (count, *array.shape)), axis...  88.9 us
    all_to_all x1, waiting for transfers between devices, sum_at_owner(): parts = lax.all_to_all(in_blocks(array, dim, count), axis, 0, 0, tiled=True)  15.6 us
    all_to_all x1, waiting for transfers between devices, in_one_piece(): lax.all_to_all(both, axis, split_axis=split_dim, concat_axis=concat_dim,...  11.8 us
    all_to_all x1, starting transfers between devices, in_one_piece(): lax.all_to_all(both, axis, split_axis=split_dim, concat_axis=concat_dim,...  8.02 us
    dot_general x2, matrix products, backward(): lax.dot_general(mixture_grad, entry_weight, (((3,), (1,)), ((), ())), pre...  6.51 us
    dot_general x2, matrix products, backward(): jnp.einsum('abhlm,albhe->ambhe', scores_grad, queries, preferred_element_...  6.44 us
    dot_general x2, matrix products, backward(): jnp.einsum('abhlm,ambhe->albhe', scores_grad, key_heads, preferred_elemen...  6.41 us
    all_to_all x1, waiting for transfers between devices, exchange_in_order(): out = lax.all_to_all(out, axes[k], k, k, tiled=True)  6.26 us
  transfers between devices with their start and end apart: 4, of which 3 were waited for; matrix products, arithmetic and copies ran while one was open for 4% of the time, Pallas kernels for 0%

commit v1 on v0

v1 whole, which is shorter than its diff:
```python
import functools
import math

import jax
import jax.numpy as jnp
from jax import lax
from jax.experimental import pallas as pl
from jax.experimental.pallas import tpu as pltpu
from jax.sharding import Mesh
from jax.sharding import PartitionSpec as P

HEADS = 8
EPSILON = 1e-05
FRAME = ("y", "zh", "c")
CHIPS = ("zl", "x", "y", "zh")
ALL = ("zl", "x", "y", "zh", "c")
BF = jnp.bfloat16
F32 = jnp.float32

NN = (((1,), (0,)), ((), ()))
NT = (((1,), (1,)), ((), ()))
TN = (((0,), (0,)), ((), ()))


def mm(a, b, dims):
    return lax.dot_general(a, b, dims, preferred_element_type=F32)


def normalize(u):
    centred = u - jnp.mean(u, axis=-1, keepdims=True)
    inverse = lax.rsqrt(jnp.mean(centred * centred, axis=-1, keepdims=True) + EPSILON)
    return centred * inverse, inverse


def half_masks(size):
    lane = lax.broadcasted_iota(jnp.int32, (1, 2 * size), 1)
    low = (lane < size).astype(F32)
    return low.astype(BF), (1.0 - low).astype(BF)


def attention_forward(mix_ref, keep, masks, save, put):
    width = 2 * (mix_ref.shape[1] // 3 // HEADS)
    side = mix_ref.shape[1] // 3
    factor = 1.0 / math.sqrt(width // 2)
    for p in range(HEADS // 2):
        q2 = mix_ref[:, p * width : (p + 1) * width]
        k2 = mix_ref[:, side + p * width : side + (p + 1) * width]
        v2 = mix_ref[:, 2 * side + p * width : 2 * side + (p + 1) * width]
        total = None
        for h in range(2):
            scores = mm(q2 * masks[h], k2, NT) * factor
            scores = jnp.where(keep, scores, -jnp.inf)
            scores = scores - jnp.max(scores, axis=-1, keepdims=True)
            expon = jnp.exp(scores)
            weights = expon / jnp.sum(expon, axis=-1, keepdims=True)
            save(2 * p + h, weights)
            part = mm(weights.astype(BF), v2 * masks[h], NN)
            total = part if total is None else total + part
        put(p, width, total.astype(BF))


def attention_backward(mix_ref, load, d_att, masks, put):
    width = 2 * (mix_ref.shape[1] // 3 // HEADS)
    side = mix_ref.shape[1] // 3
    factor = 1.0 / math.sqrt(width // 2)
    for p in range(HEADS // 2):
        q2 = mix_ref[:, p * width : (p + 1) * width]
        k2 = mix_ref[:, side + p * width : side + (p + 1) * width]
        v2 = mix_ref[:, 2 * side + p * width : 2 * side + (p + 1) * width]
        d2 = d_att[:, p * width : (p + 1) * width]
        dq = dk = dv = None
        for h in range(2):
            dh = d2 * masks[h]
            weights = load(2 * p + h)
            grad = mm(dh, v2, NT)
            centre = jnp.sum(weights * grad, axis=-1, keepdims=True)
            ds = (weights * (grad - centre) * factor).astype(BF)
            a = mm(ds, k2 * masks[h], NN)
            b = mm(ds, q2 * masks[h], TN)
            c = mm(weights.astype(BF), dh, TN)
            dq = a if dq is None else dq + a
            dk = b if dk is None else dk + b
            dv = c if dv is None else dv + c
        put(p * width, width, dq.astype(BF))
        put(side + p * width, width, dk.astype(BF))
        put(2 * side + p * width, width, dv.astype(BF))


def inputs_gradient(c, normed, inverse, d_normed):
    inner = (
        d_normed
        - jnp.mean(d_normed, axis=-1, keepdims=True)
        - normed * jnp.mean(d_normed * normed, axis=-1, keepdims=True)
    )
    return c.astype(F32) + inverse * inner


def picker(half):
    row = lax.broadcasted_iota(jnp.int32, (256, 128), 0)
    col = lax.broadcasted_iota(jnp.int32, (256, 128), 1)
    source = (col // 8) * 16 + half * 8 + col % 8
    return (row == source).astype(F32).astype(BF)


def pick(values, chosen, out_ref, at):
    for b in range(values.shape[1] // 256):
        part = mm(values[:, 256 * b : 256 * (b + 1)], chosen, NN)
        out_ref[:, at + 128 * b : at + 128 * (b + 1)] = part.astype(BF)


def spatial_forward_kernel(
    frames_ref, bottle_ref, entry_ref, exit_ref, grad_ref,
    packed_ref, normed_ref, inverse_ref, mix_ref, weights_ref, att_ref, tokens,
):
    patches, bots = frames_ref.shape[0], bottle_ref.shape[0]
    rows, width = tokens.shape
    tokens[0:patches, :] = frames_ref[...].astype(F32)
    tokens[patches:rows, :] = jnp.zeros((rows - patches, width), F32)
    tokens[patches : patches + bots, :] = bottle_ref[...].astype(F32)
    normed, inverse = normalize(tokens[...])
    normed_ref[...] = normed
    inverse_ref[...] = inverse
    low = normed.astype(BF)
    mix_ref[...] = mm(low, entry_ref[...], NN).astype(BF)
    masks = half_masks(exit_ref.shape[1] // HEADS)
    keep = lax.broadcasted_iota(jnp.int32, (rows, rows), 1) < patches + bots

    def save(h, weights):
        weights_ref[h] = weights

    def put(p, w, value):
        att_ref[:, p * w : (p + 1) * w] = value

    attention_forward(mix_ref, keep, masks, save, put)
    out = tokens[0:patches, :] + mm(att_ref[0:patches, :], exit_ref[...], NT)
    packed_ref[:, 0:width] = out.astype(BF)
    packed_ref[:, width : 2 * width] = grad_ref[...]


def temporal_kernel(
    frames, core_ref, moved_ref, entry_ref, exit_ref,
    back_ref, send_ref, kept_ref, mix_ref, weights_ref, att_ref, d_mix_ref,
):
    rows, width = back_ref.shape
    side = exit_ref.shape[1]
    seqs = rows // frames
    normed, inverse = normalize(moved_ref[:, 0:width].astype(F32))
    low = normed.astype(BF)
    mix_ref[...] = mm(low, entry_ref[...], NN).astype(BF)
    masks = half_masks(side // HEADS)
    keep = (
        lax.broadcasted_iota(jnp.int32, (rows, rows), 0) % seqs
        == lax.broadcasted_iota(jnp.int32, (rows, rows), 1) % seqs
    )

    def save(h, weights):
        weights_ref[h] = weights

    def put(p, w, value):
        att_ref[:, p * w : (p + 1) * w] = value

    attention_forward(mix_ref, keep, masks, save, put)
    c = moved_ref[:, width : 2 * width]
    d_att = mm(c, exit_ref[...], NN).astype(BF)

    def put_grad(at, w, value):
        d_mix_ref[:, at : at + w] = value

    attention_backward(mix_ref, lambda h: weights_ref[h], d_att, masks, put_grad)
    d_normed = mm(d_mix_ref[...], entry_ref[...], NT)
    back_ref[...] = inputs_gradient(c, normed, inverse, d_normed).astype(BF)
    core = core_ref[0]
    other, own = picker(1 - core), picker(core)
    pick(low, other, send_ref, 0)
    pick(c, other, send_ref, width // 2)
    send_ref[:, width : width + 3 * side] = d_mix_ref[...]
    send_ref[:, width + 3 * side : width + 4 * side] = att_ref[...]
    pick(low, own, kept_ref, 0)
    pick(c, own, kept_ref, width // 2)


def spatial_backward_kernel(
    core_ref, back_ref, joined_ref, normed_ref, inverse_ref, mix_ref, weights_ref, att_ref,
    entry_ref, exit_ref, delta_ref, bottle_ref, send_ref, kept_ref, cot, d_mix_ref,
):
    patches, width = back_ref.shape
    rows, bots, side = normed_ref.shape[0], joined_ref.shape[0], exit_ref.shape[1]
    cot[0:patches, :] = back_ref[...].astype(F32)
    cot[patches:rows, :] = jnp.zeros((rows - patches, width), F32)
    cot[patches : patches + bots, :] = joined_ref[...].astype(F32)
    c = cot[...].astype(BF)
    masks = half_masks(side // HEADS)
    d_att = mm(c, exit_ref[...], NN).astype(BF)

    def put_grad(at, w, value):
        d_mix_ref[:, at : at + w] = value

    attention_backward(mix_ref, lambda h: weights_ref[h], d_att, masks, put_grad)
    d_normed = mm(d_mix_ref[...], entry_ref[...], NT)
    normed = normed_ref[...]
    grads = inputs_gradient(c, normed, inverse_ref[...], d_normed)
    delta_ref[...] = grads[0:patches, :].astype(BF)
    bottle_ref[...] = grads[patches : patches + 8, :]
    low = normed.astype(BF)
    core = core_ref[0]
    other, own = picker(1 - core), picker(core)
    pick(low, other, send_ref, 0)
    pick(c, other, send_ref, width // 2)
    send_ref[:, width : width + 3 * side] = d_mix_ref[...]
    send_ref[:, width + 3 * side : width + 4 * side] = att_ref[...]
    pick(low, own, kept_ref, 0)
    pick(c, own, kept_ref, width // 2)


def weight_gradient_kernel(kept_ref, sent_ref, got_ref, out_ref):
    half = kept_ref.shape[1] // 2
    rows, width = kept_ref.shape
    side = (sent_ref.shape[1] - width) // 4
    left = [
        jnp.concatenate([kept_ref[:, at : at + half], got_ref[:, at : at + half]], axis=0)
        for at in (0, half)
    ]
    for j in range(4):
        cols = slice(width + j * side, width + (j + 1) * side)
        right = jnp.concatenate([sent_ref[:, cols], got_ref[:, cols]], axis=0)
        out_ref[:, j * side : (j + 1) * side] = mm(left[j // 3], right, TN).astype(BF)


def sum_kernel(scale, parts_ref, entry_ref, exit_ref):
    total = jnp.sum(parts_ref[...].astype(F32), axis=0) * scale
    entry_ref[...] = total[:, : entry_ref.shape[1]].astype(BF)
    exit_ref[...] = total[:, entry_ref.shape[1] :].astype(BF)


VMEM = pl.BlockSpec(memory_space=pltpu.VMEM)
SMEM = pl.BlockSpec(memory_space=pltpu.SMEM)


def call(kernel, out_shape, in_specs, scratch=(), flops=0, limit=40):
    return pl.pallas_call(
        kernel,
        out_shape=tuple(jax.ShapeDtypeStruct(s, d) for s, d in out_shape),
        in_specs=in_specs,
        out_specs=tuple(VMEM for _ in out_shape),
        scratch_shapes=list(scratch),
        compiler_params=pltpu.CompilerParams(vmem_limit_bytes=limit * 1024 * 1024),
        cost_estimate=pl.CostEstimate(flops=flops, bytes_accessed=4_000_000, transcendentals=0),
    )


def per_device(
    frames_in, bottleneck, spatial_entry, spatial_exit, temporal_entry, temporal_exit,
    output_grad, joined_grad,
):
    patches, width = frames_in.shape[2], frames_in.shape[3]
    bots, side = bottleneck.shape[1], spatial_exit.shape[1]
    frames = lax.axis_size(FRAME)
    chips = lax.axis_size(CHIPS)
    rows = -(-(patches + bots) // 16) * 16
    core = lax.axis_index("c").astype(jnp.int32).reshape(1)
    clips = lax.axis_size(("zl", "x"))
    scale = 1.0 / math.sqrt(clips * frames * patches)

    packed, normed, inverse, mix, weights, att = call(
        spatial_forward_kernel,
        [
            ((patches, 2 * width), BF), ((rows, width), F32), ((rows, 1), F32),
            ((rows, 3 * side), BF), ((HEADS, rows, rows), F32), ((rows, side), BF),
        ],
        [VMEM] * 5,
        [pltpu.VMEM((rows, width), F32)],
        flops=1_000_000_000,
    )(frames_in[0, 0], bottleneck[0], spatial_entry, spatial_exit, output_grad[0, 0])

    moved = lax.all_to_all(
        packed.reshape(frames, patches // frames, 2 * width), FRAME, 0, 0, tiled=True
    ).reshape(patches, 2 * width)

    back, send_t, kept_t = call(
        functools.partial(temporal_kernel, frames),
        [((patches, width), BF), ((patches, width + 4 * side), BF), ((patches, width), BF)],
        [SMEM] + [VMEM] * 3,
        [
            pltpu.VMEM((patches, 3 * side), BF), pltpu.VMEM((HEADS, patches, patches), F32),
            pltpu.VMEM((patches, side), BF), pltpu.VMEM((patches, 3 * side), BF),
        ],
        flops=2_000_000_000,
    )(core, moved, temporal_entry, temporal_exit)

    back = lax.all_to_all(
        back.reshape(frames, patches // frames, width), FRAME, 0, 0, tiled=True
    ).reshape(patches, width)

    def chip_sums(kept, sent):
        got = lax.ppermute(sent, "c", [(0, 1), (1, 0)])
        (partial,) = call(
            weight_gradient_kernel, [((width // 2, 4 * side), BF)], [VMEM] * 3,
            flops=1_000_000_000,
        )(kept, sent, got)
        return partial.reshape(chips, -1, 4 * side)

    joined = (joined_grad[0].astype(F32) / frames).astype(BF)
    delta, local_bottle, send_s, kept_s = call(
        spatial_backward_kernel,
        [
            ((patches, width), BF), ((8, width), F32),
            ((rows, width + 4 * side), BF), ((rows, width), BF),
        ],
        [SMEM] + [VMEM] * 9,
        [pltpu.VMEM((rows, width), F32), pltpu.VMEM((rows, 3 * side), BF)],
        flops=2_000_000_000,
    )(core, back, joined, normed, inverse, mix, weights, att, spatial_entry, spatial_exit)

    bottleneck_delta = lax.psum(local_bottle[:bots], FRAME).astype(BF)[None]

    def finish(partial):
        parts = lax.all_to_all(partial, CHIPS, 0, 0, tiled=True)
        own = parts.shape[1]
        return call(
            functools.partial(sum_kernel, scale),
            [((own, 3 * side), BF), ((own, side), BF)], [VMEM],
            flops=1_000_000,
        )(parts)

    t_entry, t_exit = finish(chip_sums(kept_t, send_t))
    s_entry, s_exit = finish(chip_sums(kept_s, send_s))
    return (delta[None, None], bottleneck_delta, s_entry, s_exit, t_entry, t_exit)


def solution(mesh):
    finer = Mesh(mesh.devices.reshape(2, mesh.shape["dp"] // 2, 4, 2, 2), ALL)
    dp = ("zl", "x")
    row = P(ALL, None)
    clip = P(dp, None, None)
    patch = P(dp, FRAME, None, None)
    return jax.shard_map(
        per_device,
        mesh=finer,
        in_specs=(patch, clip, P(), P(), P(), P(), patch, clip),
        out_specs=(patch, clip, row, row, row, row),
        check_vma=False,
    )
```

time: 258 us -> 184 us (0.71)
  the two profiles are of different devices: /device:TPU:0 before, /device:TPU:38 now
where the time goes in v1:
time: 184 us; the launch traced here: 183 us
  blocking collectives  83.3 us (45%)
  waiting for transfers between devices  31 us (17%)
  starting transfers between devices  27.3 us (15%)
  local copies, waits for them, and re-layouts  23 us (12%)
  Pallas kernels  17.8 us (10%)
    psum x1, blocking collectives, per_device(): bottleneck_delta = lax.psum(local_bottle[:bots], FRAME).astype(BF)[None]  83.3 us
    unnamed x44, local copies, waits for them, and re-layouts  23 us
    all_to_all x2, starting transfers between devices, finish(): parts = lax.all_to_all(partial, CHIPS, 0, 0, tiled=True)  16.8 us
    all_to_all x1, waiting for transfers between devices, per_device(): lax.all_to_all(packed.reshape(frames, patches // frames, 2 * width), FRAM...  12.4 us
    all_to_all x2, waiting for transfers between devices, finish(): parts = lax.all_to_all(partial, CHIPS, 0, 0, tiled=True)  11.2 us
    all_to_all x1, starting transfers between devices, per_device(): lax.all_to_all(packed.reshape(frames, patches // frames, 2 * width), FRAM...  6.99 us
    pallas_call x1, Pallas kernels, per_device(): call(functools.partial(temporal_kernel, frames), [((patches, width), BF),...  5.5 us
    all_to_all x1, waiting for transfers between devices, per_device(): lax.all_to_all(back.reshape(frames, patches // frames, width), FRAME, 0,...  5.02 us
  transfers between devices with their start and end apart: 6, of which 4 were waited for; matrix products, arithmetic and copies ran while one was open for 0% of the time, Pallas kernels for 4%

profile of v1, /device:TPU:38, one launch (start us, length us, event | category | flops | bytes accessed | tf_op | source)
XLA Modules:
  0.0 183.1 jit_solution(1950668995918221999)
XLA Ops:
  0.6 0.0 copy-start.2
  0.6 1.9 %copy-done.2 = bf16[1024,1536]{1,0:T(8,128)(2,1)S(1)} copy-done((bf16[1024,1536]{1,0:T(8,128)(2,1)S(1)}, bf16[1024,1536]{1,0:T(8,128)(2,1)}, u32[]{:S(2)}) %copy-start.2) | copy-done | bytes 3145752
  2.5 0.0 copy-start.4
  2.5 1.2 copy-done.4
  3.8 0.0 copy-start.8
  3.8 0.9 copy-done.8
  4.7 0.0 copy-start.9
  4.7 0.9 copy-done.9
  5.7 0.0 copy-start.10
  5.7 0.7 copy-done.10
  6.3 2.8 %shard_map.127 = (bf16[128,2048]{1,0:T(8,128)(2,1)}, f32[144,1024]{1,0:T(8,128)S(1)}, f32[144,1]{1,0:T(8,128)S(1)}, bf16[144,1536]{1,0:T(8,128)(2,1)S(1)}, f32[8...) custom-call(bf16[128,1024]{1,0:T(8,128)(2,1)S(1)} %bitcast.19, bf16[4,1024]{1,0:T(4,128)(2,1)S(1)} %bitcast.22, ...), custom_call_target="tpu_custom_call" | custom-call | flops 1000000000 | bytes 4000000 | tf_op jit(solution)/shard_map/pallas_call | solution.py:264
  9.2 0.0 copy-start.12
  9.2 1.1 copy-done.12
  10.2 0.0 copy-start.15
  10.2 0.8 copy-done.15
  11.0 0.0 copy-start.17
  11.0 0.8 copy-done.17
  11.8 0.0 copy-start.19
  11.8 0.6 copy-done.19
  12.5 7.0 %all-to-all-start = ((bf16[16,8,2048]{2,1,0:T(8,128)(2,1)}), bf16[16,8,2048]{2,1,0:T(8,128)(2,1)S(1)}, u32[]{:S(2)}, u32[]{:S(2)}) async-start(bf16[16,8,2048]{2,1,0:T(8,128)(2,1)} %bitcast.4), calls=%async_computation | async-start | bytes 1048576 | tf_op jit(solution)/shard_map/all_to_all | solution.py:275
  19.5 12.4 %all-to-all-done = bf16[16,8,2048]{2,1,0:T(8,128)(2,1)S(1)} async-done(((bf16[16,8,2048]{2,1,0:T(8,128)(2,1)}), bf16[16,8,2048]{2,1,0:T(8,128)(2,1)S(1)}, u32[]{:S(2)}, u32[]{:S(2)}) %all-to-all-start) | async-done | bytes 524320 | tf_op jit(solution)/shard_map/all_to_all | solution.py:275
  31.8 0.0 copy-start.11
  31.8 1.9 %copy-done.11 = bf16[1024,1536]{1,0:T(8,128)(2,1)S(1)} copy-done((bf16[1024,1536]{1,0:T(8,128)(2,1)S(1)}, bf16[1024,1536]{1,0:T(8,128)(2,1)}, u32[]{:S(2)}) %copy-start.11) | copy-done | bytes 3145752
  33.7 0.0 copy-start.14
  33.7 1.2 copy-done.14
  34.9 5.5 %shard_map.128 = (bf16[128,1024]{1,0:T(8,128)(2,1)}, bf16[128,3072]{1,0:T(8,128)(2,1)S(1)}, bf16[128,1024]{1,0:T(8,128)(2,1)S(1)}) custom-call(s32[1]{0:T(128)} %bitcast.core_ref, bf16[128,2048]{1,0:T(8,128)(2,1)S(1)} %bitcast.18, bf16[1024,1536]{1,0:T(8,128)(2,1)S(1)} %copy-done.11, bf16[1024,512]{1,0:T(8,128)(2,1)S(1)} %copy-done.14), custom_call_target="tpu_custom_call" | custom-call | flops 2000000000 | bytes 4000000 | tf_op jit(solution)/shard_map/pallas_call | solution.py:279
  40.4 0.0 collective-permute-start.1
  40.4 3.5 %all-to-all-start.1 = ((bf16[16,8,1024]{2,1,0:T(8,128)(2,1)}), bf16[16,8,1024]{2,1,0:T(8,128)(2,1)S(1)}, u32[]{:S(2)}, u32[]{:S(2)}) async-start(bf16[16,8,1024]{2,1,0:T(8,128)(2,1)} %bitcast.6), calls=%async_computation.1 | async-start | bytes 524288 | tf_op jit(solution)/shard_map/all_to_all | solution.py:290
  44.0 0.0 collective-permute-done.1.got_ref
  44.0 0.0 copy-start.6
  44.0 0.9 copy-done.6
  44.9 0.0 copy-start.7
  44.9 1.1 copy-done.7
  46.0 0.7 shard_map.132
  46.8 0.0 copy-start
  46.8 1.3 copy-done
  48.1 5.0 %all-to-all-done.1 = bf16[16,8,1024]{2,1,0:T(8,128)(2,1)S(1)} async-done(((bf16[16,8,1024]{2,1,0:T(8,128)(2,1)}), bf16[16,8,1024]{2,1,0:T(8,128)(2,1)S(1)}, u32[]{:S(2)}, u32[]{:S(2)}) %all-to-all-start.1) | async-done | bytes 262176 | tf_op jit(solution)/shard_map/all_to_all | solution.py:290
  53.1 0.0 copy-start.21
  53.1 0.0 copy-start.5
  53.2 7.3 %all-to-all-start.3 = ((bf16[64,8,2048]{2,1,0:T(8,128)(2,1)}), bf16[64,8,2048]{2,1,0:T(8,128)(2,1)S(1)}, u32[]{:S(2)}, u32[]{:S(2)}) async-start(bf16[64,8,2048]{2,1,0:T(8,128)(2,1)} %bitcast.16), calls=%async_computation.3 | async-start | bytes 4194304 | tf_op jit(solution)/shard_map/all_to_all | solution.py:317
  60.5 0.0 copy-done.21
  60.5 0.0 copy-done.5
  60.5 0.0 copy-start.3
  60.5 1.9 %copy-done.3 = bf16[1024,1536]{1,0:T(8,128)(2,1)S(1)} copy-done((bf16[1024,1536]{1,0:T(8,128)(2,1)S(1)}, bf16[1024,1536]{1,0:T(8,128)(2,1)}, u32[]{:S(2)}) %copy-start.3) | copy-done | bytes 3145752
  62.4 0.0 copy-start.13
  62.4 1.3 copy-done.13
  63.7 0.0 copy-start.16
  63.7 1.1 copy-done.16
  64.8 0.0 copy-start.18
  64.8 1.0 copy-done.18
  65.8 0.0 copy-start.20
  65.8 0.9 copy-done.20
  66.7 4.1 %shard_map.129 = (bf16[128,1024]{1,0:T(8,128)(2,1)}, f32[8,1024]{1,0:T(8,128)S(1)}, bf16[144,3072]{1,0:T(8,128)(2,1)S(1)}, bf16[144,1024]{1,0:T(8,128)(2,1)S(1)}) custom-call(s32[1]{0:T(128)} %bitcast.core_ref, bf16[128,1024]{1,0:T(8,128)(2,1)S(1)} %bitcast.21, bf16[4,1024]{1,0:T(4,128)(2,1)S(1)} %fusion.joined_ref, f32[144,1024]{1,0:T(8,128)S(1)} %copy-done.16, ...), custom_call_target="tpu_custom_call" | custom-call | flops 2000000000 | bytes 4000000 | tf_op jit(solution)/shard_map/pallas_call | solution.py:303
  70.7 0.0 collective-permute-start
  70.7 2.4 %collective-permute-done.got_ref = bf16[144,3072]{1,0:T(8,128)(2,1)S(1)} collective-permute-done((bf16[144,3072]{1,0:T(8,128)(2,1)S(1)}, bf16[144,3072]{1,0:T(8,128)(2,1)S(1)}, u32[]{:S(2)}, u32[]{:S(2)}) %collective-permute-start) | collective-permute-done | bytes 884768 | tf_op jit(solution)/shard_map/ppermute | solution.py:295
  73.2 1.3 shard_map.130
  74.5 0.0 copy-start.1
  74.5 1.3 copy-done.1
  75.8 11.2 %all-to-all-done.3.parts_ref = bf16[64,8,2048]{2,1,0:T(8,128)(2,1)S(1)} async-done(((bf16[64,8,2048]{2,1,0:T(8,128)(2,1)}), bf16[64,8,2048]{2,1,0:T(8,128)(2,1)S(1)}, u32[]{:S(2)}, u32[]{:S(2)}) %all-to-all-start.3) | async-done | bytes 2097184 | tf_op jit(solution)/shard_map/all_to_all | solution.py:317
  87.0 9.4 %all-to-all-start.2 = ((bf16[64,8,2048]{2,1,0:T(8,128)(2,1)}), bf16[64,8,2048]{2,1,0:T(8,128)(2,1)}, u32[]{:S(2)}, u32[]{:S(2)}) async-start(bf16[64,8,2048]{2,1,0:T(8,128)(2,1)} %bitcast.17), calls=%async_computation.2 | async-start | bytes 4194304 | tf_op jit(solution)/shard_map/all_to_all | solution.py:317
  96.4 83.3 %psum.7 = bf16[4,1024]{1,0:T(4,128)(2,1)} all-reduce(f32[4,1024]{1,0:T(4,128)S(1)} %slice.3), channel_id=1, replica_groups=mesh['zl'=2,'x'=4,'y'=4,'zh'=2,'c'=2] {'y','zh','c'}, use_global_device_ids=true, to_apply=%region_0.0 | all-reduce | flops 4096 | bytes 24576 | tf_op jit(solution)/shard_map/psum | solution.py:314
  179.7 0.9 shard_map.133
  180.6 0.0 all-to-all-done.2.parts_ref
  180.6 2.5 %shard_map.131 = (bf16[8,1536]{1,0:T(8,128)(2,1)}, bf16[8,512]{1,0:T(8,128)(2,1)}) custom-call(bf16[64,8,2048]{2,1,0:T(8,128)(2,1)} %all-to-all-done.2.parts_ref), custom_call_target="tpu_custom_call" | custom-call | flops 1000000 | bytes 4000000 | tf_op jit(solution)/shard_map/pallas_call | solution.py:319
  (2 shorter events, 0.0 us)
Async XLA Ops:
  0.6 1.9 %copy-start.2 = (bf16[1024,1536]{1,0:T(8,128)(2,1)S(1)}, bf16[1024,1536]{1,0:T(8,128)(2,1)}, u32[]{:S(2)}) copy-start(bf16[1024,1536]{1,0:T(8,128)(2,1)} %entry_ref.5) | copy-start | bytes 9437188
  2.5 1.2 copy-start.4
  3.8 0.9 copy-start.8
  4.7 0.9 copy-start.9
  5.7 0.7 copy-start.10
  9.2 1.1 copy-start.12
  10.2 0.8 copy-start.15
  11.0 0.8 copy-start.17
  11.8 0.7 copy-start.19
  12.5 19.4 %all-to-all-start = ((bf16[16,8,2048]{2,1,0:T(8,128)(2,1)}), bf16[16,8,2048]{2,1,0:T(8,128)(2,1)S(1)}, u32[]{:S(2)}, u32[]{:S(2)}) async-start(bf16[16,8,2048]{2,1,0:T(8,128)(2,1)} %bitcast.4), calls=%async_computation | async-start | bytes 1048576 | tf_op jit(solution)/shard_map/all_to_all | solution.py:275
  31.8 1.9 %copy-start.11 = (bf16[1024,1536]{1,0:T(8,128)(2,1)S(1)}, bf16[1024,1536]{1,0:T(8,128)(2,1)}, u32[]{:S(2)}) copy-start(bf16[1024,1536]{1,0:T(8,128)(2,1)} %entry_ref.4) | copy-start | bytes 9437188
  33.7 1.2 copy-start.14
  40.4 3.5 %collective-permute-start.1 = (bf16[128,3072]{1,0:T(8,128)(2,1)S(1)}, bf16[128,3072]{1,0:T(8,128)(2,1)S(1)}, u32[]{:S(2)}, u32[]{:S(2)}) collective-permute-start(bf16[128,3072]{1,0:T(8,128)(2,1)S(1)} %get-tuple-element.37.sent_ref), channel_id=1, source_target_pairs={{0,1},{1,0},{2,3},{3,2},{4,5},{5,4},{6,7},{7,6},{8,9},{9,8},{10,11... | collective-permute-start | bytes 2359304 | tf_op jit(solution)/shard_map/ppermute | solution.py:295
  40.4 12.7 %all-to-all-start.1 = ((bf16[16,8,1024]{2,1,0:T(8,128)(2,1)}), bf16[16,8,1024]{2,1,0:T(8,128)(2,1)S(1)}, u32[]{:S(2)}, u32[]{:S(2)}) async-start(bf16[16,8,1024]{2,1,0:T(8,128)(2,1)} %bitcast.6), calls=%async_computation.1 | async-start | bytes 524288 | tf_op jit(solution)/shard_map/all_to_all | solution.py:290
  44.0 0.9 copy-start.6
  44.9 1.1 copy-start.7
  46.8 1.4 copy-start
  53.1 7.3 %copy-start.21 = (bf16[1,4,1024]{2,1,0:T(4,128)(2,1)S(1)}, bf16[1,4,1024]{2,1,0:T(4,128)(2,1)}, u32[]{:S(2)}) copy-start(bf16[1,4,1024]{2,1,0:T(4,128)(2,1)} %param.15) | copy-start | bytes 24580
  53.1 7.4 %copy-start.5 = (bf16[1024,512]{1,0:T(8,128)(2,1)S(1)}, bf16[1024,512]{1,0:T(8,128)(2,1)}, u32[]{:S(2)}) copy-start(bf16[1024,512]{1,0:T(8,128)(2,1)} %exit_ref.5) | copy-start | bytes 3145732
  53.2 33.8 %all-to-all-start.3 = ((bf16[64,8,2048]{2,1,0:T(8,128)(2,1)}), bf16[64,8,2048]{2,1,0:T(8,128)(2,1)S(1)}, u32[]{:S(2)}, u32[]{:S(2)}) async-start(bf16[64,8,2048]{2,1,0:T(8,128)(2,1)} %bitcast.16), calls=%async_computation.3 | async-start | bytes 4194304 | tf_op jit(solution)/shard_map/all_to_all | solution.py:317
  60.5 1.9 %copy-start.3 = (bf16[1024,1536]{1,0:T(8,128)(2,1)S(1)}, bf16[1024,1536]{1,0:T(8,128)(2,1)}, u32[]{:S(2)}) copy-start(bf16[1024,1536]{1,0:T(8,128)(2,1)} %entry_ref.5) | copy-start | bytes 9437188
  62.4 1.3 copy-start.13
  63.7 1.1 copy-start.16
  64.8 1.0 copy-start.18
  65.8 0.9 copy-start.20
  70.7 2.4 %collective-permute-start = (bf16[144,3072]{1,0:T(8,128)(2,1)S(1)}, bf16[144,3072]{1,0:T(8,128)(2,1)S(1)}, u32[]{:S(2)}, u32[]{:S(2)}) collective-permute-start(bf16[144,3072]{1,0:T(8,128)(2,1)S(1)} %get-tuple-element.33.sent_ref), channel_id=1, source_target_pairs={{0,1},{1,0},{2,3},{3,2},{4,5},{5,4},{6,7},{7,6},{8,9},{9,8},{10,11... | collective-permute-start | bytes 2654216 | tf_op jit(solution)/shard_map/ppermute | solution.py:295
  74.5 1.3 copy-start.1
  87.0 93.7 %all-to-all-start.2 = ((bf16[64,8,2048]{2,1,0:T(8,128)(2,1)}), bf16[64,8,2048]{2,1,0:T(8,128)(2,1)}, u32[]{:S(2)}, u32[]{:S(2)}) async-start(bf16[64,8,2048]{2,1,0:T(8,128)(2,1)} %bitcast.17), calls=%async_computation.2 | async-start | bytes 4194304 | tf_op jit(solution)/shard_map/all_to_all | solution.py:317

commit v2 on v1

v2 whole, which is shorter than its diff:
```python
import functools
import math

import jax
import jax.numpy as jnp
from jax import lax
from jax.experimental import pallas as pl
from jax.experimental.pallas import tpu as pltpu
from jax.sharding import Mesh
from jax.sharding import PartitionSpec as P

HEADS = 8
EPSILON = 1e-05
FRAME = ("y", "zh", "c")
CHIPS = ("zl", "x", "y", "zh")
ALL = ("zl", "x", "y", "zh", "c")
BF = jnp.bfloat16
F32 = jnp.float32

NN = (((1,), (0,)), ((), ()))
NT = (((1,), (1,)), ((), ()))
TN = (((0,), (0,)), ((), ()))


def mm(a, b, dims):
    return lax.dot_general(a, b, dims, preferred_element_type=F32)


def normalize(u):
    centred = u - jnp.mean(u, axis=-1, keepdims=True)
    inverse = lax.rsqrt(jnp.mean(centred * centred, axis=-1, keepdims=True) + EPSILON)
    return centred * inverse, inverse


def half_masks(size):
    lane = lax.broadcasted_iota(jnp.int32, (1, 2 * size), 1)
    low = (lane < size).astype(F32)
    return low.astype(BF), (1.0 - low).astype(BF)


def attention_forward(mix_ref, keep, masks, save, put):
    width = 2 * (mix_ref.shape[1] // 3 // HEADS)
    side = mix_ref.shape[1] // 3
    factor = 1.0 / math.sqrt(width // 2)
    for p in range(HEADS // 2):
        q2 = mix_ref[:, p * width : (p + 1) * width]
        k2 = mix_ref[:, side + p * width : side + (p + 1) * width]
        v2 = mix_ref[:, 2 * side + p * width : 2 * side + (p + 1) * width]
        total = None
        for h in range(2):
            scores = mm(q2 * masks[h], k2, NT) * factor
            scores = jnp.where(keep, scores, -jnp.inf)
            scores = scores - jnp.max(scores, axis=-1, keepdims=True)
            expon = jnp.exp(scores)
            weights = expon / jnp.sum(expon, axis=-1, keepdims=True)
            save(2 * p + h, weights)
            part = mm(weights.astype(BF), v2 * masks[h], NN)
            total = part if total is None else total + part
        put(p, width, total.astype(BF))


def attention_backward(mix_ref, load, d_att, masks, put):
    width = 2 * (mix_ref.shape[1] // 3 // HEADS)
    side = mix_ref.shape[1] // 3
    factor = 1.0 / math.sqrt(width // 2)
    for p in range(HEADS // 2):
        q2 = mix_ref[:, p * width : (p + 1) * width]
        k2 = mix_ref[:, side + p * width : side + (p + 1) * width]
        v2 = mix_ref[:, 2 * side + p * width : 2 * side + (p + 1) * width]
        d2 = d_att[:, p * width : (p + 1) * width]
        dq = dk = dv = None
        for h in range(2):
            dh = d2 * masks[h]
            weights = load(2 * p + h)
            grad = mm(dh, v2, NT)
            centre = jnp.sum(weights * grad, axis=-1, keepdims=True)
            ds = (weights * (grad - centre) * factor).astype(BF)
            a = mm(ds, k2 * masks[h], NN)
            b = mm(ds, q2 * masks[h], TN)
            c = mm(weights.astype(BF), dh, TN)
            dq = a if dq is None else dq + a
            dk = b if dk is None else dk + b
            dv = c if dv is None else dv + c
        put(p * width, width, dq.astype(BF))
        put(side + p * width, width, dk.astype(BF))
        put(2 * side + p * width, width, dv.astype(BF))


def inputs_gradient(c, normed, inverse, d_normed):
    inner = (
        d_normed
        - jnp.mean(d_normed, axis=-1, keepdims=True)
        - normed * jnp.mean(d_normed * normed, axis=-1, keepdims=True)
    )
    return c.astype(F32) + inverse * inner


def picker(half):
    row = lax.broadcasted_iota(jnp.int32, (256, 128), 0)
    col = lax.broadcasted_iota(jnp.int32, (256, 128), 1)
    source = (col // 8) * 16 + half * 8 + col % 8
    return (row == source).astype(F32).astype(BF)


def pick(values, chosen, out_ref, at):
    for b in range(values.shape[1] // 256):
        part = mm(values[:, 256 * b : 256 * (b + 1)], chosen, NN)
        out_ref[:, at + 128 * b : at + 128 * (b + 1)] = part.astype(BF)


class Mover:
    def __init__(self, sems):
        self.sems, self.count = sems, 0

    def start(self, source, target):
        copy = pltpu.make_async_copy(source, target, self.sems.at[self.count])
        self.count += 1
        copy.start()
        return copy


def finish(copies):
    for copy in copies:
        copy.wait()


def fill_tokens(tokens, frames, bottle):
    patches, bots = frames.shape[0], bottle.shape[0]
    rows, width = tokens.shape
    tokens[0:patches, :] = frames[...].astype(F32)
    tokens[patches:rows, :] = jnp.zeros((rows - patches, width), F32)
    tokens[patches : patches + bots, :] = bottle[...].astype(F32)


def spatial_forward_kernel(
    frames_hbm, bottle_hbm, entry_hbm, exit_hbm, grad_hbm,
    packed_hbm, mix_hbm, weights_hbm, att_hbm,
    frames, bottle, entry, exit_, tokens, packed, mix, weights_buf, att, sems,
):
    move = Mover(sems)
    patches, bots = frames.shape[0], bottle.shape[0]
    rows, width = tokens.shape
    side = exit_.shape[1]
    first = [move.start(frames_hbm, frames), move.start(bottle_hbm, bottle)]
    columns = [slice(j * side, (j + 1) * side) for j in range(3)]
    entries = [move.start(entry_hbm.at[:, c], entry.at[:, c]) for c in columns]
    later = move.start(exit_hbm, exit_)
    grads = move.start(grad_hbm, packed.at[:, width : 2 * width])
    outs = []
    finish(first)
    fill_tokens(tokens, frames, bottle)
    low = normalize(tokens[...])[0].astype(BF)
    for c, copy in zip(columns, entries):
        copy.wait()
        mix[:, c] = mm(low, entry[:, c], NN).astype(BF)
    outs.append(move.start(mix, mix_hbm))
    masks = half_masks(side // HEADS)
    keep = lax.broadcasted_iota(jnp.int32, (rows, rows), 1) < patches + bots

    def save(h, weights):
        weights_buf[h] = weights
        outs.append(move.start(weights_buf.at[h], weights_hbm.at[h]))

    def put(p, w, value):
        att[:, p * w : (p + 1) * w] = value

    attention_forward(mix, keep, masks, save, put)
    outs.append(move.start(att, att_hbm))
    later.wait()
    out = tokens[0:patches, :] + mm(att[0:patches, :], exit_[...], NT)
    packed[:, 0:width] = out.astype(BF)
    grads.wait()
    outs.append(move.start(packed, packed_hbm))
    finish(outs)


def spatial_factors_kernel(
    core_ref, frames_hbm, bottle_hbm, att_hbm, send_hbm, kept_hbm,
    frames, bottle, tokens, send, kept, sems,
):
    move = Mover(sems)
    half = kept.shape[1]
    first = [move.start(frames_hbm, frames), move.start(bottle_hbm, bottle)]
    copied = move.start(att_hbm, send.at[:, half:])
    finish(first)
    fill_tokens(tokens, frames, bottle)
    low = normalize(tokens[...])[0].astype(BF)
    core = core_ref[0]
    pick(low, picker(1 - core), send, 0)
    copied.wait()
    outs = [move.start(send, send_hbm)]
    pick(low, picker(core), kept, 0)
    outs.append(move.start(kept, kept_hbm))
    finish(outs)


def temporal_kernel(
    frames, moved_hbm, entry_hbm, exit_hbm, back_hbm, d_mix_hbm, att_hbm,
    moved, entry, exit_, back, mix, weights_buf, att, d_mix, sems,
):
    move = Mover(sems)
    rows, width = back.shape
    side = exit_.shape[1]
    seqs = rows // frames
    first = move.start(moved_hbm, moved)
    columns = [slice(j * side, (j + 1) * side) for j in range(3)]
    entries = [move.start(entry_hbm.at[:, c], entry.at[:, c]) for c in columns]
    later = move.start(exit_hbm, exit_)
    first.wait()
    normed, inverse = normalize(moved[:, 0:width].astype(F32))
    low = normed.astype(BF)
    for c, copy in zip(columns, entries):
        copy.wait()
        mix[:, c] = mm(low, entry[:, c], NN).astype(BF)
    masks = half_masks(side // HEADS)
    keep = (
        lax.broadcasted_iota(jnp.int32, (rows, rows), 0) % seqs
        == lax.broadcasted_iota(jnp.int32, (rows, rows), 1) % seqs
    )

    def save(h, weights):
        weights_buf[h] = weights

    def put(p, w, value):
        att[:, p * w : (p + 1) * w] = value

    attention_forward(mix, keep, masks, save, put)
    outs = [move.start(att, att_hbm)]
    later.wait()
    cot = moved[:, width : 2 * width]
    d_att = mm(cot, exit_[...], NN).astype(BF)

    def put_grad(at, w, value):
        d_mix[:, at : at + w] = value

    attention_backward(mix, lambda h: weights_buf[h], d_att, masks, put_grad)
    outs.append(move.start(d_mix, d_mix_hbm))
    d_normed = mm(d_mix[...], entry[...], NT)
    back[...] = inputs_gradient(cot, normed, inverse, d_normed).astype(BF)
    outs.append(move.start(back, back_hbm))
    finish(outs)


def temporal_factors_kernel(
    core_ref, moved_hbm, att_hbm, d_mix_hbm, send_hbm, kept_hbm, moved, send, kept, sems
):
    move = Mover(sems)
    width = moved.shape[1] // 2
    half, side = width // 2, att_hbm.shape[1]
    first = move.start(moved_hbm, moved)
    copied = [
        move.start(att_hbm, send.at[:, half : half + side]),
        move.start(d_mix_hbm, send.at[:, width + side : width + 4 * side]),
    ]
    first.wait()
    low = normalize(moved[:, 0:width].astype(F32))[0].astype(BF)
    cot = moved[:, width : 2 * width]
    core = core_ref[0]
    other = picker(1 - core)
    pick(low, other, send, 0)
    pick(cot, other, send, half + side)
    finish(copied)
    outs = [move.start(send, send_hbm)]
    own = picker(core)
    pick(low, own, kept, 0)
    pick(cot, own, kept, half)
    outs.append(move.start(kept, kept_hbm))
    finish(outs)


def fill_cotangent(cot, joined, frames):
    patches = cot.shape[0] - 16
    rows = joined[...].astype(F32) / frames
    padded = jnp.concatenate([rows, jnp.zeros((16 - rows.shape[0], rows.shape[1]), F32)], axis=0)
    cot[patches:, :] = padded.astype(BF)


def spatial_backward_kernel(
    frames, core_ref, back_hbm, joined_hbm, mix_hbm, weights_hbm, exit_hbm, send_hbm, kept_hbm,
    cot, joined, mix, weights_buf, exit_, send, kept, sems,
):
    move = Mover(sems)
    side, half = exit_.shape[1], kept.shape[1]
    patches = back_hbm.shape[0]
    first = [move.start(joined_hbm, joined), move.start(back_hbm, cot.at[0:patches, :])]
    first.append(move.start(exit_hbm, exit_))
    second = move.start(mix_hbm, mix)
    heads = [move.start(weights_hbm.at[h], weights_buf.at[h]) for h in range(HEADS)]
    finish(first)
    fill_cotangent(cot, joined, frames)
    c = cot[...]
    d_att = mm(c, exit_[...], NN).astype(BF)
    core = core_ref[0]
    pick(c, picker(core), kept, 0)
    outs = [move.start(kept, kept_hbm)]
    pick(c, picker(1 - core), send, 0)
    masks = half_masks(side // HEADS)
    second.wait()

    def load(h):
        heads[h].wait()
        return weights_buf[h]

    def put_grad(at, w, value):
        send[:, half + at : half + at + w] = value

    attention_backward(mix, load, d_att, masks, put_grad)
    outs.append(move.start(send, send_hbm))
    finish(outs)


def spatial_inputs_kernel(
    frames_count, frames_hbm, bottle_hbm, back_hbm, joined_hbm, send_hbm, entry_hbm,
    delta_hbm, local_hbm, frames, bottle, cot, joined, d_mix, entry, tokens, delta, local, sems,
):
    move = Mover(sems)
    patches, width = delta.shape
    half = send_hbm.shape[1] - d_mix.shape[1]
    first = [move.start(frames_hbm, frames), move.start(bottle_hbm, bottle)]
    second = [
        move.start(send_hbm.at[:, half:], d_mix),
        move.start(entry_hbm, entry),
        move.start(joined_hbm, joined),
        move.start(back_hbm, cot.at[0:patches, :]),
    ]
    finish(first)
    fill_tokens(tokens, frames, bottle)
    normed, inverse = normalize(tokens[...])
    finish(second)
    fill_cotangent(cot, joined, frames_count)
    d_normed = mm(d_mix[...], entry[...], NT)
    grads = inputs_gradient(cot[...], normed, inverse, d_normed)
    delta[...] = grads[0:patches, :].astype(BF)
    outs = [move.start(delta, delta_hbm)]
    local[...] = grads[patches : patches + local.shape[0], :]
    outs.append(move.start(local, local_hbm))
    finish(outs)


def weight_gradient_kernel(places, in_turns, *refs):
    if in_turns:
        core_ref, refs = refs[0], refs[1:]
    arrays, refs = refs[: len(refs) - 7], refs[len(refs) - 7 :]
    out_hbm, left_n, left_c, right_m, right_a, out, sems = refs
    move = Mover(sems)
    rows = left_n.shape[0] // 2

    def both(target, pair):
        copies = []
        for k, (index, at) in enumerate(pair):
            source = arrays[index].at[:, at : at + target.shape[1]]
            copies.append(move.start(source, target.at[k * rows : (k + 1) * rows, :]))
        return copies

    ready = [both(t, places[k]) for k, t in enumerate((left_c, right_a, left_n, right_m))]
    side = right_a.shape[1]
    outs = []

    def put(at, value):
        if not in_turns:
            out[:, at : at + side] = value
        else:
            core = core_ref[0]
            for b in range(32):
                zl, x, y = b // 16, b // 4 % 4, b % 4
                turn = jnp.where(core == 0, x * 8 + y * 2 + zl, y * 8 + x * 2 + zl)
                where = pl.ds(pl.multiple_of(turn * 16, 16), 16)
                out[where, at : at + side] = value[b * 16 : (b + 1) * 16, :]
        columns = slice(at, at + side)
        outs.append(move.start(out.at[:, columns], out_hbm.at[:, columns]))

    finish(ready[0] + ready[1])
    put(3 * side, mm(left_c[...], right_a[...], TN).astype(BF))
    finish(ready[2] + ready[3])
    for j in range(3):
        put(j * side, mm(left_n[...], right_m[:, j * side : (j + 1) * side], TN).astype(BF))
    finish(outs)


def sum_kernel(
    scale, parts_hbm, summed_hbm, s_entry_hbm, s_exit_hbm, t_entry_hbm, t_exit_hbm,
    parts, summed, s_entry, s_exit, t_entry, t_exit, sems,
):
    move = Mover(sems)
    side = s_exit.shape[1]
    columns = [slice(j * side, (j + 1) * side) for j in range(4)]
    copies = [move.start(parts_hbm.at[:, :, c], parts.at[:, :, c]) for c in columns]
    temporal = move.start(summed_hbm, summed)
    for j, (c, copy) in enumerate(zip(columns, copies)):
        copy.wait()
        total = (jnp.sum(parts[:, :, c].astype(F32), axis=0) * scale).astype(BF)
        if j < 3:
            s_entry[:, c] = total
        else:
            s_exit[...] = total
    outs = [move.start(s_entry, s_entry_hbm), move.start(s_exit, s_exit_hbm)]
    temporal.wait()
    total = (summed[...].astype(F32) * scale).astype(BF)
    t_entry[...] = total[:, : 3 * side]
    t_exit[...] = total[:, 3 * side :]
    outs += [move.start(t_entry, t_entry_hbm), move.start(t_exit, t_exit_hbm)]
    finish(outs)


HBM = pl.BlockSpec(memory_space=pltpu.HBM)
SMEM = pl.BlockSpec(memory_space=pltpu.SMEM)


def call(kernel, outs, ins, scratch, copies, flops):
    moved = sum(math.prod(a.shape) * a.dtype.itemsize for a in ins)
    moved += sum(math.prod(s) * jnp.dtype(d).itemsize for s, d in outs)
    return pl.pallas_call(
        kernel,
        out_shape=tuple(jax.ShapeDtypeStruct(s, d) for s, d in outs),
        in_specs=[SMEM if a.ndim == 1 else HBM for a in ins],
        out_specs=tuple(HBM for _ in outs),
        scratch_shapes=[pltpu.VMEM(s, d) for s, d in scratch]
        + [pltpu.SemaphoreType.DMA((copies,))],
        compiler_params=pltpu.CompilerParams(vmem_limit_bytes=40 * 1024 * 1024),
        cost_estimate=pl.CostEstimate(flops=flops, bytes_accessed=moved, transcendentals=0),
    )(*ins)


def turns(shape):
    zls, xs, ys, zhs, cores = (range(n) for n in shape)

    def at(zl, x, y, zh, c):
        return (((zl * shape[1] + x) * shape[2] + y) * shape[3] + zh) * shape[4] + c

    along_x = [
        [[at(zl, x, y, zh, c) for x in xs] for zl in zls for y in ys for zh in zhs] for c in cores
    ]
    along_y = [
        [[at(zl, x, y, zh, c) for y in ys] for zl in zls for x in xs for zh in zhs] for c in cores
    ]
    along_z = [
        [at(zl, x, y, zh, c) for zl in zls for zh in zhs] for x in xs for y in ys for c in cores
    ]
    return along_x[0] + along_y[1], along_y[0] + along_x[1], along_z


def per_device(
    frames_in, bottleneck, spatial_entry, spatial_exit, temporal_entry, temporal_exit,
    output_grad, joined_grad,
):
    patches, width = frames_in.shape[2], frames_in.shape[3]
    bots, side = bottleneck.shape[1], spatial_exit.shape[1]
    half = width // 2
    frames = lax.axis_size(FRAME)
    chips = lax.axis_size(CHIPS)
    rows = patches + 16
    core = lax.axis_index("c").astype(jnp.int32).reshape(1)
    clips = lax.axis_size(("zl", "x"))
    scale = 1.0 / math.sqrt(clips * frames * patches)
    frame, bottle, joined = frames_in[0, 0], bottleneck[0], joined_grad[0]
    swap = [(0, 1), (1, 0)]

    def exchange(array):
        blocks = array.reshape(frames, patches // frames, array.shape[1])
        return lax.all_to_all(blocks, FRAME, 0, 0, tiled=True).reshape(array.shape)

    packed, mix, weights, att = call(
        spatial_forward_kernel,
        [
            ((patches, 2 * width), BF), ((rows, 3 * side), BF), ((HEADS, rows, rows), F32),
            ((rows, side), BF),
        ],
        [frame, bottle, spatial_entry, spatial_exit, output_grad[0, 0]],
        [
            ((patches, width), BF), ((bots, width), BF), ((width, 3 * side), BF),
            ((width, side), BF), ((rows, width), F32),
            ((patches, 2 * width), BF), ((rows, 3 * side), BF), ((HEADS, rows, rows), F32),
            ((rows, side), BF),
        ],
        10 + HEADS,
        1_000_000_000,
    )
    moved = exchange(packed)

    send_s1, kept_sn = call(
        spatial_factors_kernel,
        [((rows, half + side), BF), ((rows, half), BF)],
        [core, frame, bottle, att],
        [
            ((patches, width), BF), ((bots, width), BF), ((rows, width), F32),
            ((rows, half + side), BF), ((rows, half), BF),
        ],
        5,
        300_000_000,
    )
    got_s1 = lax.ppermute(send_s1, "c", swap)

    back, d_mix_t, att_t = call(
        functools.partial(temporal_kernel, frames),
        [((patches, width), BF), ((patches, 3 * side), BF), ((patches, side), BF)],
        [moved, temporal_entry, temporal_exit],
        [
            ((patches, 2 * width), BF), ((width, 3 * side), BF), ((width, side), BF),
            ((patches, width), BF), ((patches, 3 * side), BF), ((HEADS, patches, patches), F32),
            ((patches, side), BF), ((patches, 3 * side), BF),
        ],
        8,
        2_000_000_000,
    )
    back = exchange(back)

    send_t, kept_t = call(
        temporal_factors_kernel,
        [((patches, half + side + half + 3 * side), BF), ((patches, width), BF)],
        [core, moved, att_t, d_mix_t],
        [
            ((patches, 2 * width), BF), ((patches, half + side + half + 3 * side), BF),
            ((patches, width), BF),
        ],
        5,
        300_000_000,
    )
    got_t = lax.ppermute(send_t, "c", swap)

    def weight_gradient(count, places, arrays, in_turns):
        return call(
            functools.partial(weight_gradient_kernel, places, in_turns),
            [((half, 4 * side), BF)],
            ([core] if in_turns else []) + arrays,
            [
                ((2 * count, half), BF), ((2 * count, half), BF), ((2 * count, 3 * side), BF),
                ((2 * count, side), BF), ((half, 4 * side), BF),
            ],
            12,
            1_000_000_000,
        )[0]

    cot_at, mix_at = half + side, half + side + half
    partial_t = weight_gradient(
        patches,
        (
            ((0, half), (2, cot_at)), ((1, half), (2, half)),
            ((0, 0), (2, 0)), ((1, mix_at), (2, mix_at)),
        ),
        [kept_t, send_t, got_t],
        True,
    )
    summed_t = partial_t
    for groups in turns([lax.axis_size(a) for a in ALL]):
        summed_t = lax.psum_scatter(
            summed_t, ALL, scatter_dimension=0, axis_index_groups=groups, tiled=True
        )

    send_s2, kept_sc = call(
        functools.partial(spatial_backward_kernel, frames),
        [((rows, half + 3 * side), BF), ((rows, half), BF)],
        [core, back, joined, mix, weights, spatial_exit],
        [
            ((rows, width), BF), ((bots, width), BF), ((rows, 3 * side), BF),
            ((HEADS, rows, rows), F32), ((width, side), BF), ((rows, half + 3 * side), BF),
            ((rows, half), BF),
        ],
        6 + HEADS,
        1_500_000_000,
    )
    got_s2 = lax.ppermute(send_s2, "c", swap)
    delta, local = call(
        functools.partial(spatial_inputs_kernel, frames),
        [((patches, width), BF), ((8, width), F32)],
        [frame, bottle, back, joined, send_s2, spatial_entry],
        [
            ((patches, width), BF), ((bots, width), BF), ((rows, width), BF), ((bots, width), BF),
            ((rows, 3 * side), BF), ((width, 3 * side), BF), ((rows, width), F32),
            ((patches, width), BF), ((8, width), F32),
        ],
        8,
        1_000_000_000,
    )
    partial_s = weight_gradient(
        rows,
        (
            ((3, 0), (5, 0)), ((1, half), (2, half)),
            ((0, 0), (2, 0)), ((4, half), (5, half)),
        ),
        [kept_sn, send_s1, got_s1, kept_sc, send_s2, got_s2],
        False,
    )
    parts = lax.all_to_all(partial_s.reshape(chips, -1, 4 * side), CHIPS, 0, 0, tiled=True)

    local = local[:bots]
    for axis, bit in (("c", 1), ("zh", 1), ("y", 1), ("y", 2)):
        pairs = [(i, i ^ bit) for i in range(lax.axis_size(axis))]
        local = local + lax.ppermute(local, axis, pairs)

    own = parts.shape[1]
    s_entry, s_exit, t_entry, t_exit = call(
        functools.partial(sum_kernel, scale),
        [((own, 3 * side), BF), ((own, side), BF)] * 2,
        [parts, summed_t],
        [
            (parts.shape, BF), ((own, 4 * side), BF),
            ((own, 3 * side), BF), ((own, side), BF), ((own, 3 * side), BF), ((own, side), BF),
        ],
        9,
        1_000_000,
    )
    return (
        delta[None, None], local.astype(BF)[None], s_entry, s_exit, t_entry, t_exit
    )


def solution(mesh):
    finer = Mesh(mesh.devices.reshape(2, mesh.shape["dp"] // 2, 4, 2, 2), ALL)
    dp = ("zl", "x")
    row = P(ALL, None)
    clip = P(dp, None, None)
    patch = P(dp, FRAME, None, None)
    return jax.shard_map(
        per_device,
        mesh=finer,
        in_specs=(patch, clip, P(), P(), P(), P(), patch, clip),
        out_specs=(patch, clip, row, row, row, row),
        check_vma=False,
    )
```

time: 184 us -> 156 us (0.85)
  the two profiles are of different devices: /device:TPU:38 before, /device:TPU:0 now
where the time goes in v2:
time: 156 us
  waiting for transfers between devices  61.5 us (39%)
  Pallas kernels  32.8 us (21%)
  starting transfers between devices  21.3 us (14%)
  between operations  14.1 us (9%)
  local copies, waits for them, and re-layouts  13.2 us (8%)
  blocking collectives  12.2 us (8%)
    reduce_scatter x3, waiting for transfers between devices, per_device(): lax.psum_scatter(summed_t, ALL, scatter_dimension=0, axis_index_groups=gr...  36.2 us
    pallas_call x9, Pallas kernels, call(): pl.pallas_call(kernel, out_shape=tuple((jax.ShapeDtypeStruct(s, d) for s,...  32.8 us
    unnamed x44, local copies, waits for them, and re-layouts  13.2 us
    all_to_all x1, waiting for transfers between devices, exchange(): return lax.all_to_all(blocks, FRAME, 0, 0, tiled=True).reshape(array.shape)  12.3 us
    all_to_all x1, blocking collectives, exchange(): return lax.all_to_all(blocks, FRAME, 0, 0, tiled=True).reshape(array.shape)  12.2 us
    ppermute x4, waiting for transfers between devices, per_device(): local = local + lax.ppermute(local, axis, pairs)  8.79 us
    all_to_all x1, starting transfers between devices, exchange(): return lax.all_to_all(blocks, FRAME, 0, 0, tiled=True).reshape(array.shape)  7.97 us
    all_to_all x1, starting transfers between devices, per_device(): lax.all_to_all(partial_s.reshape(chips, -1, 4 * side), CHIPS, 0, 0, tiled...  7.75 us
  transfers between devices with their start and end apart: 12, of which 8 were waited for; matrix products, arithmetic and copies ran while one was open for 0% of the time, Pallas kernels for 8%

profile of v2, /device:TPU:0, one launch (start us, length us, event | category | flops | bytes accessed | tf_op | source)
XLA Modules:
  0.0 155.7 jit_solution(17501607454605047499)
XLA Ops:
  7.2 0.0 copy-start
  7.2 1.9 %copy-done = bf16[1024,1536]{1,0:T(8,128)(2,1)S(1)} copy-done((bf16[1024,1536]{1,0:T(8,128)(2,1)S(1)}, bf16[1024,1536]{1,0:T(8,128)(2,1)}, u32[]{:S(2)}) %copy-start) | copy-done | bytes 3145752
  9.1 0.9 copy-done.5
  10.0 1.2 copy-done.9
  11.2 0.9 copy-done.11
  12.2 0.7 copy-done.13
  12.9 8.0 %shard_map.127 = (bf16[128,2048]{1,0:T(8,128)(2,1)}, bf16[144,1536]{1,0:T(8,128)(2,1)S(1)}, f32[8,144,144]{2,1,0:T(8,128)S(1)}, bf16[144,512]{1,0:T(8,128)(2,1)S(1)}) custom-call(bf16[128,1024]{1,0:T(8,128)(2,1)S(1)} %bitcast.14, bf16[4,1024]{1,0:T(4,128)(2,1)S(1)} %bitcast.23, bf16[1024,1536]{1,0:T(8,128)(2,1)S(1)} %copy-done, ...), custom_call_target="tpu_custom_call" | custom-call | flops 1000000000 | bytes 6504448 | tf_op jit(solution)/shard_map/pallas_call | solution.py:412
  20.9 0.0 copy-start.18
  20.9 0.8 copy-done.18
  21.7 0.7 copy-done.20
  22.4 8.0 %all-to-all-start = ((bf16[16,8,2048]{2,1,0:T(8,128)(2,1)}), bf16[16,8,2048]{2,1,0:T(8,128)(2,1)S(1)}, u32[]{:S(2)}, u32[]{:S(2)}) async-start(bf16[16,8,2048]{2,1,0:T(8,128)(2,1)} %bitcast.3), calls=%async_computation | async-start | bytes 1048576 | tf_op jit(solution)/shard_map/all_to_all | solution.py:460
  30.4 0.0 reduce-scatter.4.cloned.1.call-start
  30.4 12.3 %all-to-all-done = bf16[16,8,2048]{2,1,0:T(8,128)(2,1)S(1)} async-done(((bf16[16,8,2048]{2,1,0:T(8,128)(2,1)}), bf16[16,8,2048]{2,1,0:T(8,128)(2,1)S(1)}, u32[]{:S(2)}, u32[]{:S(2)}) %all-to-all-start) | async-done | bytes 524320 | tf_op jit(solution)/shard_map/all_to_all | solution.py:460
  42.7 0.0 copy-done.17
  42.7 1.9 %copy-done.16 = bf16[1024,1536]{1,0:T(8,128)(2,1)S(1)} copy-done((bf16[1024,1536]{1,0:T(8,128)(2,1)S(1)}, bf16[1024,1536]{1,0:T(8,128)(2,1)}, u32[]{:S(2)}) %copy-start.16) | copy-done | bytes 3145752
  44.6 6.3 %shard_map.128 = (bf16[128,1024]{1,0:T(8,128)(2,1)S(1)}, bf16[128,1536]{1,0:T(8,128)(2,1)S(1)}, bf16[128,512]{1,0:T(8,128)(2,1)S(1)}) custom-call(bf16[128,2048]{1,0:T(8,128)(2,1)S(1)} %bitcast.19, bf16[1024,1536]{1,0:T(8,128)(2,1)S(1)} %copy-done.16, bf16[1024,512]{1,0:T(8,128)(2,1)S(1)} %copy-done.17), custom_call_target="tpu_custom_call" | custom-call | flops 2000000000 | bytes 5505024 | tf_op jit(solution)/shard_map/pallas_call | solution.py:412
  51.0 1.0 shard_map.133
  52.0 0.1 collective-permute-start.6
  52.0 2.3 %collective-permute-done.6.refs_3_ = bf16[128,3072]{1,0:T(8,128)(2,1)S(1)} collective-permute-done((bf16[128,3072]{1,0:T(8,128)(2,1)S(1)}, bf16[128,3072]{1,0:T(8,128)(2,1)S(1)}, u32[]{:S(2)}, u32[]{:S(2)}) %collective-permute-start.6) | collective-permute-done | bytes 786464 | tf_op jit(solution)/shard_map/ppermute | solution.py:518
  54.3 2.1 %shard_map.134 = bf16[512,2048]{1,0:T(8,128)(2,1)} custom-call(s32[1]{0:T(128)} %bitcast.8.core_ref.refs_0_, bf16[128,1024]{1,0:T(8,128)(2,1)S(1)} %get-tuple-element.38.refs_1_, bf16[128,3072]{1,0:T(8,128)(2,1)S(1)} %get-tuple-element.39.refs_2_, bf16[128,3072]{1,0:T(8,128)(2,1)S(1)} %collective-permute-done.6.refs_3_), custom_call_target="tpu_custom_call" | custom-call | flops 1000000000 | bytes 3932164 | tf_op jit(solution)/shard_map/pallas_call | solution.py:412
  56.5 0.0 copy-start.10
  56.5 0.0 copy-start.15
  56.5 0.0 copy-start.19
  56.5 0.0 reduce-scatter.4.cloned.1.call-update
  56.5 12.2 %all_to_all.15 = bf16[16,8,1024]{2,1,0:T(8,128)(2,1)S(1)} all-to-all(bf16[16,8,1024]{2,1,0:T(8,128)(2,1)S(1)} %bitcast.22), channel_id=1, replica_groups=mesh['zl'=2,'x'=4,'y'=4,'zh'=2,'c'=2] {'y','zh','c'}, dimensions={0} | all-to-all | bytes 524288 | tf_op jit(solution)/shard_map/all_to_all | solution.py:460
  68.8 0.0 copy-done.10
  68.8 0.0 copy-done.15
  68.8 0.0 copy-done.19
  68.8 0.0 copy-start.6
  68.8 0.0 copy-start.14
  68.8 6.4 %shard_map.129 = (bf16[144,2048]{1,0:T(8,128)(2,1)S(1)}, bf16[144,512]{1,0:T(8,128)(2,1)S(1)}) custom-call(s32[1]{0:T(128)} %bitcast.8.core_ref.refs_0_, bf16[128,1024]{1,0:T(8,128)(2,1)S(1)} %bitcast.17, bf16[4,1024]{1,0:T(4,128)(2,1)S(1)} %bitcast.26, bf16[144,1536]{1,0:T(8,128)(2,1)S(1)} %copy-done.19, f32[8,144,144]{2,1,0:T(8,128)S(1)} %get-tuple-element.28.weights_hbm, ...), custom_call_target="tpu_custom_call" | custom-call | flops 1500000000 | bytes 3162116 | tf_op jit(solution)/shard_map/pallas_call | solution.py:412
  75.2 0.1 collective-permute-start.5
  75.3 0.0 copy-done.6
  75.3 0.0 copy-done.14
  75.3 0.0 copy-done.21
  75.3 1.0 shard_map.131
  76.3 0.7 collective-permute-start.4
  77.0 1.2 collective-permute-done.4.refs_2_
  78.3 0.0 collective-permute-done.5.refs_5_
  78.3 3.0 %shard_map.132 = bf16[512,2048]{1,0:T(8,128)(2,1)S(1)} custom-call(bf16[144,512]{1,0:T(8,128)(2,1)S(1)} %get-tuple-element.33.refs_0_, bf16[144,1024]{1,0:T(8,128)(2,1)S(1)} %get-tuple-element.34.refs_1_, bf16[144,1024]{1,0:T(8,128)(2,1)S(1)} %collective-permute-done.4.refs_2_, bf16[144,512]{1,0:T(8,128)(2,1)S(1)} %get-tuple-element.35.refs_3_, ...), custom_call_target="tpu_custom_call" | custom-call | flops 1000000000 | bytes 4161536 | tf_op jit(solution)/shard_map/pallas_call | solution.py:412
  81.3 1.3 copy-done.2
  82.6 7.8 %all-to-all-start.2 = ((bf16[64,8,2048]{2,1,0:T(8,128)(2,1)}), bf16[64,8,2048]{2,1,0:T(8,128)(2,1)}, u32[]{:S(2)}, u32[]{:S(2)}) async-start(bf16[64,8,2048]{2,1,0:T(8,128)(2,1)} %bitcast.13), calls=%async_computation.2 | async-start | bytes 4194304 | tf_op jit(solution)/shard_map/all_to_all | solution.py:583
  90.4 0.0 reduce-scatter.6.cloned.1.call-start
  90.4 0.0 reduce-scatter.4.cloned.1.call-done
  90.5 0.7 reduce-scatter.6.cloned.1.call-update
  91.1 0.0 reduce-scatter.8.cloned.1.call-start
  91.2 1.1 copy-done.4
  92.3 0.9 copy-done.8
  93.2 2.6 %shard_map.130 = (bf16[128,1024]{1,0:T(8,128)(2,1)}, f32[8,1024]{1,0:T(8,128)S(1)}) custom-call(bf16[128,1024]{1,0:T(8,128)(2,1)S(1)} %bitcast.16, bf16[4,1024]{1,0:T(4,128)(2,1)S(1)} %bitcast.25, bf16[128,1024]{1,0:T(8,128)(2,1)S(1)} %bitcast.18, bf16[4,1024]{1,0:T(4,128)(2,1)S(1)} %bitcast.27, bf16[144,2048]{1,0:T(8,128)(2,1)S(1)} %copy-done.4, ...), custom_call_target="tpu_custom_call" | custom-call | flops 1000000000 | bytes 4571136 | tf_op jit(solution)/shard_map/pallas_call | solution.py:412
  95.9 0.1 collective-permute-start
  96.0 1.2 collective-permute-done
  97.1 3.0 %collective-permute-start.1 = (f32[4,1024]{1,0:T(4,128)S(1)}, f32[4,1024]{1,0:T(4,128)S(1)}, u32[]{:S(2)}, u32[]{:S(2)}) collective-permute-start(f32[4,1024]{1,0:T(4,128)S(1)} %slice_add_fusion), channel_id=1, source_target_pairs={{0,2},{2,0},{1,3},{3,1},{4,6},{6,4},{5,7},{7,5},{8,10},{10,8},{9,1... | collective-permute-start | bytes 49160 | tf_op jit(solution)/shard_map/ppermute | solution.py:588
  100.1 20.6 %reduce-scatter.6.cloned.1.call-done = bf16[32,2048]{1,0:T(8,128)(2,1)} async-done(((bf16[128,2048]{1,0:T(8,128)(2,1)}), bf16[32,2048]{1,0:T(8,128)(2,1)}) %reduce-scatter.6.cloned.1.call-update) | async-done | bytes 131088 | tf_op jit(solution)/shard_map/reduce_scatter | solution.py:545
  120.7 0.0 reduce-scatter.8.cloned.1.call-update
  120.8 0.0 collective-permute-done.1
  120.8 0.1 collective-permute-start.2
  120.9 3.7 %collective-permute-done.2 = f32[4,1024]{1,0:T(4,128)S(1)} collective-permute-done((f32[4,1024]{1,0:T(4,128)S(1)}, f32[4,1024]{1,0:T(4,128)S(1)}, u32[]{:S(2)}, u32[]{:S(2)}) %collective-permute-start.2) | collective-permute-done | bytes 16416 | tf_op jit(solution)/shard_map/ppermute | solution.py:588
  124.6 1.4 collective-permute-start.3
  126.0 3.9 %collective-permute-done.3 = f32[4,1024]{1,0:T(4,128)S(1)} collective-permute-done((f32[4,1024]{1,0:T(4,128)S(1)}, f32[4,1024]{1,0:T(4,128)S(1)}, u32[]{:S(2)}, u32[]{:S(2)}) %collective-permute-start.3) | collective-permute-done | bytes 16416 | tf_op jit(solution)/shard_map/ppermute | solution.py:588
  129.9 0.6 fusion
  130.5 0.0 all-to-all-done.2.parts_hbm
  130.5 15.6 %reduce-scatter.8.cloned.1.call-done.summed_hbm = bf16[8,2048]{1,0:T(8,128)(2,1)} async-done(((bf16[32,2048]{1,0:T(8,128)(2,1)}), bf16[8,2048]{1,0:T(8,128)(2,1)}) %reduce-scatter.8.cloned.1.call-update) | async-done | bytes 32784 | tf_op jit(solution)/shard_map/reduce_scatter | solution.py:545
  146.1 0.8 copy-done.12
  146.8 2.3 %shard_map.135 = (bf16[8,1536]{1,0:T(8,128)(2,1)}, bf16[8,512]{1,0:T(8,128)(2,1)}, bf16[8,1536]{1,0:T(8,128)(2,1)}, bf16[8,512]{1,0:T(8,128)(2,1)}) custom-call(bf16[64,8,2048]{2,1,0:T(8,128)(2,1)} %all-to-all-done.2.parts_hbm, bf16[8,2048]{1,0:T(8,128)(2,1)S(1)} %copy-done.12), custom_call_target="tpu_custom_call" | custom-call | flops 1000000 | bytes 2195456 | tf_op jit(solution)/shard_map/pallas_call | solution.py:412
  (22 shorter events, 0.1 us)
Async XLA Ops:
  7.2 1.9 %copy-start = (bf16[1024,1536]{1,0:T(8,128)(2,1)S(1)}, bf16[1024,1536]{1,0:T(8,128)(2,1)}, u32[]{:S(2)}) copy-start(bf16[1024,1536]{1,0:T(8,128)(2,1)} %entry_hbm.5) | copy-start | bytes 9437188
  9.1 0.9 copy-start.5
  10.0 1.2 copy-start.9
  11.2 0.9 copy-start.11
  12.2 0.7 copy-start.13
  12.9 29.8 %copy-start.17 = (bf16[1024,512]{1,0:T(8,128)(2,1)S(1)}, bf16[1024,512]{1,0:T(8,128)(2,1)}, u32[]{:S(2)}) copy-start(bf16[1024,512]{1,0:T(8,128)(2,1)} %exit_hbm.4) | copy-start | bytes 3145732
  20.9 0.8 copy-start.18
  21.7 0.7 copy-start.20
  22.4 20.3 %all-to-all-start = ((bf16[16,8,2048]{2,1,0:T(8,128)(2,1)}), bf16[16,8,2048]{2,1,0:T(8,128)(2,1)S(1)}, u32[]{:S(2)}, u32[]{:S(2)}) async-start(bf16[16,8,2048]{2,1,0:T(8,128)(2,1)} %bitcast.3), calls=%async_computation | async-start | bytes 1048576 | tf_op jit(solution)/shard_map/all_to_all | solution.py:460
  30.4 60.1 %reduce-scatter.4.cloned.1.call-start = ((), (), s32[]{:S(2)}) async-start(), calls=%async_computation.6 | async-start | bytes 2621440 | tf_op jit(solution)/shard_map/reduce_scatter | solution.py:545
  42.7 1.9 %copy-start.16 = (bf16[1024,1536]{1,0:T(8,128)(2,1)S(1)}, bf16[1024,1536]{1,0:T(8,128)(2,1)}, u32[]{:S(2)}) copy-start(bf16[1024,1536]{1,0:T(8,128)(2,1)} %entry_hbm.4) | copy-start | bytes 9437188
  52.0 2.4 %collective-permute-start.6 = (bf16[128,3072]{1,0:T(8,128)(2,1)S(1)}, bf16[128,3072]{1,0:T(8,128)(2,1)S(1)}, u32[]{:S(2)}, u32[]{:S(2)}) collective-permute-start(bf16[128,3072]{1,0:T(8,128)(2,1)S(1)} %get-tuple-element.39.refs_2_), channel_id=1, source_target_pairs={{0,1},{1,0},{2,3},{3,2},{4,5},{5,4},{6,7},{7,6},{8,9},{9,8},{10,11... | collective-permute-start | bytes 2359304 | tf_op jit(solution)/shard_map/ppermute | solution.py:518
  56.5 12.3 %copy-start.10 = (bf16[1024,512]{1,0:T(8,128)(2,1)S(1)}, bf16[1024,512]{1,0:T(8,128)(2,1)}, u32[]{:S(2)}) copy-start(bf16[1024,512]{1,0:T(8,128)(2,1)} %exit_hbm.5) | copy-start | bytes 3145732
  56.5 12.3 %copy-start.15 = (bf16[1,4,1024]{2,1,0:T(4,128)(2,1)S(1)}, bf16[1,4,1024]{2,1,0:T(4,128)(2,1)}, u32[]{:S(2)}) copy-start(bf16[1,4,1024]{2,1,0:T(4,128)(2,1)} %param.15) | copy-start | bytes 24580
  56.5 12.3 %copy-start.19 = (bf16[144,1536]{1,0:T(8,128)(2,1)S(1)}, bf16[144,1536]{1,0:T(8,128)(2,1)}, u32[]{:S(2)}) copy-start(bf16[144,1536]{1,0:T(8,128)(2,1)} %copy-done.18) | copy-start | bytes 1327108
  68.8 6.4 %copy-start.7 = (bf16[16,8,1024]{2,1,0:T(8,128)(2,1)}, bf16[16,8,1024]{2,1,0:T(8,128)(2,1)S(1)}, u32[]{:S(2)}) copy-start(bf16[16,8,1024]{2,1,0:T(8,128)(2,1)S(1)} %all_to_all.15) | copy-start | bytes 786436
  68.8 6.5 %copy-start.6 = (bf16[1,1,128,1024]{3,2,1,0:T(8,128)(2,1)S(1)}, bf16[1,1,128,1024]{3,2,1,0:T(8,128)(2,1)}, u32[]{:S(2)}) copy-start(bf16[1,1,128,1024]{3,2,1,0:T(8,128)(2,1)} %param.8) | copy-start | bytes 786436
  68.8 6.5 %copy-start.14 = (bf16[1,4,1024]{2,1,0:T(4,128)(2,1)S(1)}, bf16[1,4,1024]{2,1,0:T(4,128)(2,1)}, u32[]{:S(2)}) copy-start(bf16[1,4,1024]{2,1,0:T(4,128)(2,1)} %param.9) | copy-start | bytes 24580
  68.8 6.5 %copy-start.21 = (bf16[144,512]{1,0:T(8,128)(2,1)S(1)}, bf16[144,512]{1,0:T(8,128)(2,1)}, u32[]{:S(2)}) copy-start(bf16[144,512]{1,0:T(8,128)(2,1)} %copy-done.20) | copy-start | bytes 442372
  75.2 6.1 %copy-start.3 = (bf16[144,2048]{1,0:T(8,128)(2,1)}, bf16[144,2048]{1,0:T(8,128)(2,1)S(1)}, u32[]{:S(2)}) copy-start(bf16[144,2048]{1,0:T(8,128)(2,1)S(1)} %get-tuple-element.29.send_hbm.refs_4_) | copy-start | bytes 1769476
  75.2 3.1 %collective-permute-start.5 = (bf16[144,2048]{1,0:T(8,128)(2,1)S(1)}, bf16[144,2048]{1,0:T(8,128)(2,1)S(1)}, u32[]{:S(2)}, u32[]{:S(2)}) collective-permute-start(bf16[144,2048]{1,0:T(8,128)(2,1)S(1)} %get-tuple-element.29.send_hbm.refs_4_), channel_id=1, source_target_pairs={{0,1},{1,0},{2,3},{3,2},{4,5},{5,4},{6,7},{7,6},{8,9},{9,8},{10,11... | collective-permute-start | bytes 1769480 | tf_op jit(solution)/shard_map/ppermute | solution.py:561
  76.3 1.9 %collective-permute-start.4 = (bf16[144,1024]{1,0:T(8,128)(2,1)S(1)}, bf16[144,1024]{1,0:T(8,128)(2,1)S(1)}, u32[]{:S(2)}, u32[]{:S(2)}) collective-permute-start(bf16[144,1024]{1,0:T(8,128)(2,1)S(1)} %get-tuple-element.34.refs_1_), channel_id=1, source_target_pairs={{0,1},{1,0},{2,3},{3,2},{4,5},{5,4},{6,7},{7,6},{8,9},{9,8},{10,11... | collective-permute-start | bytes 884744 | tf_op jit(solution)/shard_map/ppermute | solution.py:491
  81.3 1.3 copy-start.2
  82.6 8.6 %copy-start.1 = (bf16[1024,1536]{1,0:T(8,128)(2,1)S(1)}, bf16[1024,1536]{1,0:T(8,128)(2,1)}, u32[]{:S(2)}) copy-start(bf16[1024,1536]{1,0:T(8,128)(2,1)} %entry_hbm.5) | copy-start | bytes 9437188
  82.6 47.8 %all-to-all-start.2 = ((bf16[64,8,2048]{2,1,0:T(8,128)(2,1)}), bf16[64,8,2048]{2,1,0:T(8,128)(2,1)}, u32[]{:S(2)}, u32[]{:S(2)}) async-start(bf16[64,8,2048]{2,1,0:T(8,128)(2,1)} %bitcast.13), calls=%async_computation.2 | async-start | bytes 4194304 | tf_op jit(solution)/shard_map/all_to_all | solution.py:583
  90.4 30.3 %reduce-scatter.6.cloned.1.call-start = ((), (), s32[]{:S(2)}) async-start(), calls=%async_computation.7 | async-start | bytes 655360 | tf_op jit(solution)/shard_map/reduce_scatter | solution.py:545
  91.1 54.9 %reduce-scatter.8.cloned.1.call-start = ((), (), s32[]{:S(2)}) async-start(), calls=%async_computation.8 | async-start | bytes 163840 | tf_op jit(solution)/shard_map/reduce_scatter | solution.py:545
  91.2 1.1 copy-start.4
  92.3 0.9 copy-start.8
  95.9 1.3 collective-permute-start
  97.1 23.6 %collective-permute-start.1 = (f32[4,1024]{1,0:T(4,128)S(1)}, f32[4,1024]{1,0:T(4,128)S(1)}, u32[]{:S(2)}, u32[]{:S(2)}) collective-permute-start(f32[4,1024]{1,0:T(4,128)S(1)} %slice_add_fusion), channel_id=1, source_target_pairs={{0,2},{2,0},{1,3},{3,1},{4,6},{6,4},{5,7},{7,5},{8,10},{10,8},{9,1... | collective-permute-start | bytes 49160 | tf_op jit(solution)/shard_map/ppermute | solution.py:588
  120.8 3.8 %collective-permute-start.2 = (f32[4,1024]{1,0:T(4,128)S(1)}, f32[4,1024]{1,0:T(4,128)S(1)}, u32[]{:S(2)}, u32[]{:S(2)}) collective-permute-start(f32[4,1024]{1,0:T(4,128)S(1)} %add.19), channel_id=1, source_target_pairs={{0,4},{4,0},{8,12},{12,8},{1,5},{5,1},{9,13},{13,9},{2,6},{6,2},{1... | collective-permute-start | bytes 49160 | tf_op jit(solution)/shard_map/ppermute | solution.py:588
  124.6 5.2 %collective-permute-start.3 = (f32[4,1024]{1,0:T(4,128)S(1)}, f32[4,1024]{1,0:T(4,128)S(1)}, u32[]{:S(2)}, u32[]{:S(2)}) collective-permute-start(f32[4,1024]{1,0:T(4,128)S(1)} %add.20), channel_id=1, source_target_pairs={{0,8},{4,12},{8,0},{12,4},{1,9},{5,13},{9,1},{13,5},{2,10},{6,14},... | collective-permute-start | bytes 49160 | tf_op jit(solution)/shard_map/ppermute | solution.py:588
  146.1 0.8 copy-start.12
Sparse Core Ops, SparseCore 0:
  56.6 21.5 reduce-scatter.3
  93.7 26.9 reduce-scatter.5
  123.2 22.7 reduce-scatter.7

commit v3 on v2

--- a/solution.py
+++ b/solution.py
@@ -1,4 +1,5 @@
 import functools
+import itertools
 import math
 
 import jax
@@ -12,7 +13,6 @@
 HEADS = 8
 EPSILON = 1e-05
 FRAME = ("y", "zh", "c")
-CHIPS = ("zl", "x", "y", "zh")
 ALL = ("zl", "x", "y", "zh", "c")
 BF = jnp.bfloat16
 F32 = jnp.float32
@@ -337,13 +337,12 @@
     finish(outs)
 
 
-def weight_gradient_kernel(places, in_turns, *refs):
-    if in_turns:
-        core_ref, refs = refs[0], refs[1:]
-    arrays, refs = refs[: len(refs) - 7], refs[len(refs) - 7 :]
-    out_hbm, left_n, left_c, right_m, right_a, out, sems = refs
+def weight_gradient_kernel(places, place_ref, *refs):
+    arrays, refs = refs[: len(refs) - 10], refs[len(refs) - 10 :]
+    outs_hbm, (left_n, left_c, right_m, right_a, out, sems) = refs[:4], refs[4:]
     move = Mover(sems)
     rows = left_n.shape[0] // 2
+    share = out.shape[0] // 4
 
     def both(target, pair):
         copies = []
@@ -354,20 +353,22 @@
 
     ready = [both(t, places[k]) for k, t in enumerate((left_c, right_a, left_n, right_m))]
     side = right_a.shape[1]
+    core, place = place_ref[0], place_ref[1]
+    where = []
+    for b in range(32):
+        zl, x, y = b // 16, b // 4 % 4, b % 4
+        on_x = ((x + 4 - place) % 4) * 8 + y * 2 + zl
+        on_y = ((y + 4 - place) % 4) * 8 + x * 2 + zl
+        where.append(pl.multiple_of(jnp.where(core == 0, on_x, on_y) * 16, 16))
     outs = []
 
     def put(at, value):
-        if not in_turns:
-            out[:, at : at + side] = value
-        else:
-            core = core_ref[0]
-            for b in range(32):
-                zl, x, y = b // 16, b // 4 % 4, b % 4
-                turn = jnp.where(core == 0, x * 8 + y * 2 + zl, y * 8 + x * 2 + zl)
-                where = pl.ds(pl.multiple_of(turn * 16, 16), 16)
-                out[where, at : at + side] = value[b * 16 : (b + 1) * 16, :]
+        for b in range(32):
+            out[pl.ds(where[b], 16), at : at + side] = value[b * 16 : (b + 1) * 16, :]
         columns = slice(at, at + side)
-        outs.append(move.start(out.at[:, columns], out_hbm.at[:, columns]))
+        for k in (1, 2, 3, 0):
+            source = out.at[k * share : (k + 1) * share, columns]
+            outs.append(move.start(source, outs_hbm[k].at[:, columns]))
 
     finish(ready[0] + ready[1])
     put(3 * side, mm(left_c[...], right_a[...], TN).astype(BF))
@@ -377,28 +378,66 @@
     finish(outs)
 
 
-def sum_kernel(
-    scale, parts_hbm, summed_hbm, s_entry_hbm, s_exit_hbm, t_entry_hbm, t_exit_hbm,
-    parts, summed, s_entry, s_exit, t_entry, t_exit, sems,
+def add_four(parts, columns):
+    total = parts[0, :, columns].astype(F32)
+    for k in range(1, 4):
+        total = total + parts[k, :, columns].astype(F32)
+    return total.astype(BF)
+
+
+def first_sum_kernel(own_hbm, a_hbm, b_hbm, c_hbm, out_hbm, parts, out, sems):
+    move = Mover(sems)
+    sources = (own_hbm, a_hbm, b_hbm, c_hbm)
+    step = out.shape[1] // 4
+    columns = [slice(j * step, (j + 1) * step) for j in range(4)]
+    copies = [[move.start(r.at[:, c], parts.at[k, :, c]) for k, r in enumerate(sources)] for c in columns]
+    outs = []
+    for c, ready in zip(columns, copies):
+        finish(ready)
+        out[:, c] = add_four(parts, c)
+        outs.append(move.start(out.at[:, c], out_hbm.at[:, c]))
+    finish(outs)
+
+
+def join_kernel(own_hbm, a_hbm, b_hbm, c_hbm, other_hbm, out_hbm, parts, out, sems):
+    move = Mover(sems)
+    sources = (own_hbm, a_hbm, b_hbm, c_hbm)
+    width = parts.shape[2]
+    step = width // 4
+    columns = [slice(j * step, (j + 1) * step) for j in range(4)]
+    copies = [[move.start(r.at[:, c], parts.at[k, :, c]) for k, r in enumerate(sources)] for c in columns]
+    other = move.start(other_hbm, out.at[:, width:])
+    outs = []
+    for c, ready in zip(columns, copies):
+        finish(ready)
+        out[:, c] = add_four(parts, c)
+        outs.append(move.start(out.at[:, c], out_hbm.at[:, c]))
+    other.wait()
+    outs.append(move.start(out.at[:, width:], out_hbm.at[:, width:]))
+    finish(outs)
+
+
+def last_sum_kernel(
+    scale, parts_hbm, s_entry_hbm, s_exit_hbm, t_entry_hbm, t_exit_hbm,
+    parts, s_entry, s_exit, t_entry, t_exit, sems,
 ):
     move = Mover(sems)
     side = s_exit.shape[1]
-    columns = [slice(j * side, (j + 1) * side) for j in range(4)]
+    columns = [slice(j * side, (j + 1) * side) for j in range(8)]
     copies = [move.start(parts_hbm.at[:, :, c], parts.at[:, :, c]) for c in columns]
-    temporal = move.start(summed_hbm, summed)
+    outs = []
     for j, (c, copy) in enumerate(zip(columns, copies)):
         copy.wait()
         total = (jnp.sum(parts[:, :, c].astype(F32), axis=0) * scale).astype(BF)
-        if j < 3:
-            s_entry[:, c] = total
+        entry, exit_ = ((s_entry, s_exit), (t_entry, t_exit))[j // 4]
+        if j % 4 < 3:
+            entry[:, (j % 4) * side : (j % 4 + 1) * side] = total
         else:
-            s_exit[...] = total
-    outs = [move.start(s_entry, s_entry_hbm), move.start(s_exit, s_exit_hbm)]
-    temporal.wait()
-    total = (summed[...].astype(F32) * scale).astype(BF)
-    t_entry[...] = total[:, : 3 * side]
-    t_exit[...] = total[:, 3 * side :]
-    outs += [move.start(t_entry, t_entry_hbm), move.start(t_exit, t_exit_hbm)]
+            exit_[...] = total
+    for value, target in (
+        (s_entry, s_entry_hbm), (s_exit, s_exit_hbm), (t_entry, t_entry_hbm), (t_exit, t_exit_hbm)
+    ):
+        outs.append(move.start(value, target))
     finish(outs)
 
 
@@ -407,8 +446,6 @@
 
 
 def call(kernel, outs, ins, scratch, copies, flops):
-    moved = sum(math.prod(a.shape) * a.dtype.itemsize for a in ins)
-    moved += sum(math.prod(s) * jnp.dtype(d).itemsize for s, d in outs)
     return pl.pallas_call(
         kernel,
         out_shape=tuple(jax.ShapeDtypeStruct(s, d) for s, d in outs),
@@ -416,27 +453,28 @@
         out_specs=tuple(HBM for _ in outs),
         scratch_shapes=[pltpu.VMEM(s, d) for s, d in scratch]
         + [pltpu.SemaphoreType.DMA((copies,))],
-        compiler_params=pltpu.CompilerParams(vmem_limit_bytes=40 * 1024 * 1024),
-        cost_estimate=pl.CostEstimate(flops=flops, bytes_accessed=moved, transcendentals=0),
+        compiler_params=pltpu.CompilerParams(vmem_limit_bytes=(64 * 1024 - 256) * 1024),
+        cost_estimate=pl.CostEstimate(flops=flops, bytes_accessed=1000, transcendentals=0),
     )(*ins)
 
 
-def turns(shape):
-    zls, xs, ys, zhs, cores = (range(n) for n in shape)
-
-    def at(zl, x, y, zh, c):
-        return (((zl * shape[1] + x) * shape[2] + y) * shape[3] + zh) * shape[4] + c
-
-    along_x = [
-        [[at(zl, x, y, zh, c) for x in xs] for zl in zls for y in ys for zh in zhs] for c in cores
-    ]
-    along_y = [
-        [[at(zl, x, y, zh, c) for y in ys] for zl in zls for x in xs for zh in zhs] for c in cores
-    ]
-    along_z = [
-        [at(zl, x, y, zh, c) for zl in zls for zh in zhs] for x in xs for y in ys for c in cores
-    ]
-    return along_x[0] + along_y[1], along_y[0] + along_x[1], along_z
+def index_of(shape, zl, x, y, zh, c):
+    return (((zl * shape[1] + x) * shape[2] + y) * shape[3] + zh) * shape[4] + c
+
+
+def first_pairs(shape, step):
+    pairs = []
+    for zl, x, y, zh, c in itertools.product(*(range(n) for n in shape)):
+        to = (zl, (x + step) % shape[1], y) if c == 0 else (zl, x, (y + step) % shape[2])
+        pairs.append((index_of(shape, zl, x, y, zh, c), index_of(shape, *to, zh, c)))
+    return pairs
+
+
+def second_groups(shape):
+    zls, xs, ys, zhs = (range(n) for n in shape[:4])
+    on_0 = [[index_of(shape, l, x, y, h, 0) for y in ys for l in zls for h in zhs] for x in xs]
+    on_1 = [[index_of(shape, l, x, y, h, 1) for x in xs for l in zls for h in zhs] for y in ys]
+    return on_0 + on_1
 
 
 def per_device(
@@ -447,9 +485,12 @@
     bots, side = bottleneck.shape[1], spatial_exit.shape[1]
     half = width // 2
     frames = lax.axis_size(FRAME)
-    chips = lax.axis_size(CHIPS)
     rows = patches + 16
-    core = lax.axis_index("c").astype(jnp.int32).reshape(1)
+    on = lax.axis_index("c")
+    core = on.astype(jnp.int32).reshape(1)
+    place = jnp.stack([on, jnp.where(on == 0, lax.axis_index("x"), lax.axis_index("y"))])
+    place = place.astype(jnp.int32)
+    shape = [lax.axis_size(a) for a in ALL]
     clips = lax.axis_size(("zl", "x"))
     scale = 1.0 / math.sqrt(clips * frames * patches)
     frame, bottle, joined = frames_in[0, 0], bottleneck[0], joined_grad[0]
@@ -473,7 +514,7 @@
             ((rows, side), BF),
         ],
         10 + HEADS,
-        1_000_000_000,
+        1000,
     )
     moved = exchange(packed)
 
@@ -486,9 +527,10 @@
             ((rows, half + side), BF), ((rows, half), BF),
         ],
         5,
-        300_000_000,
+        1000,
     )
     got_s1 = lax.ppermute(send_s1, "c", swap)
+    moved, got_s1 = lax.optimization_barrier((moved, got_s1))
 
     back, d_mix_t, att_t = call(
         functools.partial(temporal_kernel, frames),
@@ -500,7 +542,7 @@
             ((patches, side), BF), ((patches, 3 * side), BF),
         ],
         8,
-        2_000_000_000,
+        1000,
     )
     back = exchange(back)
 
@@ -513,38 +555,44 @@
             ((patches, width), BF),
         ],
         5,
-        300_000_000,
+        1000,
     )
     got_t = lax.ppermute(send_t, "c", swap)
 
-    def weight_gradient(count, places, arrays, in_turns):
-        return call(
-            functools.partial(weight_gradient_kernel, places, in_turns),
-            [((half, 4 * side), BF)],
-            ([core] if in_turns else []) + arrays,
+    def weight_gradient(count, places, arrays):
+        parts = call(
+            functools.partial(weight_gradient_kernel, places),
+            [((half // 4, 4 * side), BF)] * 4,
+            [place] + arrays,
             [
                 ((2 * count, half), BF), ((2 * count, half), BF), ((2 * count, 3 * side), BF),
                 ((2 * count, side), BF), ((half, 4 * side), BF),
             ],
-            12,
-            1_000_000_000,
-        )[0]
+            24,
+            1000,
+        )
+        return parts
+
+    def passed_on(parts):
+        return [parts[0]] + [
+            lax.ppermute(parts[k], ALL, first_pairs(shape, k)) for k in range(1, 4)
+        ]
 
     cot_at, mix_at = half + side, half + side + half
-    partial_t = weight_gradient(
+    parts_t = weight_gradient(
         patches,
         (
             ((0, half), (2, cot_at)), ((1, half), (2, half)),
             ((0, 0), (2, 0)), ((1, mix_at), (2, mix_at)),
         ),
         [kept_t, send_t, got_t],
-        True,
-    )
-    summed_t = partial_t
-    for groups in turns([lax.axis_size(a) for a in ALL]):
-        summed_t = lax.psum_scatter(
-            summed_t, ALL, scatter_dimension=0, axis_index_groups=groups, tiled=True
-        )
+    )
+    back, *parts_t = lax.optimization_barrier((back, *parts_t))
+    parts_t = passed_on(parts_t)
+    share = (half // 4, 4 * side)
+    (sum_t,) = call(
+        first_sum_kernel, [(share, BF)], parts_t, [((4, *share), BF), (share, BF)], 20, 1000
+    )
 
     send_s2, kept_sc = call(
         functools.partial(spatial_backward_kernel, frames),
@@ -556,48 +604,64 @@
             ((rows, half), BF),
         ],
         6 + HEADS,
-        1_500_000_000,
+        1000,
     )
     got_s2 = lax.ppermute(send_s2, "c", swap)
-    delta, local = call(
-        functools.partial(spatial_inputs_kernel, frames),
-        [((patches, width), BF), ((8, width), F32)],
-        [frame, bottle, back, joined, send_s2, spatial_entry],
-        [
-            ((patches, width), BF), ((bots, width), BF), ((rows, width), BF), ((bots, width), BF),
-            ((rows, 3 * side), BF), ((width, 3 * side), BF), ((rows, width), F32),
-            ((patches, width), BF), ((8, width), F32),
-        ],
-        8,
-        1_000_000_000,
-    )
-    partial_s = weight_gradient(
+    parts_s = weight_gradient(
         rows,
         (
             ((3, 0), (5, 0)), ((1, half), (2, half)),
             ((0, 0), (2, 0)), ((4, half), (5, half)),
         ),
         [kept_sn, send_s1, got_s1, kept_sc, send_s2, got_s2],
-        False,
-    )
-    parts = lax.all_to_all(partial_s.reshape(chips, -1, 4 * side), CHIPS, 0, 0, tiled=True)
-
-    local = local[:bots]
-    for axis, bit in (("c", 1), ("zh", 1), ("y", 1), ("y", 2)):
+    )
+    after, *parts_s = lax.optimization_barrier((send_s2, *parts_s))
+    parts_s = passed_on(parts_s)
+    delta, local = call(
+        functools.partial(spatial_inputs_kernel, frames),
+        [((patches, width), BF), ((bots, width), F32)],
+        [frame, bottle, back, joined, after, spatial_entry],
+        [
+            ((patches, width), BF), ((bots, width), BF), ((rows, width), BF), ((bots, width), BF),
+            ((rows, 3 * side), BF), ((width, 3 * side), BF), ((rows, width), F32),
+            ((patches, width), BF), ((bots, width), F32),
+        ],
+        8,
+        1000,
+    )
+
+    def with_partner(local, axis, bit):
         pairs = [(i, i ^ bit) for i in range(lax.axis_size(axis))]
-        local = local + lax.ppermute(local, axis, pairs)
-
-    own = parts.shape[1]
+        return local + lax.ppermute(local, axis, pairs)
+
+    local = with_partner(with_partner(local, "c", 1), "zh", 1)
+    local, *parts_s = lax.optimization_barrier((local, *parts_s))
+    local = with_partner(with_partner(local, "y", 1), "y", 2)
+    (both,) = call(
+        join_kernel,
+        [((half // 4, 8 * side), BF)],
+        parts_s + [sum_t],
+        [((4, *share), BF), ((half // 4, 8 * side), BF)],
+        22,
+        1000,
+    )
+    groups = second_groups(shape)
+    count = len(groups[0])
+    last = lax.all_to_all(
+        both.reshape(count, -1, 8 * side), ALL, 0, 0, axis_index_groups=groups, tiled=True
+    )
+
+    own = last.shape[1]
     s_entry, s_exit, t_entry, t_exit = call(
-        functools.partial(sum_kernel, scale),
+        functools.partial(last_sum_kernel, scale),
         [((own, 3 * side), BF), ((own, side), BF)] * 2,
-        [parts, summed_t],
-        [
-            (parts.shape, BF), ((own, 4 * side), BF),
+        [last],
+        [
+            (last.shape, BF),
             ((own, 3 * side), BF), ((own, side), BF), ((own, 3 * side), BF), ((own, side), BF),
         ],
-        9,
-        1_000_000,
+        12,
+        1000,
     )
     return (
         delta[None, None], local.astype(BF)[None], s_entry, s_exit, t_entry, t_exit

time: 156 us -> 115 us (0.74)
  waiting for transfers between devices: 61.5 us -> 36.1 us
  local copies, waits for them, and re-layouts: 13.2 us -> 0 us
  between operations: 14.1 us -> 0.96 us
  blocking collectives: 12.2 us -> 0 us
  starting transfers between devices: 21.3 us -> 32.7 us
  Pallas kernels: 32.8 us -> 42.7 us
    reduce_scatter x3 -> x0, waiting for transfers between devices: 36.2 us -> none  [per_device(): lax.psum_scatter(summed_t, ALL, scatter_dimension=0, axis_index_groups=gr...]
    unnamed x44 -> x0, local copies, waits for them, and re-layouts: 13.2 us -> none
    ppermute x4 -> x10, waiting for transfers between devices: 8.79 us -> 21.3 us  [the longest x6 11.9 us: passed_on(): lax.ppermute(parts[k], ALL, first_pairs(shape, k))]
    all_to_all x1 -> x0, blocking collectives: 12.2 us -> none  [exchange(): return lax.all_to_all(blocks, FRAME, 0, 0, tiled=True).reshape(array.shape)]
    ppermute x4 -> x10, starting transfers between devices: 4.53 us -> 15.4 us  [the longest x6 9.03 us: passed_on(): lax.ppermute(parts[k], ALL, first_pairs(shape, k))]
    pallas_call x9 -> x11, Pallas kernels: 32.8 us -> 42.7 us  [call(): pl.pallas_call(kernel, out_shape=tuple((jax.ShapeDtypeStruct(s, d) for s,...]
    all_to_all x1 -> x2, starting transfers between devices: 7.97 us -> 12.2 us  [exchange(): return lax.all_to_all(blocks, FRAME, 0, 0, tiled=True).reshape(array.shape)]
    all_to_all x1, starting transfers between devices: 7.75 us -> 4.35 us  [per_device(): lax.all_to_all(both.reshape(count, -1, 8 * side), ALL, 0, 0, axis_index_g...]
  transfers between devices with their start and end apart: 12 -> 16, of which waited for: 8 -> 9; matrix products, arithmetic and copies ran while one was open for 0% -> 2% of each run, Pallas kernels for 8% -> 15%
where the time goes in v3:
time: 115 us; the launch traced here: 114 us
  Pallas kernels  42.7 us (37%)
  waiting for transfers between devices  36.1 us (31%)
  starting transfers between devices  32.7 us (28%)
  other arithmetic  1.93 us (2%)
    pallas_call x11, Pallas kernels, call(): pl.pallas_call(kernel, out_shape=tuple((jax.ShapeDtypeStruct(s, d) for s,...  42.7 us
    all_to_all x2, waiting for transfers between devices, exchange(): return lax.all_to_all(blocks, FRAME, 0, 0, tiled=True).reshape(array.shape)  12.8 us
    all_to_all x2, starting transfers between devices, exchange(): return lax.all_to_all(blocks, FRAME, 0, 0, tiled=True).reshape(array.shape)  12.2 us
    ppermute x6, waiting for transfers between devices, passed_on(): lax.ppermute(parts[k], ALL, first_pairs(shape, k))  11.9 us
    ppermute x4, waiting for transfers between devices, with_partner(): return local + lax.ppermute(local, axis, pairs)  9.48 us
    ppermute x6, starting transfers between devices, passed_on(): lax.ppermute(parts[k], ALL, first_pairs(shape, k))  9.03 us
    ppermute x4, starting transfers between devices, with_partner(): return local + lax.ppermute(local, axis, pairs)  6.37 us
    all_to_all x1, starting transfers between devices, per_device(): lax.all_to_all(both.reshape(count, -1, 8 * side), ALL, 0, 0, axis_index_g...  4.35 us
  transfers between devices with their start and end apart: 16, of which 9 were waited for; matrix products, arithmetic and copies ran while one was open for 2% of the time, Pallas kernels for 15%

profile of v3, /device:TPU:0, one launch (start us, length us, event | category | flops | bytes accessed | tf_op | source)
XLA Modules:
  0.0 114.3 jit_solution(17880550158929341730)
XLA Ops:
  0.6 4.6 %shard_map.127 = (bf16[128,2048]{1,0:T(8,128)(2,1)}, bf16[144,1536]{1,0:T(8,128)(2,1)}, f32[8,144,144]{2,1,0:T(8,128)}, bf16[144,512]{1,0:T(8,128)(2,1)}) custom-call(bf16[128,1024]{1,0:T(8,128)(2,1)} %bitcast.15, bf16[4,1024]{1,0:T(4,128)(2,1)} %bitcast.21, bf16[1024,1536]{1,0:T(8,128)(2,1)} %entry_hbm.5, bf16[1024,512]{1,0:T(8,128)(2,1)} %exit_hbm.5, ...), custom_call_target="tpu_custom_call" | custom-call | flops 1000 | bytes 1000 | tf_op jit(solution)/shard_map/pallas_call | solution.py:449
  5.3 8.0 %all-to-all-start = ((bf16[16,8,2048]{2,1,0:T(8,128)(2,1)}), bf16[16,8,2048]{2,1,0:T(8,128)(2,1)}, u32[]{:S(2)}, u32[]{:S(2)}) async-start(bf16[16,8,2048]{2,1,0:T(8,128)(2,1)} %bitcast.18), calls=%async_computation | async-start | bytes 1048576 | tf_op jit(solution)/shard_map/all_to_all | solution.py:501
  13.3 2.3 %shard_map.128 = (bf16[144,1024]{1,0:T(8,128)(2,1)}, bf16[144,512]{1,0:T(8,128)(2,1)}) custom-call(s32[1]{0:T(128)} %bitcast.5.core_ref, bf16[128,1024]{1,0:T(8,128)(2,1)} %bitcast.16, bf16[4,1024]{1,0:T(4,128)(2,1)} %bitcast.22, bf16[144,512]{1,0:T(8,128)(2,1)} %get-tuple-element.51.att_hbm), custom_call_target="tpu_custom_call" | custom-call | flops 1000 | bytes 1000 | tf_op jit(solution)/shard_map/pallas_call | solution.py:449
  15.6 0.4 collective-permute-start
  16.0 1.6 %collective-permute-done.refs_2_ = bf16[144,1024]{1,0:T(8,128)(2,1)} collective-permute-done((bf16[144,1024]{1,0:T(8,128)(2,1)}, bf16[144,1024]{1,0:T(8,128)(2,1)}, u32[]{:S(2)}, u32[]{:S(2)}) %collective-permute-start) | collective-permute-done | bytes 294944 | tf_op jit(solution)/shard_map/ppermute | solution.py:532
  17.6 8.1 %all-to-all-done = bf16[16,8,2048]{2,1,0:T(8,128)(2,1)} async-done(((bf16[16,8,2048]{2,1,0:T(8,128)(2,1)}), bf16[16,8,2048]{2,1,0:T(8,128)(2,1)}, u32[]{:S(2)}, u32[]{:S(2)}) %all-to-all-start) | async-done | bytes 524320 | tf_op jit(solution)/shard_map/all_to_all | solution.py:501
  25.7 7.3 %shard_map.129 = (bf16[128,1024]{1,0:T(8,128)(2,1)}, bf16[128,1536]{1,0:T(8,128)(2,1)}, bf16[128,512]{1,0:T(8,128)(2,1)}) custom-call(bf16[128,2048]{1,0:T(8,128)(2,1)} %bitcast.4.moved_hbm, bf16[1024,1536]{1,0:T(8,128)(2,1)} %entry_hbm.4, bf16[1024,512]{1,0:T(8,128)(2,1)} %exit_hbm.4), custom_call_target="tpu_custom_call" | custom-call | flops 1000 | bytes 1000 | tf_op jit(solution)/shard_map/pallas_call | solution.py:449
  33.0 2.6 %shard_map.130 = (bf16[128,3072]{1,0:T(8,128)(2,1)}, bf16[128,1024]{1,0:T(8,128)(2,1)}) custom-call(s32[1]{0:T(128)} %bitcast.5.core_ref, bf16[128,2048]{1,0:T(8,128)(2,1)} %bitcast.4.moved_hbm, bf16[128,512]{1,0:T(8,128)(2,1)} %get-tuple-element.55.att_hbm, bf16[128,1536]{1,0:T(8,128)(2,1)} %get-tuple-element.56.d_mix_hbm), custom_call_target="tpu_custom_call" | custom-call | flops 1000 | bytes 1000 | tf_op jit(solution)/shard_map/pallas_call | solution.py:449
  35.6 0.1 collective-permute-start.1
  35.7 4.2 %all-to-all-start.1 = ((bf16[16,8,1024]{2,1,0:T(8,128)(2,1)}), bf16[16,8,1024]{2,1,0:T(8,128)(2,1)}, u32[]{:S(2)}, u32[]{:S(2)}) async-start(bf16[16,8,1024]{2,1,0:T(8,128)(2,1)} %bitcast.20), calls=%async_computation.1 | async-start | bytes 524288 | tf_op jit(solution)/shard_map/all_to_all | solution.py:501
  39.9 0.6 pad_add_fusion.place_ref
  40.5 0.0 collective-permute-done.1.refs_2_
  40.5 3.9 %shard_map.131 = (bf16[128,2048]{1,0:T(8,128)(2,1)}, bf16[128,2048]{1,0:T(8,128)(2,1)}, bf16[128,2048]{1,0:T(8,128)(2,1)}, bf16[128,2048]{1,0:T(8,128)(2,1)}) custom-call(s32[2]{0:T(128)} %pad_add_fusion.place_ref, bf16[128,1024]{1,0:T(8,128)(2,1)} %get-tuple-element.57.refs_0_, bf16[128,3072]{1,0:T(8,128)(2,1)} %get-tuple-element.58.refs_1_, ...), custom_call_target="tpu_custom_call" | custom-call | flops 1000 | bytes 1000 | tf_op jit(solution)/shard_map/pallas_call | solution.py:449
  44.4 4.7 %all-to-all-done.1 = bf16[16,8,1024]{2,1,0:T(8,128)(2,1)} async-done(((bf16[16,8,1024]{2,1,0:T(8,128)(2,1)}), bf16[16,8,1024]{2,1,0:T(8,128)(2,1)}, u32[]{:S(2)}, u32[]{:S(2)}) %all-to-all-start.1) | async-done | bytes 262176 | tf_op jit(solution)/shard_map/all_to_all | solution.py:501
  49.1 6.2 %shard_map.132 = (bf16[144,2048]{1,0:T(8,128)(2,1)}, bf16[144,512]{1,0:T(8,128)(2,1)}) custom-call(s32[1]{0:T(128)} %bitcast.5.core_ref, bf16[128,1024]{1,0:T(8,128)(2,1)} %bitcast.7.back_hbm, bf16[4,1024]{1,0:T(4,128)(2,1)} %bitcast.24, bf16[144,1536]{1,0:T(8,128)(2,1)} %get-tuple-element.64.mix_hbm, f32[8,144,144]{2,1,0:T(8,128)} %get-tuple-element.65.weights_hbm, ...), custom_call_target="tpu_custom_call" | custom-call | flops 1000 | bytes 1000 | tf_op jit(solution)/shard_map/pallas_call | solution.py:449
  55.3 0.2 collective-permute-start.2
  55.4 1.5 %collective-permute-start.10 = (bf16[128,2048]{1,0:T(8,128)(2,1)}, bf16[128,2048]{1,0:T(8,128)(2,1)}, u32[]{:S(2)}, u32[]{:S(2)}) collective-permute-start(bf16[128,2048]{1,0:T(8,128)(2,1)} %get-tuple-element.87), channel_id=1, source_target_pairs={{0,16},{1,5},{2,18},{3,7},{4,20},{5,9},{6,22},{7,11},{8,24},{9,13}... | collective-permute-start | bytes 1572872 | tf_op jit(solution)/shard_map/ppermute | solution.py:578
  56.9 2.7 %collective-permute-start.11 = (bf16[128,2048]{1,0:T(8,128)(2,1)}, bf16[128,2048]{1,0:T(8,128)(2,1)}, u32[]{:S(2)}, u32[]{:S(2)}) collective-permute-start(bf16[128,2048]{1,0:T(8,128)(2,1)} %get-tuple-element.88), channel_id=1, source_target_pairs={{0,32},{1,9},{2,34},{3,11},{4,36},{5,13},{6,38},{7,15},{8,40},{9,1... | collective-permute-start | bytes 1572872 | tf_op jit(solution)/shard_map/ppermute | solution.py:578
  59.6 0.0 collective-permute-done.2.refs_5_
  59.7 4.3 %shard_map.133 = (bf16[128,2048]{1,0:T(8,128)(2,1)}, bf16[128,2048]{1,0:T(8,128)(2,1)}, bf16[128,2048]{1,0:T(8,128)(2,1)}, bf16[128,2048]{1,0:T(8,128)(2,1)}) custom-call(s32[2]{0:T(128)} %pad_add_fusion.place_ref, bf16[144,512]{1,0:T(8,128)(2,1)} %get-tuple-element.67.refs_0_, bf16[144,1024]{1,0:T(8,128)(2,1)} %get-tuple-element.52.refs_1_, ...), custom_call_target="tpu_custom_call" | custom-call | flops 1000 | bytes 1000 | tf_op jit(solution)/shard_map/pallas_call | solution.py:449
  64.0 4.2 %shard_map.134 = (bf16[128,1024]{1,0:T(8,128)(2,1)}, f32[4,1024]{1,0:T(4,128)}) custom-call(bf16[128,1024]{1,0:T(8,128)(2,1)} %bitcast.17, bf16[4,1024]{1,0:T(4,128)(2,1)} %bitcast.23, bf16[128,1024]{1,0:T(8,128)(2,1)} %bitcast.7.back_hbm, bf16[4,1024]{1,0:T(4,128)(2,1)} %bitcast.25, bf16[144,2048]{1,0:T(8,128)(2,1)} %get-tuple-element.74.refs_4_.send_hbm, ...), custom_call_target="tpu_custom_call" | custom-call | flops 1000 | bytes 1000 | tf_op jit(solution)/shard_map/pallas_call | solution.py:449
  68.2 0.1 collective-permute-start.3
  68.3 1.5 %collective-permute-start.12 = (bf16[128,2048]{1,0:T(8,128)(2,1)}, bf16[128,2048]{1,0:T(8,128)(2,1)}, u32[]{:S(2)}, u32[]{:S(2)}) collective-permute-start(bf16[128,2048]{1,0:T(8,128)(2,1)} %get-tuple-element.89), channel_id=1, source_target_pairs={{0,48},{1,13},{2,50},{3,15},{4,52},{5,1},{6,54},{7,3},{8,56},{9,5}... | collective-permute-start | bytes 1572872 | tf_op jit(solution)/shard_map/ppermute | solution.py:578
  69.8 0.6 collective-permute-start.5
  70.4 0.0 collective-permute-done.10.a_hbm
  70.4 1.3 %collective-permute-start.6 = (bf16[128,2048]{1,0:T(8,128)(2,1)}, bf16[128,2048]{1,0:T(8,128)(2,1)}, u32[]{:S(2)}, u32[]{:S(2)}) collective-permute-start(bf16[128,2048]{1,0:T(8,128)(2,1)} %get-tuple-element.79), channel_id=1, source_target_pairs={{0,32},{1,9},{2,34},{3,11},{4,36},{5,13},{6,38},{7,15},{8,40},{9,1... | collective-permute-start | bytes 1572872 | tf_op jit(solution)/shard_map/ppermute | solution.py:578
  71.7 0.0 collective-permute-done.3
  71.7 1.4 %collective-permute-start.7 = (bf16[128,2048]{1,0:T(8,128)(2,1)}, bf16[128,2048]{1,0:T(8,128)(2,1)}, u32[]{:S(2)}, u32[]{:S(2)}) collective-permute-start(bf16[128,2048]{1,0:T(8,128)(2,1)} %get-tuple-element.80), channel_id=1, source_target_pairs={{0,48},{1,13},{2,50},{3,15},{4,52},{5,1},{6,54},{7,3},{8,56},{9,5}... | collective-permute-start | bytes 1572872 | tf_op jit(solution)/shard_map/ppermute | solution.py:578
  73.1 0.7 add.12
  73.9 0.0 collective-permute-done.11.b_hbm
  73.9 0.9 collective-permute-start.4
  74.8 3.1 %collective-permute-done.12.c_hbm = bf16[128,2048]{1,0:T(8,128)(2,1)} collective-permute-done((bf16[128,2048]{1,0:T(8,128)(2,1)}, bf16[128,2048]{1,0:T(8,128)(2,1)}, u32[]{:S(2)}, u32[]{:S(2)}) %collective-permute-start.12) | collective-permute-done | bytes 524320 | tf_op jit(solution)/shard_map/ppermute | solution.py:578
  77.9 2.5 %shard_map.135.other_hbm = bf16[128,2048]{1,0:T(8,128)(2,1)} custom-call(bf16[128,2048]{1,0:T(8,128)(2,1)} %get-tuple-element.86.own_hbm, bf16[128,2048]{1,0:T(8,128)(2,1)} %collective-permute-done.10.a_hbm, bf16[128,2048]{1,0:T(8,128)(2,1)} %collective-permute-done.11.b_hbm, bf16[128,2048]{1,0:T(8,128)(2,1)} %collective-permute-done.12.c_hbm), custom_call_target="tpu_custom_call" | custom-call | flops 1000 | bytes 1000 | tf_op jit(solution)/shard_map/pallas_call | solution.py:449
  80.4 0.0 collective-permute-done.4
  80.4 5.7 %collective-permute-done.5.a_hbm = bf16[128,2048]{1,0:T(8,128)(2,1)} collective-permute-done((bf16[128,2048]{1,0:T(8,128)(2,1)}, bf16[128,2048]{1,0:T(8,128)(2,1)}, u32[]{:S(2)}, u32[]{:S(2)}) %collective-permute-start.5) | collective-permute-done | bytes 524320 | tf_op jit(solution)/shard_map/ppermute | solution.py:578
  86.1 0.0 collective-permute-done.6.b_hbm
  86.1 3.0 %collective-permute-done.7.c_hbm = bf16[128,2048]{1,0:T(8,128)(2,1)} collective-permute-done((bf16[128,2048]{1,0:T(8,128)(2,1)}, bf16[128,2048]{1,0:T(8,128)(2,1)}, u32[]{:S(2)}, u32[]{:S(2)}) %collective-permute-start.7) | collective-permute-done | bytes 524320 | tf_op jit(solution)/shard_map/ppermute | solution.py:578
  89.2 2.8 %shard_map.136 = bf16[128,4096]{1,0:T(8,128)(2,1)} custom-call(bf16[128,2048]{1,0:T(8,128)(2,1)} %get-tuple-element.82.own_hbm, bf16[128,2048]{1,0:T(8,128)(2,1)} %collective-permute-done.5.a_hbm, bf16[128,2048]{1,0:T(8,128)(2,1)} %collective-permute-done.6.b_hbm, bf16[128,2048]{1,0:T(8,128)(2,1)} %collective-permute-done.7.c_hbm, ...), custom_call_target="tpu_custom_call" | custom-call | flops 1000 | bytes 1000 | tf_op jit(solution)/shard_map/pallas_call | solution.py:449
  92.0 4.3 %all-to-all-start.2 = ((bf16[16,8,4096]{2,1,0:T(8,128)(2,1)}), bf16[16,8,4096]{2,1,0:T(8,128)(2,1)}, u32[]{:S(2)}, u32[]{:S(2)}) async-start(bf16[16,8,4096]{2,1,0:T(8,128)(2,1)} %bitcast.14), calls=%async_computation.2 | async-start | bytes 2097152 | tf_op jit(solution)/shard_map/all_to_all | solution.py:650
  96.3 1.8 %collective-permute-start.8 = (f32[4,1024]{1,0:T(4,128)S(1)}, f32[4,1024]{1,0:T(4,128)S(1)}, u32[]{:S(2)}, u32[]{:S(2)}) collective-permute-start(f32[4,1024]{1,0:T(4,128)S(1)} %add.13), channel_id=1, source_target_pairs={{0,4},{4,0},{8,12},{12,8},{1,5},{5,1},{9,13},{13,9},{2,6},{6,2},{1... | collective-permute-start | bytes 49160 | tf_op jit(solution)/shard_map/ppermute | solution.py:635
  98.1 7.8 %collective-permute-done.8 = f32[4,1024]{1,0:T(4,128)S(1)} collective-permute-done((f32[4,1024]{1,0:T(4,128)S(1)}, f32[4,1024]{1,0:T(4,128)S(1)}, u32[]{:S(2)}, u32[]{:S(2)}) %collective-permute-start.8) | collective-permute-done | bytes 16416 | tf_op jit(solution)/shard_map/ppermute | solution.py:635
  105.9 3.6 %collective-permute-start.9 = (f32[4,1024]{1,0:T(4,128)S(1)}, f32[4,1024]{1,0:T(4,128)S(1)}, u32[]{:S(2)}, u32[]{:S(2)}) collective-permute-start(f32[4,1024]{1,0:T(4,128)S(1)} %add.14), channel_id=1, source_target_pairs={{0,8},{4,12},{8,0},{12,4},{1,9},{5,13},{9,1},{13,5},{2,10},{6,14},... | collective-permute-start | bytes 49160 | tf_op jit(solution)/shard_map/ppermute | solution.py:635
  109.5 1.7 %collective-permute-done.9 = f32[4,1024]{1,0:T(4,128)S(1)} collective-permute-done((f32[4,1024]{1,0:T(4,128)S(1)}, f32[4,1024]{1,0:T(4,128)S(1)}, u32[]{:S(2)}, u32[]{:S(2)}) %collective-permute-start.9) | collective-permute-done | bytes 16416 | tf_op jit(solution)/shard_map/ppermute | solution.py:635
  111.2 0.6 fusion
  111.8 0.3 all-to-all-done.2.parts_hbm
  112.2 2.0 %shard_map.137 = (bf16[8,1536]{1,0:T(8,128)(2,1)}, bf16[8,512]{1,0:T(8,128)(2,1)}, bf16[8,1536]{1,0:T(8,128)(2,1)}, bf16[8,512]{1,0:T(8,128)(2,1)}) custom-call(bf16[16,8,4096]{2,1,0:T(8,128)(2,1)} %all-to-all-done.2.parts_hbm), custom_call_target="tpu_custom_call" | custom-call | flops 1000 | bytes 1000 | tf_op jit(solution)/shard_map/pallas_call | solution.py:449
  (2 shorter events, 0.0 us)
Async XLA Ops:
  5.3 20.5 %all-to-all-start = ((bf16[16,8,2048]{2,1,0:T(8,128)(2,1)}), bf16[16,8,2048]{2,1,0:T(8,128)(2,1)}, u32[]{:S(2)}, u32[]{:S(2)}) async-start(bf16[16,8,2048]{2,1,0:T(8,128)(2,1)} %bitcast.18), calls=%async_computation | async-start | bytes 1048576 | tf_op jit(solution)/shard_map/all_to_all | solution.py:501
  15.6 2.0 %collective-permute-start = (bf16[144,1024]{1,0:T(8,128)(2,1)}, bf16[144,1024]{1,0:T(8,128)(2,1)}, u32[]{:S(2)}, u32[]{:S(2)}) collective-permute-start(bf16[144,1024]{1,0:T(8,128)(2,1)} %get-tuple-element.52.refs_1_), channel_id=1, source_target_pairs={{0,1},{1,0},{2,3},{3,2},{4,5},{5,4},{6,7},{7,6},{8,9},{9,8},{10,11... | collective-permute-start | bytes 884744 | tf_op jit(solution)/shard_map/ppermute | solution.py:532
  35.6 4.9 %collective-permute-start.1 = (bf16[128,3072]{1,0:T(8,128)(2,1)}, bf16[128,3072]{1,0:T(8,128)(2,1)}, u32[]{:S(2)}, u32[]{:S(2)}) collective-permute-start(bf16[128,3072]{1,0:T(8,128)(2,1)} %get-tuple-element.58.refs_1_), channel_id=1, source_target_pairs={{0,1},{1,0},{2,3},{3,2},{4,5},{5,4},{6,7},{7,6},{8,9},{9,8},{10,11... | collective-permute-start | bytes 2359304 | tf_op jit(solution)/shard_map/ppermute | solution.py:560
  35.7 13.4 %all-to-all-start.1 = ((bf16[16,8,1024]{2,1,0:T(8,128)(2,1)}), bf16[16,8,1024]{2,1,0:T(8,128)(2,1)}, u32[]{:S(2)}, u32[]{:S(2)}) async-start(bf16[16,8,1024]{2,1,0:T(8,128)(2,1)} %bitcast.20), calls=%async_computation.1 | async-start | bytes 524288 | tf_op jit(solution)/shard_map/all_to_all | solution.py:501
  55.3 4.4 %collective-permute-start.2 = (bf16[144,2048]{1,0:T(8,128)(2,1)}, bf16[144,2048]{1,0:T(8,128)(2,1)}, u32[]{:S(2)}, u32[]{:S(2)}) collective-permute-start(bf16[144,2048]{1,0:T(8,128)(2,1)} %get-tuple-element.74.refs_4_.send_hbm), channel_id=1, source_target_pairs={{0,1},{1,0},{2,3},{3,2},{4,5},{5,4},{6,7},{7,6},{8,9},{9,8},{10,11... | collective-permute-start | bytes 1769480 | tf_op jit(solution)/shard_map/ppermute | solution.py:609
  55.4 15.0 %collective-permute-start.10 = (bf16[128,2048]{1,0:T(8,128)(2,1)}, bf16[128,2048]{1,0:T(8,128)(2,1)}, u32[]{:S(2)}, u32[]{:S(2)}) collective-permute-start(bf16[128,2048]{1,0:T(8,128)(2,1)} %get-tuple-element.87), channel_id=1, source_target_pairs={{0,16},{1,5},{2,18},{3,7},{4,20},{5,9},{6,22},{7,11},{8,24},{9,13}... | collective-permute-start | bytes 1572872 | tf_op jit(solution)/shard_map/ppermute | solution.py:578
  56.9 16.9 %collective-permute-start.11 = (bf16[128,2048]{1,0:T(8,128)(2,1)}, bf16[128,2048]{1,0:T(8,128)(2,1)}, u32[]{:S(2)}, u32[]{:S(2)}) collective-permute-start(bf16[128,2048]{1,0:T(8,128)(2,1)} %get-tuple-element.88), channel_id=1, source_target_pairs={{0,32},{1,9},{2,34},{3,11},{4,36},{5,13},{6,38},{7,15},{8,40},{9,1... | collective-permute-start | bytes 1572872 | tf_op jit(solution)/shard_map/ppermute | solution.py:578
  68.2 3.5 %collective-permute-start.3 = (f32[4,1024]{1,0:T(4,128)}, f32[4,1024]{1,0:T(4,128)S(1)}, u32[]{:S(2)}, u32[]{:S(2)}) collective-permute-start(f32[4,1024]{1,0:T(4,128)} %get-tuple-element.76), channel_id=1, source_target_pairs={{0,1},{1,0},{2,3},{3,2},{4,5},{5,4},{6,7},{7,6},{8,9},{9,8},{10,11... | collective-permute-start | bytes 49160 | tf_op jit(solution)/shard_map/ppermute | solution.py:635
  68.3 9.6 %collective-permute-start.12 = (bf16[128,2048]{1,0:T(8,128)(2,1)}, bf16[128,2048]{1,0:T(8,128)(2,1)}, u32[]{:S(2)}, u32[]{:S(2)}) collective-permute-start(bf16[128,2048]{1,0:T(8,128)(2,1)} %get-tuple-element.89), channel_id=1, source_target_pairs={{0,48},{1,13},{2,50},{3,15},{4,52},{5,1},{6,54},{7,3},{8,56},{9,5}... | collective-permute-start | bytes 1572872 | tf_op jit(solution)/shard_map/ppermute | solution.py:578
  69.8 16.3 %collective-permute-start.5 = (bf16[128,2048]{1,0:T(8,128)(2,1)}, bf16[128,2048]{1,0:T(8,128)(2,1)}, u32[]{:S(2)}, u32[]{:S(2)}) collective-permute-start(bf16[128,2048]{1,0:T(8,128)(2,1)} %get-tuple-element.78), channel_id=1, source_target_pairs={{0,16},{1,5},{2,18},{3,7},{4,20},{5,9},{6,22},{7,11},{8,24},{9,13}... | collective-permute-start | bytes 1572872 | tf_op jit(solution)/shard_map/ppermute | solution.py:578
  70.4 15.7 %collective-permute-start.6 = (bf16[128,2048]{1,0:T(8,128)(2,1)}, bf16[128,2048]{1,0:T(8,128)(2,1)}, u32[]{:S(2)}, u32[]{:S(2)}) collective-permute-start(bf16[128,2048]{1,0:T(8,128)(2,1)} %get-tuple-element.79), channel_id=1, source_target_pairs={{0,32},{1,9},{2,34},{3,11},{4,36},{5,13},{6,38},{7,15},{8,40},{9,1... | collective-permute-start | bytes 1572872 | tf_op jit(solution)/shard_map/ppermute | solution.py:578
  71.7 17.4 %collective-permute-start.7 = (bf16[128,2048]{1,0:T(8,128)(2,1)}, bf16[128,2048]{1,0:T(8,128)(2,1)}, u32[]{:S(2)}, u32[]{:S(2)}) collective-permute-start(bf16[128,2048]{1,0:T(8,128)(2,1)} %get-tuple-element.80), channel_id=1, source_target_pairs={{0,48},{1,13},{2,50},{3,15},{4,52},{5,1},{6,54},{7,3},{8,56},{9,5}... | collective-permute-start | bytes 1572872 | tf_op jit(solution)/shard_map/ppermute | solution.py:578
  73.9 6.5 %collective-permute-start.4 = (f32[4,1024]{1,0:T(4,128)S(1)}, f32[4,1024]{1,0:T(4,128)S(1)}, u32[]{:S(2)}, u32[]{:S(2)}) collective-permute-start(f32[4,1024]{1,0:T(4,128)S(1)} %add.12), channel_id=1, source_target_pairs={{0,2},{2,0},{1,3},{3,1},{4,6},{6,4},{5,7},{7,5},{8,10},{10,8},{9,1... | collective-permute-start | bytes 49160 | tf_op jit(solution)/shard_map/ppermute | solution.py:635
  92.0 20.2 %all-to-all-start.2 = ((bf16[16,8,4096]{2,1,0:T(8,128)(2,1)}), bf16[16,8,4096]{2,1,0:T(8,128)(2,1)}, u32[]{:S(2)}, u32[]{:S(2)}) async-start(bf16[16,8,4096]{2,1,0:T(8,128)(2,1)} %bitcast.14), calls=%async_computation.2 | async-start | bytes 2097152 | tf_op jit(solution)/shard_map/all_to_all | solution.py:650
  96.3 9.5 %collective-permute-start.8 = (f32[4,1024]{1,0:T(4,128)S(1)}, f32[4,1024]{1,0:T(4,128)S(1)}, u32[]{:S(2)}, u32[]{:S(2)}) collective-permute-start(f32[4,1024]{1,0:T(4,128)S(1)} %add.13), channel_id=1, source_target_pairs={{0,4},{4,0},{8,12},{12,8},{1,5},{5,1},{9,13},{13,9},{2,6},{6,2},{1... | collective-permute-start | bytes 49160 | tf_op jit(solution)/shard_map/ppermute | solution.py:635
  105.9 5.3 %collective-permute-start.9 = (f32[4,1024]{1,0:T(4,128)S(1)}, f32[4,1024]{1,0:T(4,128)S(1)}, u32[]{:S(2)}, u32[]{:S(2)}) collective-permute-start(f32[4,1024]{1,0:T(4,128)S(1)} %add.14), channel_id=1, source_target_pairs={{0,8},{4,12},{8,0},{12,4},{1,9},{5,13},{9,1},{13,5},{2,10},{6,14},... | collective-permute-start | bytes 49160 | tf_op jit(solution)/shard_map/ppermute | solution.py:635

commit v4 on v3

--- a/solution.py
+++ b/solution.py
@@ -48,13 +48,12 @@
         v2 = mix_ref[:, 2 * side + p * width : 2 * side + (p + 1) * width]
         total = None
         for h in range(2):
-            scores = mm(q2 * masks[h], k2, NT) * factor
+            scores = mm(k2 * masks[h], q2, NT) * factor
             scores = jnp.where(keep, scores, -jnp.inf)
-            scores = scores - jnp.max(scores, axis=-1, keepdims=True)
-            expon = jnp.exp(scores)
-            weights = expon / jnp.sum(expon, axis=-1, keepdims=True)
+            expon = jnp.exp(scores - jnp.max(scores, axis=0, keepdims=True))
+            weights = expon * (1.0 / jnp.sum(expon, axis=0, keepdims=True))
             save(2 * p + h, weights)
-            part = mm(weights.astype(BF), v2 * masks[h], NN)
+            part = mm(weights.astype(BF), v2 * masks[h], TN)
             total = part if total is None else total + part
         put(p, width, total.astype(BF))
 
@@ -72,12 +71,12 @@
         for h in range(2):
             dh = d2 * masks[h]
             weights = load(2 * p + h)
-            grad = mm(dh, v2, NT)
-            centre = jnp.sum(weights * grad, axis=-1, keepdims=True)
+            grad = mm(v2, dh, NT)
+            centre = jnp.sum(weights * grad, axis=0, keepdims=True)
             ds = (weights * (grad - centre) * factor).astype(BF)
-            a = mm(ds, k2 * masks[h], NN)
-            b = mm(ds, q2 * masks[h], TN)
-            c = mm(weights.astype(BF), dh, TN)
+            a = mm(ds, k2 * masks[h], TN)
+            b = mm(ds, q2 * masks[h], NN)
+            c = mm(weights.astype(BF), dh, NN)
             dq = a if dq is None else dq + a
             dk = b if dk is None else dk + b
             dv = c if dv is None else dv + c
@@ -155,7 +154,7 @@
         mix[:, c] = mm(low, entry[:, c], NN).astype(BF)
     outs.append(move.start(mix, mix_hbm))
     masks = half_masks(side // HEADS)
-    keep = lax.broadcasted_iota(jnp.int32, (rows, rows), 1) < patches + bots
+    keep = lax.broadcasted_iota(jnp.int32, (rows, rows), 0) < patches + bots
 
     def save(h, weights):
         weights_buf[h] = weights
@@ -195,23 +194,31 @@
 
 
 def temporal_kernel(
-    frames, moved_hbm, entry_hbm, exit_hbm, back_hbm, d_mix_hbm, att_hbm,
-    moved, entry, exit_, back, mix, weights_buf, att, d_mix, sems,
+    frames, core_ref, moved_hbm, entry_hbm, exit_hbm, back_hbm, send_hbm, kept_hbm,
+    moved, entry, exit_, back, mix, weights_buf, send, kept, sems,
 ):
     move = Mover(sems)
     rows, width = back.shape
-    side = exit_.shape[1]
+    half, side = width // 2, exit_.shape[1]
     seqs = rows // frames
     first = move.start(moved_hbm, moved)
     columns = [slice(j * side, (j + 1) * side) for j in range(3)]
     entries = [move.start(entry_hbm.at[:, c], entry.at[:, c]) for c in columns]
     later = move.start(exit_hbm, exit_)
+    core = core_ref[0]
+    other, own = picker(1 - core), picker(core)
     first.wait()
+    cot = moved[:, width : 2 * width]
     normed, inverse = normalize(moved[:, 0:width].astype(F32))
     low = normed.astype(BF)
+    pick(cot, other, send, half + side)
+    pick(cot, own, kept, half)
     for c, copy in zip(columns, entries):
         copy.wait()
         mix[:, c] = mm(low, entry[:, c], NN).astype(BF)
+    pick(low, other, send, 0)
+    pick(low, own, kept, 0)
+    outs = [move.start(kept, kept_hbm)]
     masks = half_masks(side // HEADS)
     keep = (
         lax.broadcasted_iota(jnp.int32, (rows, rows), 0) % seqs
@@ -222,49 +229,21 @@
         weights_buf[h] = weights
 
     def put(p, w, value):
-        att[:, p * w : (p + 1) * w] = value
+        send[:, half + p * w : half + (p + 1) * w] = value
 
     attention_forward(mix, keep, masks, save, put)
-    outs = [move.start(att, att_hbm)]
     later.wait()
-    cot = moved[:, width : 2 * width]
     d_att = mm(cot, exit_[...], NN).astype(BF)
+    at_mix = width + side
 
     def put_grad(at, w, value):
-        d_mix[:, at : at + w] = value
+        send[:, at_mix + at : at_mix + at + w] = value
 
     attention_backward(mix, lambda h: weights_buf[h], d_att, masks, put_grad)
-    outs.append(move.start(d_mix, d_mix_hbm))
-    d_normed = mm(d_mix[...], entry[...], NT)
+    outs.append(move.start(send, send_hbm))
+    d_normed = mm(send[:, at_mix:], entry[...], NT)
     back[...] = inputs_gradient(cot, normed, inverse, d_normed).astype(BF)
     outs.append(move.start(back, back_hbm))
-    finish(outs)
-
-
-def temporal_factors_kernel(
-    core_ref, moved_hbm, att_hbm, d_mix_hbm, send_hbm, kept_hbm, moved, send, kept, sems
-):
-    move = Mover(sems)
-    width = moved.shape[1] // 2
-    half, side = width // 2, att_hbm.shape[1]
-    first = move.start(moved_hbm, moved)
-    copied = [
-        move.start(att_hbm, send.at[:, half : half + side]),
-        move.start(d_mix_hbm, send.at[:, width + side : width + 4 * side]),
-    ]
-    first.wait()
-    low = normalize(moved[:, 0:width].astype(F32))[0].astype(BF)
-    cot = moved[:, width : 2 * width]
-    core = core_ref[0]
-    other = picker(1 - core)
-    pick(low, other, send, 0)
-    pick(cot, other, send, half + side)
-    finish(copied)
-    outs = [move.start(send, send_hbm)]
-    own = picker(core)
-    pick(low, own, kept, 0)
-    pick(cot, own, kept, half)
-    outs.append(move.start(kept, kept_hbm))
     finish(outs)
 
 
@@ -399,33 +378,51 @@
     finish(outs)
 
 
-def join_kernel(own_hbm, a_hbm, b_hbm, c_hbm, other_hbm, out_hbm, parts, out, sems):
+def join_kernel(
+    own_hbm, a_hbm, b_hbm, c_hbm, other_hbm, local_hbm, out_hbm, parts, out, local, twice, sems
+):
     move = Mover(sems)
     sources = (own_hbm, a_hbm, b_hbm, c_hbm)
     width = parts.shape[2]
     step = width // 4
     columns = [slice(j * step, (j + 1) * step) for j in range(4)]
+    bottle = move.start(local_hbm, local)
+    other = move.start(other_hbm, out.at[:, width : 2 * width])
     copies = [[move.start(r.at[:, c], parts.at[k, :, c]) for k, r in enumerate(sources)] for c in columns]
-    other = move.start(other_hbm, out.at[:, width:])
-    outs = []
+    bottle.wait()
+    bots, half = local.shape[0], twice.shape[1]
+    for k in range(16 // bots):
+        twice[k * bots : (k + 1) * bots, :] = local[:, k % 2 * half : (k % 2 + 1) * half]
+    rows = twice[...].astype(BF)
+    for k in range(out.shape[0] // 16):
+        out[16 * k : 16 * (k + 1), 2 * width :] = rows
+    outs = [move.start(out.at[:, 2 * width :], out_hbm.at[:, 2 * width :])]
+    other.wait()
+    outs.append(move.start(out.at[:, width : 2 * width], out_hbm.at[:, width : 2 * width]))
     for c, ready in zip(columns, copies):
         finish(ready)
         out[:, c] = add_four(parts, c)
         outs.append(move.start(out.at[:, c], out_hbm.at[:, c]))
-    other.wait()
-    outs.append(move.start(out.at[:, width:], out_hbm.at[:, width:]))
     finish(outs)
 
 
 def last_sum_kernel(
-    scale, parts_hbm, s_entry_hbm, s_exit_hbm, t_entry_hbm, t_exit_hbm,
-    parts, s_entry, s_exit, t_entry, t_exit, sems,
+    scale, place_ref, parts_hbm, bottle_hbm, s_entry_hbm, s_exit_hbm, t_entry_hbm, t_exit_hbm,
+    parts, rows, bottle, s_entry, s_exit, t_entry, t_exit, sems,
 ):
     move = Mover(sems)
     side = s_exit.shape[1]
+    first = move.start(parts_hbm.at[:, :, 8 * side :], rows)
     columns = [slice(j * side, (j + 1) * side) for j in range(8)]
     copies = [move.start(parts_hbm.at[:, :, c], parts.at[:, :, c]) for c in columns]
     outs = []
+    first.wait()
+    zl = place_ref[2]
+    total = jnp.zeros(bottle.shape, F32)
+    for k in range(rows.shape[0] // 2):
+        total = total + rows[(k // 2) * 4 + zl * 2 + k % 2].astype(F32)
+    bottle[...] = total.astype(BF)
+    outs.append(move.start(bottle, bottle_hbm))
     for j, (c, copy) in enumerate(zip(columns, copies)):
         copy.wait()
         total = (jnp.sum(parts[:, :, c].astype(F32), axis=0) * scale).astype(BF)
@@ -488,7 +485,8 @@
     rows = patches + 16
     on = lax.axis_index("c")
     core = on.astype(jnp.int32).reshape(1)
-    place = jnp.stack([on, jnp.where(on == 0, lax.axis_index("x"), lax.axis_index("y"))])
+    first = jnp.where(on == 0, lax.axis_index("x"), lax.axis_index("y"))
+    place = jnp.stack([on, first, lax.axis_index("zl")])
     place = place.astype(jnp.int32)
     shape = [lax.axis_size(a) for a in ALL]
     clips = lax.axis_size(("zl", "x"))
@@ -532,31 +530,21 @@
     got_s1 = lax.ppermute(send_s1, "c", swap)
     moved, got_s1 = lax.optimization_barrier((moved, got_s1))
 
-    back, d_mix_t, att_t = call(
+    factors = half + side + half + 3 * side
+    back, send_t, kept_t = call(
         functools.partial(temporal_kernel, frames),
-        [((patches, width), BF), ((patches, 3 * side), BF), ((patches, side), BF)],
-        [moved, temporal_entry, temporal_exit],
+        [((patches, width), BF), ((patches, factors), BF), ((patches, width), BF)],
+        [core, moved, temporal_entry, temporal_exit],
         [
             ((patches, 2 * width), BF), ((width, 3 * side), BF), ((width, side), BF),
             ((patches, width), BF), ((patches, 3 * side), BF), ((HEADS, patches, patches), F32),
-            ((patches, side), BF), ((patches, 3 * side), BF),
+            ((patches, factors), BF), ((patches, width), BF),
         ],
         8,
         1000,
     )
     back = exchange(back)
 
-    send_t, kept_t = call(
-        temporal_factors_kernel,
-        [((patches, half + side + half + 3 * side), BF), ((patches, width), BF)],
-        [core, moved, att_t, d_mix_t],
-        [
-            ((patches, 2 * width), BF), ((patches, half + side + half + 3 * side), BF),
-            ((patches, width), BF),
-        ],
-        5,
-        1000,
-    )
     got_t = lax.ppermute(send_t, "c", swap)
 
     def weight_gradient(count, places, arrays):
@@ -587,8 +575,8 @@
         ),
         [kept_t, send_t, got_t],
     )
-    back, *parts_t = lax.optimization_barrier((back, *parts_t))
     parts_t = passed_on(parts_t)
+    back, parts_t[0] = lax.optimization_barrier((back, parts_t[0]))
     share = (half // 4, 4 * side)
     (sum_t,) = call(
         first_sum_kernel, [(share, BF)], parts_t, [((4, *share), BF), (share, BF)], 20, 1000
@@ -615,7 +603,8 @@
         ),
         [kept_sn, send_s1, got_s1, kept_sc, send_s2, got_s2],
     )
-    after, *parts_s = lax.optimization_barrier((send_s2, *parts_s))
+    after, sum_t, stays = lax.optimization_barrier((send_s2, sum_t, parts_s[0]))
+    parts_s = (stays, *parts_s[1:])
     parts_s = passed_on(parts_s)
     delta, local = call(
         functools.partial(spatial_inputs_kernel, frames),
@@ -634,37 +623,41 @@
         pairs = [(i, i ^ bit) for i in range(lax.axis_size(axis))]
         return local + lax.ppermute(local, axis, pairs)
 
-    local = with_partner(with_partner(local, "c", 1), "zh", 1)
-    local, *parts_s = lax.optimization_barrier((local, *parts_s))
-    local = with_partner(with_partner(local, "y", 1), "y", 2)
+    local = with_partner(local, "c", 1)
+    wide = 8 * side + width // 2
     (both,) = call(
         join_kernel,
-        [((half // 4, 8 * side), BF)],
-        parts_s + [sum_t],
-        [((4, *share), BF), ((half // 4, 8 * side), BF)],
-        22,
+        [((half // 4, wide), BF)],
+        parts_s + [sum_t, local],
+        [
+            ((4, *share), BF), ((half // 4, wide), BF), ((bots, width), F32),
+            ((16, width // 2), F32),
+        ],
+        24,
         1000,
     )
     groups = second_groups(shape)
     count = len(groups[0])
     last = lax.all_to_all(
-        both.reshape(count, -1, 8 * side), ALL, 0, 0, axis_index_groups=groups, tiled=True
-    )
-
+        both.reshape(count, -1, wide), ALL, 0, 0, axis_index_groups=groups, tiled=True
+    )
+    halves = (2 * bots, width // 2)
     own = last.shape[1]
-    s_entry, s_exit, t_entry, t_exit = call(
+    total, s_entry, s_exit, t_entry, t_exit = call(
         functools.partial(last_sum_kernel, scale),
-        [((own, 3 * side), BF), ((own, side), BF)] * 2,
-        [last],
-        [
-            (last.shape, BF),
+        [(halves, BF)] + [((own, 3 * side), BF), ((own, side), BF)] * 2,
+        [place, last],
+        [
+            ((count, own, 8 * side), BF), ((count, *halves), BF), (halves, BF),
             ((own, 3 * side), BF), ((own, side), BF), ((own, 3 * side), BF), ((own, side), BF),
         ],
-        12,
+        14,
         1000,
     )
+    total = jnp.where(on == 0, total, lax.ppermute(total, "c", [(0, 1)]))
+    local = jnp.concatenate([total[:bots], total[bots:]], axis=1)
     return (
-        delta[None, None], local.astype(BF)[None], s_entry, s_exit, t_entry, t_exit
+        delta[None, None], local[None], s_entry, s_exit, t_entry, t_exit
     )
 
 

time: 115 us -> 112 us (0.974)
  blocking collectives: 0 us -> 20.7 us
  waiting for transfers between devices: 36.1 us -> 22.2 us
  starting transfers between devices: 32.7 us -> 23.6 us
  Pallas kernels: 42.7 us -> 40.1 us
  other arithmetic: 1.93 us -> 3.29 us
    all_to_all x0 -> x1, blocking collectives: none -> 20.7 us  [per_device(): lax.all_to_all(both.reshape(count, -1, wide), ALL, 0, 0, axis_index_group...]
    ppermute x4 -> x1, waiting for transfers between devices: 9.48 us -> 1.38 us  [with_partner(): return local + lax.ppermute(local, axis, pairs)]
    ppermute x6, waiting for transfers between devices: 11.9 us -> 5.4 us  [passed_on(): lax.ppermute(parts[k], ALL, first_pairs(shape, k))]
    ppermute x4 -> x1, starting transfers between devices: 6.37 us -> 0.08 us  [with_partner(): return local + lax.ppermute(local, axis, pairs)]
    all_to_all x1 -> x0, starting transfers between devices: 4.35 us -> none  [per_device(): lax.all_to_all(both.reshape(count, -1, 8 * side), ALL, 0, 0, axis_index_g...]
    pallas_call x11 -> x10, Pallas kernels: 42.7 us -> 40.1 us  [call(): pl.pallas_call(kernel, out_shape=tuple((jax.ShapeDtypeStruct(s, d) for s,...]
    ppermute x0 -> x1, starting transfers between devices: none -> 1.29 us  [per_device(): total = jnp.where(on == 0, total, lax.ppermute(total, 'c', [(0, 1)]))]
  transfers between devices with their start and end apart: 16 -> 13, of which waited for: 9 -> 7; matrix products, arithmetic and copies ran while one was open for 2% -> 2% of each run, Pallas kernels for 15% -> 16%
where the time goes in v4:
time: 112 us; the launch traced here: 111 us
  Pallas kernels  40.1 us (36%)
  starting transfers between devices  23.6 us (21%)
  waiting for transfers between devices  22.2 us (20%)
  blocking collectives  20.7 us (18%)
  other arithmetic  3.29 us (3%)
    pallas_call x10, Pallas kernels, call(): pl.pallas_call(kernel, out_shape=tuple((jax.ShapeDtypeStruct(s, d) for s,...  40.1 us
    all_to_all x1, blocking collectives, per_device(): lax.all_to_all(both.reshape(count, -1, wide), ALL, 0, 0, axis_index_group...  20.7 us
    all_to_all x2, waiting for transfers between devices, exchange(): return lax.all_to_all(blocks, FRAME, 0, 0, tiled=True).reshape(array.shape)  12.8 us
    all_to_all x2, starting transfers between devices, exchange(): return lax.all_to_all(blocks, FRAME, 0, 0, tiled=True).reshape(array.shape)  12.2 us
    ppermute x6, starting transfers between devices, passed_on(): lax.ppermute(parts[k], ALL, first_pairs(shape, k))  9.26 us
    ppermute x6, waiting for transfers between devices, passed_on(): lax.ppermute(parts[k], ALL, first_pairs(shape, k))  5.4 us
  transfers between devices with their start and end apart: 13, of which 7 were waited for; matrix products, arithmetic and copies ran while one was open for 2% of the time, Pallas kernels for 16%

profile of v4, /device:TPU:0, one launch (start us, length us, event | category | flops | bytes accessed | tf_op | source)
XLA Modules:
  0.0 110.6 jit_solution(11864429558502448067)
XLA Ops:
  0.6 4.6 %shard_map.127 = (bf16[128,2048]{1,0:T(8,128)(2,1)}, bf16[144,1536]{1,0:T(8,128)(2,1)}, f32[8,144,144]{2,1,0:T(8,128)}, bf16[144,512]{1,0:T(8,128)(2,1)}) custom-call(bf16[128,1024]{1,0:T(8,128)(2,1)} %bitcast.16, bf16[4,1024]{1,0:T(4,128)(2,1)} %bitcast.22, bf16[1024,1536]{1,0:T(8,128)(2,1)} %entry_hbm.5, bf16[1024,512]{1,0:T(8,128)(2,1)} %exit_hbm.5, ...), custom_call_target="tpu_custom_call" | custom-call | flops 1000 | bytes 1000 | tf_op jit(solution)/shard_map/pallas_call | solution.py:446
  5.2 8.0 %all-to-all-start = ((bf16[16,8,2048]{2,1,0:T(8,128)(2,1)}), bf16[16,8,2048]{2,1,0:T(8,128)(2,1)}, u32[]{:S(2)}, u32[]{:S(2)}) async-start(bf16[16,8,2048]{2,1,0:T(8,128)(2,1)} %bitcast.19), calls=%async_computation | async-start | bytes 1048576 | tf_op jit(solution)/shard_map/all_to_all | solution.py:499
  13.3 2.3 %shard_map.128 = (bf16[144,1024]{1,0:T(8,128)(2,1)}, bf16[144,512]{1,0:T(8,128)(2,1)}) custom-call(s32[1]{0:T(128)} %bitcast.2.core_ref, bf16[128,1024]{1,0:T(8,128)(2,1)} %bitcast.17, bf16[4,1024]{1,0:T(4,128)(2,1)} %bitcast.23, bf16[144,512]{1,0:T(8,128)(2,1)} %get-tuple-element.40.att_hbm), custom_call_target="tpu_custom_call" | custom-call | flops 1000 | bytes 1000 | tf_op jit(solution)/shard_map/pallas_call | solution.py:446
  15.6 0.4 collective-permute-start
  16.0 1.6 %collective-permute-done.refs_2_ = bf16[144,1024]{1,0:T(8,128)(2,1)} collective-permute-done((bf16[144,1024]{1,0:T(8,128)(2,1)}, bf16[144,1024]{1,0:T(8,128)(2,1)}, u32[]{:S(2)}, u32[]{:S(2)}) %collective-permute-start) | collective-permute-done | bytes 294944 | tf_op jit(solution)/shard_map/ppermute | solution.py:530
  17.6 8.1 %all-to-all-done = bf16[16,8,2048]{2,1,0:T(8,128)(2,1)} async-done(((bf16[16,8,2048]{2,1,0:T(8,128)(2,1)}), bf16[16,8,2048]{2,1,0:T(8,128)(2,1)}, u32[]{:S(2)}, u32[]{:S(2)}) %all-to-all-start) | async-done | bytes 524320 | tf_op jit(solution)/shard_map/all_to_all | solution.py:499
  25.7 7.0 %shard_map.129 = (bf16[128,1024]{1,0:T(8,128)(2,1)}, bf16[128,3072]{1,0:T(8,128)(2,1)}, bf16[128,1024]{1,0:T(8,128)(2,1)}) custom-call(s32[1]{0:T(128)} %bitcast.2.core_ref, bf16[128,2048]{1,0:T(8,128)(2,1)} %bitcast.5.moved_hbm, bf16[1024,1536]{1,0:T(8,128)(2,1)} %entry_hbm.4, bf16[1024,512]{1,0:T(8,128)(2,1)} %exit_hbm.4), custom_call_target="tpu_custom_call" | custom-call | flops 1000 | bytes 1000 | tf_op jit(solution)/shard_map/pallas_call | solution.py:446
  32.7 0.1 collective-permute-start.1
  32.8 4.2 %all-to-all-start.1 = ((bf16[16,8,1024]{2,1,0:T(8,128)(2,1)}), bf16[16,8,1024]{2,1,0:T(8,128)(2,1)}, u32[]{:S(2)}, u32[]{:S(2)}) async-start(bf16[16,8,1024]{2,1,0:T(8,128)(2,1)} %bitcast.21), calls=%async_computation.1 | async-start | bytes 524288 | tf_op jit(solution)/shard_map/all_to_all | solution.py:499
  37.0 0.7 pad_add_fusion.place_ref
  37.7 0.0 collective-permute-done.1.refs_2_
  37.7 3.8 %shard_map.130 = (bf16[128,2048]{1,0:T(8,128)(2,1)}, bf16[128,2048]{1,0:T(8,128)(2,1)}, bf16[128,2048]{1,0:T(8,128)(2,1)}, bf16[128,2048]{1,0:T(8,128)(2,1)}) custom-call(s32[3]{0:T(128)} %pad_add_fusion.place_ref, bf16[128,1024]{1,0:T(8,128)(2,1)} %get-tuple-element.44.refs_0_, bf16[128,3072]{1,0:T(8,128)(2,1)} %get-tuple-element.45.refs_1_, ...), custom_call_target="tpu_custom_call" | custom-call | flops 1000 | bytes 1000 | tf_op jit(solution)/shard_map/pallas_call | solution.py:446
  41.5 4.7 %all-to-all-done.1 = bf16[16,8,1024]{2,1,0:T(8,128)(2,1)} async-done(((bf16[16,8,1024]{2,1,0:T(8,128)(2,1)}), bf16[16,8,1024]{2,1,0:T(8,128)(2,1)}, u32[]{:S(2)}, u32[]{:S(2)}) %all-to-all-start.1) | async-done | bytes 262176 | tf_op jit(solution)/shard_map/all_to_all | solution.py:499
  46.2 5.9 %shard_map.131 = (bf16[144,2048]{1,0:T(8,128)(2,1)}, bf16[144,512]{1,0:T(8,128)(2,1)}) custom-call(s32[1]{0:T(128)} %bitcast.2.core_ref, bf16[128,1024]{1,0:T(8,128)(2,1)} %bitcast.7.back_hbm, bf16[4,1024]{1,0:T(4,128)(2,1)} %bitcast.25, bf16[144,1536]{1,0:T(8,128)(2,1)} %get-tuple-element.48.mix_hbm, f32[8,144,144]{2,1,0:T(8,128)} %get-tuple-element.49.weights_hbm, ...), custom_call_target="tpu_custom_call" | custom-call | flops 1000 | bytes 1000 | tf_op jit(solution)/shard_map/pallas_call | solution.py:446
  52.1 0.2 collective-permute-start.5
  52.3 1.5 %collective-permute-start.2 = (bf16[128,2048]{1,0:T(8,128)(2,1)}, bf16[128,2048]{1,0:T(8,128)(2,1)}, u32[]{:S(2)}, u32[]{:S(2)}) collective-permute-start(bf16[128,2048]{1,0:T(8,128)(2,1)} %get-tuple-element.52), channel_id=1, source_target_pairs={{0,16},{1,5},{2,18},{3,7},{4,20},{5,9},{6,22},{7,11},{8,24},{9,13}... | collective-permute-start | bytes 1572872 | tf_op jit(solution)/shard_map/ppermute | solution.py:566
  53.7 2.7 %collective-permute-start.3 = (bf16[128,2048]{1,0:T(8,128)(2,1)}, bf16[128,2048]{1,0:T(8,128)(2,1)}, u32[]{:S(2)}, u32[]{:S(2)}) collective-permute-start(bf16[128,2048]{1,0:T(8,128)(2,1)} %get-tuple-element.53), channel_id=1, source_target_pairs={{0,32},{1,9},{2,34},{3,11},{4,36},{5,13},{6,38},{7,15},{8,40},{9,1... | collective-permute-start | bytes 1572872 | tf_op jit(solution)/shard_map/ppermute | solution.py:566
  56.5 1.4 %collective-permute-start.4 = (bf16[128,2048]{1,0:T(8,128)(2,1)}, bf16[128,2048]{1,0:T(8,128)(2,1)}, u32[]{:S(2)}, u32[]{:S(2)}) collective-permute-start(bf16[128,2048]{1,0:T(8,128)(2,1)} %get-tuple-element.54), channel_id=1, source_target_pairs={{0,48},{1,13},{2,50},{3,15},{4,52},{5,1},{6,54},{7,3},{8,56},{9,5}... | collective-permute-start | bytes 1572872 | tf_op jit(solution)/shard_map/ppermute | solution.py:566
  57.9 0.0 collective-permute-done.5.refs_5_
  57.9 4.4 %shard_map.133 = (bf16[128,2048]{1,0:T(8,128)(2,1)}, bf16[128,2048]{1,0:T(8,128)(2,1)}, bf16[128,2048]{1,0:T(8,128)(2,1)}, bf16[128,2048]{1,0:T(8,128)(2,1)}) custom-call(s32[3]{0:T(128)} %pad_add_fusion.place_ref, bf16[144,512]{1,0:T(8,128)(2,1)} %get-tuple-element.55.refs_0_, bf16[144,1024]{1,0:T(8,128)(2,1)} %get-tuple-element.41.refs_1_, ...), custom_call_target="tpu_custom_call" | custom-call | flops 1000 | bytes 1000 | tf_op jit(solution)/shard_map/pallas_call | solution.py:446
  62.3 0.8 collective-permute-start.6
  63.1 0.9 collective-permute-start.7
  64.0 0.0 collective-permute-done.2.a_hbm
  64.0 1.9 %collective-permute-start.8 = (bf16[128,2048]{1,0:T(8,128)(2,1)}, bf16[128,2048]{1,0:T(8,128)(2,1)}, u32[]{:S(2)}, u32[]{:S(2)}) collective-permute-start(bf16[128,2048]{1,0:T(8,128)(2,1)} %get-tuple-element.64), channel_id=1, source_target_pairs={{0,48},{1,13},{2,50},{3,15},{4,52},{5,1},{6,54},{7,3},{8,56},{9,5}... | collective-permute-start | bytes 1572872 | tf_op jit(solution)/shard_map/ppermute | solution.py:566
  65.9 3.8 %collective-permute-done.3.b_hbm = bf16[128,2048]{1,0:T(8,128)(2,1)} collective-permute-done((bf16[128,2048]{1,0:T(8,128)(2,1)}, bf16[128,2048]{1,0:T(8,128)(2,1)}, u32[]{:S(2)}, u32[]{:S(2)}) %collective-permute-start.3) | collective-permute-done | bytes 524320 | tf_op jit(solution)/shard_map/ppermute | solution.py:566
  69.7 0.0 collective-permute-done.4.c_hbm
  69.7 2.5 %shard_map.132.other_hbm = bf16[128,2048]{1,0:T(8,128)(2,1)} custom-call(bf16[128,2048]{1,0:T(8,128)(2,1)} %get-tuple-element.51.own_hbm, bf16[128,2048]{1,0:T(8,128)(2,1)} %collective-permute-done.2.a_hbm, bf16[128,2048]{1,0:T(8,128)(2,1)} %collective-permute-done.3.b_hbm, bf16[128,2048]{1,0:T(8,128)(2,1)} %collective-permute-done.4.c_hbm), custom_call_target="tpu_custom_call" | custom-call | flops 1000 | bytes 1000 | tf_op jit(solution)/shard_map/pallas_call | solution.py:446
  72.2 4.2 %shard_map.134 = (bf16[128,1024]{1,0:T(8,128)(2,1)}, f32[4,1024]{1,0:T(4,128)}) custom-call(bf16[128,1024]{1,0:T(8,128)(2,1)} %bitcast.18, bf16[4,1024]{1,0:T(4,128)(2,1)} %bitcast.24, bf16[128,1024]{1,0:T(8,128)(2,1)} %bitcast.7.back_hbm, bf16[4,1024]{1,0:T(4,128)(2,1)} %bitcast.26, bf16[144,2048]{1,0:T(8,128)(2,1)} %get-tuple-element.59.refs_4_.send_hbm, ...), custom_call_target="tpu_custom_call" | custom-call | flops 1000 | bytes 1000 | tf_op jit(solution)/shard_map/pallas_call | solution.py:446
  76.4 0.1 collective-permute-start.9
  76.5 1.4 %collective-permute-done.9 = f32[4,1024]{1,0:T(4,128)S(1)} collective-permute-done((f32[4,1024]{1,0:T(4,128)}, f32[4,1024]{1,0:T(4,128)S(1)}, u32[]{:S(2)}, u32[]{:S(2)}) %collective-permute-start.9) | collective-permute-done | bytes 16416 | tf_op jit(solution)/shard_map/ppermute | solution.py:624
  77.9 1.3 %add.3.local_hbm = f32[4,1024]{1,0:T(4,128)} add(f32[4,1024]{1,0:T(4,128)} %get-tuple-element.66, f32[4,1024]{1,0:T(4,128)S(1)} %collective-permute-done.9) | non-fusion elementwise | flops 4096 | bytes 49152 | tf_op jit(solution)/shard_map/add | solution.py:624
  79.2 0.0 collective-permute-done.6.a_hbm
  79.2 1.6 %collective-permute-done.7.b_hbm = bf16[128,2048]{1,0:T(8,128)(2,1)} collective-permute-done((bf16[128,2048]{1,0:T(8,128)(2,1)}, bf16[128,2048]{1,0:T(8,128)(2,1)}, u32[]{:S(2)}, u32[]{:S(2)}) %collective-permute-start.7) | collective-permute-done | bytes 524320 | tf_op jit(solution)/shard_map/ppermute | solution.py:566
  80.8 0.0 collective-permute-done.8.c_hbm
  80.8 2.7 %shard_map.135 = bf16[128,4608]{1,0:T(8,128)(2,1)} custom-call(bf16[128,2048]{1,0:T(8,128)(2,1)} %get-tuple-element.61.own_hbm, bf16[128,2048]{1,0:T(8,128)(2,1)} %collective-permute-done.6.a_hbm, bf16[128,2048]{1,0:T(8,128)(2,1)} %collective-permute-done.7.b_hbm, bf16[128,2048]{1,0:T(8,128)(2,1)} %collective-permute-done.8.c_hbm, ...), custom_call_target="tpu_custom_call" | custom-call | flops 1000 | bytes 1000 | tf_op jit(solution)/shard_map/pallas_call | solution.py:446
  83.6 20.7 %all_to_all.15.parts_hbm = bf16[16,8,4608]{2,1,0:T(8,128)(2,1)} all-to-all(bf16[16,8,4608]{2,1,0:T(8,128)(2,1)} %bitcast.15), channel_id=1, replica_groups={{0,2,64,66,4,6,68,70,8,10,72,74,12,14,76,78},{16,18,80,82,20,22,84,86,2..., dimensions={0} | all-to-all | bytes 2359296 | tf_op jit(solution)/shard_map/all_to_all | solution.py:641
  104.3 2.7 %shard_map.136 = (bf16[8,512]{1,0:T(8,128)(2,1)}, bf16[8,1536]{1,0:T(8,128)(2,1)}, bf16[8,512]{1,0:T(8,128)(2,1)}, bf16[8,1536]{1,0:T(8,128)(2,1)}, bf16[8,512]{1,0:T(8,128)(2,1)}) custom-call(s32[3]{0:T(128)} %pad_add_fusion.place_ref, bf16[16,8,4608]{2,1,0:T(8,128)(2,1)} %all_to_all.15.parts_hbm), custom_call_target="tpu_custom_call" | custom-call | flops 1000 | bytes 1000 | tf_op jit(solution)/shard_map/pallas_call | solution.py:446
  107.0 1.3 %collective-permute-start.10 = (bf16[8,512]{1,0:T(8,128)(2,1)}, bf16[8,512]{1,0:T(8,128)(2,1)S(1)}, u32[]{:S(2)}, u32[]{:S(2)}) collective-permute-start(bf16[8,512]{1,0:T(8,128)(2,1)} %get-tuple-element.67), channel_id=1, source_target_pairs={{0,1},{2,3},{4,5},{6,7},{8,9},{10,11},{12,13},{14,15},{16,17},{18,... | collective-permute-start | bytes 24584 | tf_op jit(solution)/shard_map/ppermute | solution.py:657
  108.3 1.0 collective-permute-done.10
  109.3 0.7 broadcast_select_fusion
  110.0 0.6 maximum_bitcast_fusion
  (1 shorter events, 0.0 us)
Async XLA Ops:
  5.2 20.5 %all-to-all-start = ((bf16[16,8,2048]{2,1,0:T(8,128)(2,1)}), bf16[16,8,2048]{2,1,0:T(8,128)(2,1)}, u32[]{:S(2)}, u32[]{:S(2)}) async-start(bf16[16,8,2048]{2,1,0:T(8,128)(2,1)} %bitcast.19), calls=%async_computation | async-start | bytes 1048576 | tf_op jit(solution)/shard_map/all_to_all | solution.py:499
  15.6 2.0 %collective-permute-start = (bf16[144,1024]{1,0:T(8,128)(2,1)}, bf16[144,1024]{1,0:T(8,128)(2,1)}, u32[]{:S(2)}, u32[]{:S(2)}) collective-permute-start(bf16[144,1024]{1,0:T(8,128)(2,1)} %get-tuple-element.41.refs_1_), channel_id=1, source_target_pairs={{0,1},{1,0},{2,3},{3,2},{4,5},{5,4},{6,7},{7,6},{8,9},{9,8},{10,11... | collective-permute-start | bytes 884744 | tf_op jit(solution)/shard_map/ppermute | solution.py:530
  32.7 5.0 %collective-permute-start.1 = (bf16[128,3072]{1,0:T(8,128)(2,1)}, bf16[128,3072]{1,0:T(8,128)(2,1)}, u32[]{:S(2)}, u32[]{:S(2)}) collective-permute-start(bf16[128,3072]{1,0:T(8,128)(2,1)} %get-tuple-element.45.refs_1_), channel_id=1, source_target_pairs={{0,1},{1,0},{2,3},{3,2},{4,5},{5,4},{6,7},{7,6},{8,9},{9,8},{10,11... | collective-permute-start | bytes 2359304 | tf_op jit(solution)/shard_map/ppermute | solution.py:548
  32.8 13.4 %all-to-all-start.1 = ((bf16[16,8,1024]{2,1,0:T(8,128)(2,1)}), bf16[16,8,1024]{2,1,0:T(8,128)(2,1)}, u32[]{:S(2)}, u32[]{:S(2)}) async-start(bf16[16,8,1024]{2,1,0:T(8,128)(2,1)} %bitcast.21), calls=%async_computation.1 | async-start | bytes 524288 | tf_op jit(solution)/shard_map/all_to_all | solution.py:499
  52.1 5.8 %collective-permute-start.5 = (bf16[144,2048]{1,0:T(8,128)(2,1)}, bf16[144,2048]{1,0:T(8,128)(2,1)}, u32[]{:S(2)}, u32[]{:S(2)}) collective-permute-start(bf16[144,2048]{1,0:T(8,128)(2,1)} %get-tuple-element.59.refs_4_.send_hbm), channel_id=1, source_target_pairs={{0,1},{1,0},{2,3},{3,2},{4,5},{5,4},{6,7},{7,6},{8,9},{9,8},{10,11... | collective-permute-start | bytes 1769480 | tf_op jit(solution)/shard_map/ppermute | solution.py:597
  52.3 11.7 %collective-permute-start.2 = (bf16[128,2048]{1,0:T(8,128)(2,1)}, bf16[128,2048]{1,0:T(8,128)(2,1)}, u32[]{:S(2)}, u32[]{:S(2)}) collective-permute-start(bf16[128,2048]{1,0:T(8,128)(2,1)} %get-tuple-element.52), channel_id=1, source_target_pairs={{0,16},{1,5},{2,18},{3,7},{4,20},{5,9},{6,22},{7,11},{8,24},{9,13}... | collective-permute-start | bytes 1572872 | tf_op jit(solution)/shard_map/ppermute | solution.py:566
  53.7 15.9 %collective-permute-start.3 = (bf16[128,2048]{1,0:T(8,128)(2,1)}, bf16[128,2048]{1,0:T(8,128)(2,1)}, u32[]{:S(2)}, u32[]{:S(2)}) collective-permute-start(bf16[128,2048]{1,0:T(8,128)(2,1)} %get-tuple-element.53), channel_id=1, source_target_pairs={{0,32},{1,9},{2,34},{3,11},{4,36},{5,13},{6,38},{7,15},{8,40},{9,1... | collective-permute-start | bytes 1572872 | tf_op jit(solution)/shard_map/ppermute | solution.py:566
  56.5 13.2 %collective-permute-start.4 = (bf16[128,2048]{1,0:T(8,128)(2,1)}, bf16[128,2048]{1,0:T(8,128)(2,1)}, u32[]{:S(2)}, u32[]{:S(2)}) collective-permute-start(bf16[128,2048]{1,0:T(8,128)(2,1)} %get-tuple-element.54), channel_id=1, source_target_pairs={{0,48},{1,13},{2,50},{3,15},{4,52},{5,1},{6,54},{7,3},{8,56},{9,5}... | collective-permute-start | bytes 1572872 | tf_op jit(solution)/shard_map/ppermute | solution.py:566
  62.3 17.0 %collective-permute-start.6 = (bf16[128,2048]{1,0:T(8,128)(2,1)}, bf16[128,2048]{1,0:T(8,128)(2,1)}, u32[]{:S(2)}, u32[]{:S(2)}) collective-permute-start(bf16[128,2048]{1,0:T(8,128)(2,1)} %get-tuple-element.62), channel_id=1, source_target_pairs={{0,16},{1,5},{2,18},{3,7},{4,20},{5,9},{6,22},{7,11},{8,24},{9,13}... | collective-permute-start | bytes 1572872 | tf_op jit(solution)/shard_map/ppermute | solution.py:566
  63.1 17.7 %collective-permute-start.7 = (bf16[128,2048]{1,0:T(8,128)(2,1)}, bf16[128,2048]{1,0:T(8,128)(2,1)}, u32[]{:S(2)}, u32[]{:S(2)}) collective-permute-start(bf16[128,2048]{1,0:T(8,128)(2,1)} %get-tuple-element.63), channel_id=1, source_target_pairs={{0,32},{1,9},{2,34},{3,11},{4,36},{5,13},{6,38},{7,15},{8,40},{9,1... | collective-permute-start | bytes 1572872 | tf_op jit(solution)/shard_map/ppermute | solution.py:566
  64.0 16.8 %collective-permute-start.8 = (bf16[128,2048]{1,0:T(8,128)(2,1)}, bf16[128,2048]{1,0:T(8,128)(2,1)}, u32[]{:S(2)}, u32[]{:S(2)}) collective-permute-start(bf16[128,2048]{1,0:T(8,128)(2,1)} %get-tuple-element.64), channel_id=1, source_target_pairs={{0,48},{1,13},{2,50},{3,15},{4,52},{5,1},{6,54},{7,3},{8,56},{9,5}... | collective-permute-start | bytes 1572872 | tf_op jit(solution)/shard_map/ppermute | solution.py:566
  76.4 1.5 %collective-permute-start.9 = (f32[4,1024]{1,0:T(4,128)}, f32[4,1024]{1,0:T(4,128)S(1)}, u32[]{:S(2)}, u32[]{:S(2)}) collective-permute-start(f32[4,1024]{1,0:T(4,128)} %get-tuple-element.66), channel_id=1, source_target_pairs={{0,1},{1,0},{2,3},{3,2},{4,5},{5,4},{6,7},{7,6},{8,9},{9,8},{10,11... | collective-permute-start | bytes 49160 | tf_op jit(solution)/shard_map/ppermute | solution.py:624
  107.0 2.3 %collective-permute-start.10 = (bf16[8,512]{1,0:T(8,128)(2,1)}, bf16[8,512]{1,0:T(8,128)(2,1)S(1)}, u32[]{:S(2)}, u32[]{:S(2)}) collective-permute-start(bf16[8,512]{1,0:T(8,128)(2,1)} %get-tuple-element.67), channel_id=1, source_target_pairs={{0,1},{2,3},{4,5},{6,7},{8,9},{10,11},{12,13},{14,15},{16,17},{18,... | collective-permute-start | bytes 24584 | tf_op jit(solution)/shard_map/ppermute | solution.py:657

commit v5 on v4

--- a/solution.py
+++ b/solution.py
@@ -255,11 +255,12 @@
 
 
 def spatial_backward_kernel(
-    frames, core_ref, back_hbm, joined_hbm, mix_hbm, weights_hbm, exit_hbm, send_hbm, kept_hbm,
-    cot, joined, mix, weights_buf, exit_, send, kept, sems,
-):
-    move = Mover(sems)
-    side, half = exit_.shape[1], kept.shape[1]
+    frames, core_ref, back_hbm, joined_hbm, mix_hbm, weights_hbm, exit_hbm,
+    picked_hbm, kept_hbm, d_mix_hbm,
+    cot, joined, mix, weights_buf, exit_, picked, kept, d_mix, sems,
+):
+    move = Mover(sems)
+    side = exit_.shape[1]
     patches = back_hbm.shape[0]
     first = [move.start(joined_hbm, joined), move.start(back_hbm, cot.at[0:patches, :])]
     first.append(move.start(exit_hbm, exit_))
@@ -272,7 +273,8 @@
     core = core_ref[0]
     pick(c, picker(core), kept, 0)
     outs = [move.start(kept, kept_hbm)]
-    pick(c, picker(1 - core), send, 0)
+    pick(c, picker(1 - core), picked, 0)
+    outs.append(move.start(picked, picked_hbm))
     masks = half_masks(side // HEADS)
     second.wait()
 
@@ -281,39 +283,53 @@
         return weights_buf[h]
 
     def put_grad(at, w, value):
-        send[:, half + at : half + at + w] = value
+        d_mix[:, at : at + w] = value
 
     attention_backward(mix, load, d_att, masks, put_grad)
-    outs.append(move.start(send, send_hbm))
-    finish(outs)
-
-
-def spatial_inputs_kernel(
-    frames_count, frames_hbm, bottle_hbm, back_hbm, joined_hbm, send_hbm, entry_hbm,
-    delta_hbm, local_hbm, frames, bottle, cot, joined, d_mix, entry, tokens, delta, local, sems,
-):
-    move = Mover(sems)
-    patches, width = delta.shape
-    half = send_hbm.shape[1] - d_mix.shape[1]
-    first = [move.start(frames_hbm, frames), move.start(bottle_hbm, bottle)]
+    outs.append(move.start(d_mix, d_mix_hbm))
+    finish(outs)
+
+
+def bottle_inputs_kernel(
+    frames_count, bottle_hbm, joined_hbm, d_mix_hbm, entry_hbm, local_hbm,
+    bottle, joined, d_mix, entry, tokens, local, sems,
+):
+    move = Mover(sems)
+    bots = bottle.shape[0]
     second = [
-        move.start(send_hbm.at[:, half:], d_mix),
         move.start(entry_hbm, entry),
-        move.start(joined_hbm, joined),
-        move.start(back_hbm, cot.at[0:patches, :]),
+        move.start(d_mix_hbm.at[d_mix_hbm.shape[0] - 16 :, :], d_mix),
     ]
+    first = [move.start(bottle_hbm, bottle), move.start(joined_hbm, joined)]
     finish(first)
-    fill_tokens(tokens, frames, bottle)
+    tokens[...] = jnp.zeros(tokens.shape, F32)
+    tokens[0:bots, :] = bottle[...].astype(F32)
     normed, inverse = normalize(tokens[...])
+    c = (joined[...].astype(F32) / frames_count).astype(BF)
     finish(second)
-    fill_cotangent(cot, joined, frames_count)
     d_normed = mm(d_mix[...], entry[...], NT)
-    grads = inputs_gradient(cot[...], normed, inverse, d_normed)
-    delta[...] = grads[0:patches, :].astype(BF)
-    outs = [move.start(delta, delta_hbm)]
-    local[...] = grads[patches : patches + local.shape[0], :]
-    outs.append(move.start(local, local_hbm))
-    finish(outs)
+    grads = inputs_gradient(c, normed[0:bots], inverse[0:bots], d_normed[0:bots])
+    local[...] = grads
+    move.start(local, local_hbm).wait()
+
+
+def patch_inputs_kernel(
+    frames_hbm, back_hbm, d_mix_hbm, entry_hbm, delta_hbm,
+    frames, cot, d_mix, entry, delta, sems,
+):
+    move = Mover(sems)
+    first = move.start(frames_hbm, frames)
+    second = [
+        move.start(d_mix_hbm.at[0 : d_mix.shape[0], :], d_mix),
+        move.start(entry_hbm, entry),
+        move.start(back_hbm, cot),
+    ]
+    first.wait()
+    normed, inverse = normalize(frames[...].astype(F32))
+    finish(second)
+    d_normed = mm(d_mix[...], entry[...], NT)
+    delta[...] = inputs_gradient(cot[...], normed, inverse, d_normed).astype(BF)
+    move.start(delta, delta_hbm).wait()
 
 
 def weight_gradient_kernel(places, place_ref, *refs):
@@ -352,8 +368,9 @@
     finish(ready[0] + ready[1])
     put(3 * side, mm(left_c[...], right_a[...], TN).astype(BF))
     finish(ready[2] + ready[3])
+    product = mm(left_n[...], right_m[...], TN).astype(BF)
     for j in range(3):
-        put(j * side, mm(left_n[...], right_m[:, j * side : (j + 1) * side], TN).astype(BF))
+        put(j * side, product[:, j * side : (j + 1) * side])
     finish(outs)
 
 
@@ -378,51 +395,33 @@
     finish(outs)
 
 
-def join_kernel(
-    own_hbm, a_hbm, b_hbm, c_hbm, other_hbm, local_hbm, out_hbm, parts, out, local, twice, sems
-):
+def join_kernel(own_hbm, a_hbm, b_hbm, c_hbm, other_hbm, out_hbm, parts, out, sems):
     move = Mover(sems)
     sources = (own_hbm, a_hbm, b_hbm, c_hbm)
     width = parts.shape[2]
     step = width // 4
     columns = [slice(j * step, (j + 1) * step) for j in range(4)]
-    bottle = move.start(local_hbm, local)
-    other = move.start(other_hbm, out.at[:, width : 2 * width])
     copies = [[move.start(r.at[:, c], parts.at[k, :, c]) for k, r in enumerate(sources)] for c in columns]
-    bottle.wait()
-    bots, half = local.shape[0], twice.shape[1]
-    for k in range(16 // bots):
-        twice[k * bots : (k + 1) * bots, :] = local[:, k % 2 * half : (k % 2 + 1) * half]
-    rows = twice[...].astype(BF)
-    for k in range(out.shape[0] // 16):
-        out[16 * k : 16 * (k + 1), 2 * width :] = rows
-    outs = [move.start(out.at[:, 2 * width :], out_hbm.at[:, 2 * width :])]
-    other.wait()
-    outs.append(move.start(out.at[:, width : 2 * width], out_hbm.at[:, width : 2 * width]))
+    other = move.start(other_hbm, out.at[:, width:])
+    outs = []
     for c, ready in zip(columns, copies):
         finish(ready)
         out[:, c] = add_four(parts, c)
         outs.append(move.start(out.at[:, c], out_hbm.at[:, c]))
+    other.wait()
+    outs.append(move.start(out.at[:, width:], out_hbm.at[:, width:]))
     finish(outs)
 
 
 def last_sum_kernel(
-    scale, place_ref, parts_hbm, bottle_hbm, s_entry_hbm, s_exit_hbm, t_entry_hbm, t_exit_hbm,
-    parts, rows, bottle, s_entry, s_exit, t_entry, t_exit, sems,
+    scale, parts_hbm, s_entry_hbm, s_exit_hbm, t_entry_hbm, t_exit_hbm,
+    parts, s_entry, s_exit, t_entry, t_exit, sems,
 ):
     move = Mover(sems)
     side = s_exit.shape[1]
-    first = move.start(parts_hbm.at[:, :, 8 * side :], rows)
     columns = [slice(j * side, (j + 1) * side) for j in range(8)]
     copies = [move.start(parts_hbm.at[:, :, c], parts.at[:, :, c]) for c in columns]
     outs = []
-    first.wait()
-    zl = place_ref[2]
-    total = jnp.zeros(bottle.shape, F32)
-    for k in range(rows.shape[0] // 2):
-        total = total + rows[(k // 2) * 4 + zl * 2 + k % 2].astype(F32)
-    bottle[...] = total.astype(BF)
-    outs.append(move.start(bottle, bottle_hbm))
     for j, (c, copy) in enumerate(zip(columns, copies)):
         copy.wait()
         total = (jnp.sum(parts[:, :, c].astype(F32), axis=0) * scale).astype(BF)
@@ -450,7 +449,7 @@
         out_specs=tuple(HBM for _ in outs),
         scratch_shapes=[pltpu.VMEM(s, d) for s, d in scratch]
         + [pltpu.SemaphoreType.DMA((copies,))],
-        compiler_params=pltpu.CompilerParams(vmem_limit_bytes=(64 * 1024 - 256) * 1024),
+        compiler_params=pltpu.CompilerParams(vmem_limit_bytes=(64 * 1024 - 128) * 1024),
         cost_estimate=pl.CostEstimate(flops=flops, bytes_accessed=1000, transcendentals=0),
     )(*ins)
 
@@ -486,7 +485,7 @@
     on = lax.axis_index("c")
     core = on.astype(jnp.int32).reshape(1)
     first = jnp.where(on == 0, lax.axis_index("x"), lax.axis_index("y"))
-    place = jnp.stack([on, first, lax.axis_index("zl")])
+    place = jnp.stack([on, first])
     place = place.astype(jnp.int32)
     shape = [lax.axis_size(a) for a in ALL]
     clips = lax.axis_size(("zl", "x"))
@@ -578,44 +577,40 @@
     parts_t = passed_on(parts_t)
     back, parts_t[0] = lax.optimization_barrier((back, parts_t[0]))
     share = (half // 4, 4 * side)
-    (sum_t,) = call(
-        first_sum_kernel, [(share, BF)], parts_t, [((4, *share), BF), (share, BF)], 20, 1000
-    )
-
-    send_s2, kept_sc = call(
+    send_sc, kept_sc, d_mix_s = call(
         functools.partial(spatial_backward_kernel, frames),
-        [((rows, half + 3 * side), BF), ((rows, half), BF)],
+        [((rows, half), BF), ((rows, half), BF), ((rows, 3 * side), BF)],
         [core, back, joined, mix, weights, spatial_exit],
         [
             ((rows, width), BF), ((bots, width), BF), ((rows, 3 * side), BF),
-            ((HEADS, rows, rows), F32), ((width, side), BF), ((rows, half + 3 * side), BF),
-            ((rows, half), BF),
-        ],
-        6 + HEADS,
-        1000,
-    )
-    got_s2 = lax.ppermute(send_s2, "c", swap)
+            ((HEADS, rows, rows), F32), ((width, side), BF), ((rows, half), BF),
+            ((rows, half), BF), ((rows, 3 * side), BF),
+        ],
+        7 + HEADS,
+        1000,
+    )
+    got_sc = lax.ppermute(send_sc, "c", swap)
+    got_sm = lax.ppermute(d_mix_s, "c", swap)
     parts_s = weight_gradient(
         rows,
         (
-            ((3, 0), (5, 0)), ((1, half), (2, half)),
-            ((0, 0), (2, 0)), ((4, half), (5, half)),
+            ((3, 0), (4, 0)), ((1, half), (2, half)),
+            ((0, 0), (2, 0)), ((5, 0), (6, 0)),
         ),
-        [kept_sn, send_s1, got_s1, kept_sc, send_s2, got_s2],
-    )
-    after, sum_t, stays = lax.optimization_barrier((send_s2, sum_t, parts_s[0]))
-    parts_s = (stays, *parts_s[1:])
+        [kept_sn, send_s1, got_s1, kept_sc, got_sc, d_mix_s, got_sm],
+    )
+    tied = lax.optimization_barrier((d_mix_s, *parts_s, *parts_t))
+    after, parts_s, parts_t = tied[0], tied[1:5], list(tied[5:])
     parts_s = passed_on(parts_s)
-    delta, local = call(
-        functools.partial(spatial_inputs_kernel, frames),
-        [((patches, width), BF), ((bots, width), F32)],
-        [frame, bottle, back, joined, after, spatial_entry],
-        [
-            ((patches, width), BF), ((bots, width), BF), ((rows, width), BF), ((bots, width), BF),
-            ((rows, 3 * side), BF), ((width, 3 * side), BF), ((rows, width), F32),
-            ((patches, width), BF), ((bots, width), F32),
-        ],
-        8,
+    (local,) = call(
+        functools.partial(bottle_inputs_kernel, frames),
+        [((bots, width), F32)],
+        [bottle, joined, after, spatial_entry],
+        [
+            ((bots, width), BF), ((bots, width), BF), ((16, 3 * side), BF),
+            ((width, 3 * side), BF), ((16, width), F32), ((bots, width), F32),
+        ],
+        5,
         1000,
     )
 
@@ -623,41 +618,54 @@
         pairs = [(i, i ^ bit) for i in range(lax.axis_size(axis))]
         return local + lax.ppermute(local, axis, pairs)
 
-    local = with_partner(local, "c", 1)
-    wide = 8 * side + width // 2
+    local = with_partner(local, "zh", 1)
+    local, after, *parts_s = lax.optimization_barrier((local, after, *parts_s))
+    (delta,) = call(
+        patch_inputs_kernel,
+        [((patches, width), BF)],
+        [frame, back, after, spatial_entry],
+        [
+            ((patches, width), BF), ((patches, width), BF), ((patches, 3 * side), BF),
+            ((width, 3 * side), BF), ((patches, width), BF),
+        ],
+        5,
+        1000,
+    )
+    local = with_partner(with_partner(local, "c", 1), "y", 1)
+    local, delta = lax.optimization_barrier((local, delta))
+    local = with_partner(local, "y", 2)
+    (sum_t,) = call(
+        first_sum_kernel, [(share, BF)], parts_t, [((4, *share), BF), (share, BF)], 20, 1000
+    )
+
     (both,) = call(
         join_kernel,
-        [((half // 4, wide), BF)],
-        parts_s + [sum_t, local],
-        [
-            ((4, *share), BF), ((half // 4, wide), BF), ((bots, width), F32),
-            ((16, width // 2), F32),
-        ],
-        24,
+        [((half // 4, 8 * side), BF)],
+        parts_s + [sum_t],
+        [((4, *share), BF), ((half // 4, 8 * side), BF)],
+        22,
         1000,
     )
     groups = second_groups(shape)
     count = len(groups[0])
     last = lax.all_to_all(
-        both.reshape(count, -1, wide), ALL, 0, 0, axis_index_groups=groups, tiled=True
-    )
-    halves = (2 * bots, width // 2)
+        both.reshape(count, -1, 8 * side), ALL, 0, 0, axis_index_groups=groups, tiled=True
+    )
+
     own = last.shape[1]
-    total, s_entry, s_exit, t_entry, t_exit = call(
+    s_entry, s_exit, t_entry, t_exit = call(
         functools.partial(last_sum_kernel, scale),
-        [(halves, BF)] + [((own, 3 * side), BF), ((own, side), BF)] * 2,
-        [place, last],
-        [
-            ((count, own, 8 * side), BF), ((count, *halves), BF), (halves, BF),
+        [((own, 3 * side), BF), ((own, side), BF)] * 2,
+        [last],
+        [
+            (last.shape, BF),
             ((own, 3 * side), BF), ((own, side), BF), ((own, 3 * side), BF), ((own, side), BF),
         ],
-        14,
-        1000,
-    )
-    total = jnp.where(on == 0, total, lax.ppermute(total, "c", [(0, 1)]))
-    local = jnp.concatenate([total[:bots], total[bots:]], axis=1)
+        12,
+        1000,
+    )
     return (
-        delta[None, None], local[None], s_entry, s_exit, t_entry, t_exit
+        delta[None, None], local.astype(BF)[None], s_entry, s_exit, t_entry, t_exit
     )
 
 

time: 112 us -> 106 us (0.946)
  blocking collectives: 20.7 us -> 0 us
  starting transfers between devices: 23.6 us -> 39.3 us
  Pallas kernels: 40.1 us -> 42.9 us
  waiting for transfers between devices: 22.2 us -> 19.7 us
  other arithmetic: 3.29 us -> 1.93 us
    all_to_all x1 -> x0, blocking collectives: 20.7 us -> none  [per_device(): lax.all_to_all(both.reshape(count, -1, wide), ALL, 0, 0, axis_index_group...]
    ppermute x1 -> x4, starting transfers between devices: 0.08 us -> 8.06 us  [with_partner(): return local + lax.ppermute(local, axis, pairs)]
    all_to_all x0 -> x1, starting transfers between devices: none -> 7.3 us  [per_device(): lax.all_to_all(both.reshape(count, -1, 8 * side), ALL, 0, 0, axis_index_g...]
    all_to_all x2, waiting for transfers between devices: 12.8 us -> 8.1 us  [exchange(): return lax.all_to_all(blocks, FRAME, 0, 0, tiled=True).reshape(array.shape)]
    ppermute x1 -> x4, waiting for transfers between devices: 1.38 us -> 5.68 us  [with_partner(): return local + lax.ppermute(local, axis, pairs)]
    ppermute x6, waiting for transfers between devices: 5.4 us -> 2.48 us  [passed_on(): lax.ppermute(parts[k], ALL, first_pairs(shape, k))]
    pallas_call x10 -> x11, Pallas kernels: 40.1 us -> 42.9 us  [call(): pl.pallas_call(kernel, out_shape=tuple((jax.ShapeDtypeStruct(s, d) for s,...]
    ppermute x6, starting transfers between devices: 9.26 us -> 10.6 us  [passed_on(): lax.ppermute(parts[k], ALL, first_pairs(shape, k))]
  transfers between devices with their start and end apart: 13 -> 17, of which waited for: 7 -> 8; matrix products, arithmetic and copies ran while one was open for 2% -> 2% of each run, Pallas kernels for 16% -> 25%
where the time goes in v5:
time: 106 us; the launch traced here: 105 us
  Pallas kernels  42.9 us (40%)
  starting transfers between devices  39.3 us (37%)
  waiting for transfers between devices  19.7 us (19%)
  other arithmetic  1.93 us (2%)
    pallas_call x11, Pallas kernels, call(): pl.pallas_call(kernel, out_shape=tuple((jax.ShapeDtypeStruct(s, d) for s,...  42.9 us
    all_to_all x2, starting transfers between devices, exchange(): return lax.all_to_all(blocks, FRAME, 0, 0, tiled=True).reshape(array.shape)  12.2 us
    ppermute x6, starting transfers between devices, passed_on(): lax.ppermute(parts[k], ALL, first_pairs(shape, k))  10.6 us
    all_to_all x2, waiting for transfers between devices, exchange(): return lax.all_to_all(blocks, FRAME, 0, 0, tiled=True).reshape(array.shape)  8.1 us
    ppermute x4, starting transfers between devices, with_partner(): return local + lax.ppermute(local, axis, pairs)  8.06 us
    all_to_all x1, starting transfers between devices, per_device(): lax.all_to_all(both.reshape(count, -1, 8 * side), ALL, 0, 0, axis_index_g...  7.3 us
    ppermute x4, waiting for transfers between devices, with_partner(): return local + lax.ppermute(local, axis, pairs)  5.68 us
    ppermute x6, waiting for transfers between devices, passed_on(): lax.ppermute(parts[k], ALL, first_pairs(shape, k))  2.48 us
  transfers between devices with their start and end apart: 17, of which 8 were waited for; matrix products, arithmetic and copies ran while one was open for 2% of the time, Pallas kernels for 25%

profile of v5, /device:TPU:0, one launch (start us, length us, event | category | flops | bytes accessed | tf_op | source)
XLA Modules:
  0.0 104.8 jit_solution(2106639074009092530)
XLA Ops:
  0.6 4.6 %shard_map.127 = (bf16[128,2048]{1,0:T(8,128)(2,1)}, bf16[144,1536]{1,0:T(8,128)(2,1)}, f32[8,144,144]{2,1,0:T(8,128)}, bf16[144,512]{1,0:T(8,128)(2,1)}) custom-call(bf16[128,1024]{1,0:T(8,128)(2,1)} %bitcast.15, bf16[4,1024]{1,0:T(4,128)(2,1)} %bitcast.22, bf16[1024,1536]{1,0:T(8,128)(2,1)} %entry_hbm.7, bf16[1024,512]{1,0:T(8,128)(2,1)} %exit_hbm.5, ...), custom_call_target="tpu_custom_call" | custom-call | flops 1000 | bytes 1000 | tf_op jit(solution)/shard_map/pallas_call | solution.py:445
  5.2 8.0 %all-to-all-start = ((bf16[16,8,2048]{2,1,0:T(8,128)(2,1)}), bf16[16,8,2048]{2,1,0:T(8,128)(2,1)}, u32[]{:S(2)}, u32[]{:S(2)}) async-start(bf16[16,8,2048]{2,1,0:T(8,128)(2,1)} %bitcast.18), calls=%async_computation | async-start | bytes 1048576 | tf_op jit(solution)/shard_map/all_to_all | solution.py:498
  13.3 2.3 %shard_map.128 = (bf16[144,1024]{1,0:T(8,128)(2,1)}, bf16[144,512]{1,0:T(8,128)(2,1)}) custom-call(s32[1]{0:T(128)} %bitcast.2.core_ref, bf16[128,1024]{1,0:T(8,128)(2,1)} %bitcast.16, bf16[4,1024]{1,0:T(4,128)(2,1)} %bitcast.23, bf16[144,512]{1,0:T(8,128)(2,1)} %get-tuple-element.52.att_hbm), custom_call_target="tpu_custom_call" | custom-call | flops 1000 | bytes 1000 | tf_op jit(solution)/shard_map/pallas_call | solution.py:445
  15.6 0.4 collective-permute-start
  16.0 1.6 %collective-permute-done.refs_2_ = bf16[144,1024]{1,0:T(8,128)(2,1)} collective-permute-done((bf16[144,1024]{1,0:T(8,128)(2,1)}, bf16[144,1024]{1,0:T(8,128)(2,1)}, u32[]{:S(2)}, u32[]{:S(2)}) %collective-permute-start) | collective-permute-done | bytes 294944 | tf_op jit(solution)/shard_map/ppermute | solution.py:529
  17.6 8.1 %all-to-all-done = bf16[16,8,2048]{2,1,0:T(8,128)(2,1)} async-done(((bf16[16,8,2048]{2,1,0:T(8,128)(2,1)}), bf16[16,8,2048]{2,1,0:T(8,128)(2,1)}, u32[]{:S(2)}, u32[]{:S(2)}) %all-to-all-start) | async-done | bytes 524320 | tf_op jit(solution)/shard_map/all_to_all | solution.py:498
  25.7 7.0 %shard_map.129 = (bf16[128,1024]{1,0:T(8,128)(2,1)}, bf16[128,3072]{1,0:T(8,128)(2,1)}, bf16[128,1024]{1,0:T(8,128)(2,1)}) custom-call(s32[1]{0:T(128)} %bitcast.2.core_ref, bf16[128,2048]{1,0:T(8,128)(2,1)} %bitcast.6.moved_hbm, bf16[1024,1536]{1,0:T(8,128)(2,1)} %entry_hbm.5, bf16[1024,512]{1,0:T(8,128)(2,1)} %exit_hbm.4), custom_call_target="tpu_custom_call" | custom-call | flops 1000 | bytes 1000 | tf_op jit(solution)/shard_map/pallas_call | solution.py:445
  32.7 0.1 collective-permute-start.1
  32.8 4.2 %all-to-all-start.1 = ((bf16[16,8,1024]{2,1,0:T(8,128)(2,1)}), bf16[16,8,1024]{2,1,0:T(8,128)(2,1)}, u32[]{:S(2)}, u32[]{:S(2)}) async-start(bf16[16,8,1024]{2,1,0:T(8,128)(2,1)} %bitcast.21), calls=%async_computation.1 | async-start | bytes 524288 | tf_op jit(solution)/shard_map/all_to_all | solution.py:498
  37.0 0.6 pad_add_fusion.place_ref
  37.6 0.0 collective-permute-done.1.refs_2_
  37.6 3.8 %shard_map.130 = (bf16[128,2048]{1,0:T(8,128)(2,1)}, bf16[128,2048]{1,0:T(8,128)(2,1)}, bf16[128,2048]{1,0:T(8,128)(2,1)}, bf16[128,2048]{1,0:T(8,128)(2,1)}) custom-call(s32[2]{0:T(128)} %pad_add_fusion.place_ref, bf16[128,1024]{1,0:T(8,128)(2,1)} %get-tuple-element.56.refs_0_, bf16[128,3072]{1,0:T(8,128)(2,1)} %get-tuple-element.57.refs_1_, ...), custom_call_target="tpu_custom_call" | custom-call | flops 1000 | bytes 1000 | tf_op jit(solution)/shard_map/pallas_call | solution.py:445
  41.4 1.5 %collective-permute-start.4 = (bf16[128,2048]{1,0:T(8,128)(2,1)}, bf16[128,2048]{1,0:T(8,128)(2,1)}, u32[]{:S(2)}, u32[]{:S(2)}) collective-permute-start(bf16[128,2048]{1,0:T(8,128)(2,1)} %get-tuple-element.72), channel_id=1, source_target_pairs={{0,16},{1,5},{2,18},{3,7},{4,20},{5,9},{6,22},{7,11},{8,24},{9,13}... | collective-permute-start | bytes 1572872 | tf_op jit(solution)/shard_map/ppermute | solution.py:565
  43.0 2.7 %collective-permute-start.5 = (bf16[128,2048]{1,0:T(8,128)(2,1)}, bf16[128,2048]{1,0:T(8,128)(2,1)}, u32[]{:S(2)}, u32[]{:S(2)}) collective-permute-start(bf16[128,2048]{1,0:T(8,128)(2,1)} %get-tuple-element.73), channel_id=1, source_target_pairs={{0,32},{1,9},{2,34},{3,11},{4,36},{5,13},{6,38},{7,15},{8,40},{9,1... | collective-permute-start | bytes 1572872 | tf_op jit(solution)/shard_map/ppermute | solution.py:565
  45.7 1.4 %collective-permute-start.6 = (bf16[128,2048]{1,0:T(8,128)(2,1)}, bf16[128,2048]{1,0:T(8,128)(2,1)}, u32[]{:S(2)}, u32[]{:S(2)}) collective-permute-start(bf16[128,2048]{1,0:T(8,128)(2,1)} %get-tuple-element.74), channel_id=1, source_target_pairs={{0,48},{1,13},{2,50},{3,15},{4,52},{5,1},{6,54},{7,3},{8,56},{9,5}... | collective-permute-start | bytes 1572872 | tf_op jit(solution)/shard_map/ppermute | solution.py:565
  47.2 0.0 all-to-all-done.1
  47.2 5.8 %shard_map.131 = (bf16[144,512]{1,0:T(8,128)(2,1)}, bf16[144,512]{1,0:T(8,128)(2,1)}, bf16[144,1536]{1,0:T(8,128)(2,1)}) custom-call(s32[1]{0:T(128)} %bitcast.2.core_ref, bf16[128,1024]{1,0:T(8,128)(2,1)} %bitcast.8.back_hbm, bf16[4,1024]{1,0:T(4,128)(2,1)} %bitcast.25, bf16[144,1536]{1,0:T(8,128)(2,1)} %get-tuple-element.60.mix_hbm, ...), custom_call_target="tpu_custom_call" | custom-call | flops 1000 | bytes 1000 | tf_op jit(solution)/shard_map/pallas_call | solution.py:445
  53.0 0.1 collective-permute-start.3
  53.1 0.5 collective-permute-start.2
  53.6 1.8 %collective-permute-done.2.refs_4_ = bf16[144,512]{1,0:T(8,128)(2,1)} collective-permute-done((bf16[144,512]{1,0:T(8,128)(2,1)}, bf16[144,512]{1,0:T(8,128)(2,1)}, u32[]{:S(2)}, u32[]{:S(2)}) %collective-permute-start.2) | collective-permute-done | bytes 147488 | tf_op jit(solution)/shard_map/ppermute | solution.py:592
  55.4 0.0 collective-permute-done.3.refs_6_
  55.4 4.3 %shard_map.132 = (bf16[128,2048]{1,0:T(8,128)(2,1)}, bf16[128,2048]{1,0:T(8,128)(2,1)}, bf16[128,2048]{1,0:T(8,128)(2,1)}, bf16[128,2048]{1,0:T(8,128)(2,1)}) custom-call(s32[2]{0:T(128)} %pad_add_fusion.place_ref, bf16[144,512]{1,0:T(8,128)(2,1)} %get-tuple-element.63.refs_0_, bf16[144,1024]{1,0:T(8,128)(2,1)} %get-tuple-element.53.refs_1_, ...), custom_call_target="tpu_custom_call" | custom-call | flops 1000 | bytes 1000 | tf_op jit(solution)/shard_map/pallas_call | solution.py:445
  59.8 0.0 collective-permute-done.4.a_hbm
  59.8 0.0 collective-permute-done.5.b_hbm
  59.8 0.0 collective-permute-done.6.c_hbm
  59.8 0.9 collective-permute-start.8
  60.7 2.5 %collective-permute-start.9 = (bf16[128,2048]{1,0:T(8,128)(2,1)}, bf16[128,2048]{1,0:T(8,128)(2,1)}, u32[]{:S(2)}, u32[]{:S(2)}) collective-permute-start(bf16[128,2048]{1,0:T(8,128)(2,1)} %get-tuple-element.78), channel_id=1, source_target_pairs={{0,32},{1,9},{2,34},{3,11},{4,36},{5,13},{6,38},{7,15},{8,40},{9,1... | collective-permute-start | bytes 1572872 | tf_op jit(solution)/shard_map/ppermute | solution.py:565
  63.3 1.4 %collective-permute-start.10 = (bf16[128,2048]{1,0:T(8,128)(2,1)}, bf16[128,2048]{1,0:T(8,128)(2,1)}, u32[]{:S(2)}, u32[]{:S(2)}) collective-permute-start(bf16[128,2048]{1,0:T(8,128)(2,1)} %get-tuple-element.79), channel_id=1, source_target_pairs={{0,48},{1,13},{2,50},{3,15},{4,52},{5,1},{6,54},{7,3},{8,56},{9,5}... | collective-permute-start | bytes 1572872 | tf_op jit(solution)/shard_map/ppermute | solution.py:565
  64.7 3.5 %shard_map.133 = f32[4,1024]{1,0:T(4,128)} custom-call(bf16[4,1024]{1,0:T(4,128)(2,1)} %bitcast.24, bf16[4,1024]{1,0:T(4,128)(2,1)} %bitcast.26, bf16[144,1536]{1,0:T(8,128)(2,1)} %get-tuple-element.81.refs_5_.d_mix_hbm, bf16[1024,1536]{1,0:T(8,128)(2,1)} %entry_hbm.7), custom_call_target="tpu_custom_call" | custom-call | flops 1000 | bytes 1000 | tf_op jit(solution)/shard_map/pallas_call | solution.py:445
  68.3 3.1 %collective-permute-start.7 = (f32[4,1024]{1,0:T(4,128)}, f32[4,1024]{1,0:T(4,128)S(1)}, u32[]{:S(2)}, u32[]{:S(2)}) collective-permute-start(f32[4,1024]{1,0:T(4,128)} %shard_map.133), channel_id=1, source_target_pairs={{0,2},{2,0},{1,3},{3,1},{4,6},{6,4},{5,7},{7,5},{8,10},{10,8},{9,1... | collective-permute-start | bytes 49160 | tf_op jit(solution)/shard_map/ppermute | solution.py:619
  71.3 2.5 %shard_map.135.other_hbm = bf16[128,2048]{1,0:T(8,128)(2,1)} custom-call(bf16[128,2048]{1,0:T(8,128)(2,1)} %get-tuple-element.88.own_hbm, bf16[128,2048]{1,0:T(8,128)(2,1)} %collective-permute-done.4.a_hbm, bf16[128,2048]{1,0:T(8,128)(2,1)} %collective-permute-done.5.b_hbm, bf16[128,2048]{1,0:T(8,128)(2,1)} %collective-permute-done.6.c_hbm), custom_call_target="tpu_custom_call" | custom-call | flops 1000 | bytes 1000 | tf_op jit(solution)/shard_map/pallas_call | solution.py:445
  73.9 0.0 collective-permute-done.7
  73.9 0.7 add.12
  74.6 0.0 collective-permute-done.8.a_hbm
  74.6 1.7 %collective-permute-done.9.b_hbm = bf16[128,2048]{1,0:T(8,128)(2,1)} collective-permute-done((bf16[128,2048]{1,0:T(8,128)(2,1)}, bf16[128,2048]{1,0:T(8,128)(2,1)}, u32[]{:S(2)}, u32[]{:S(2)}) %collective-permute-start.9) | collective-permute-done | bytes 524320 | tf_op jit(solution)/shard_map/ppermute | solution.py:565
  76.4 0.7 collective-permute-done.10.c_hbm
  77.1 2.8 %shard_map.136 = bf16[128,4096]{1,0:T(8,128)(2,1)} custom-call(bf16[128,2048]{1,0:T(8,128)(2,1)} %get-tuple-element.84.own_hbm, bf16[128,2048]{1,0:T(8,128)(2,1)} %collective-permute-done.8.a_hbm, bf16[128,2048]{1,0:T(8,128)(2,1)} %collective-permute-done.9.b_hbm, bf16[128,2048]{1,0:T(8,128)(2,1)} %collective-permute-done.10.c_hbm, ...), custom_call_target="tpu_custom_call" | custom-call | flops 1000 | bytes 1000 | tf_op jit(solution)/shard_map/pallas_call | solution.py:445
  79.9 7.3 %all-to-all-start.2 = ((bf16[16,8,4096]{2,1,0:T(8,128)(2,1)}), bf16[16,8,4096]{2,1,0:T(8,128)(2,1)}, u32[]{:S(2)}, u32[]{:S(2)}) async-start(bf16[16,8,4096]{2,1,0:T(8,128)(2,1)} %bitcast.14), calls=%async_computation.2 | async-start | bytes 2097152 | tf_op jit(solution)/shard_map/all_to_all | solution.py:651
  87.2 0.1 collective-permute-start.11
  87.3 1.2 %collective-permute-done.11 = f32[4,1024]{1,0:T(4,128)S(1)} collective-permute-done((f32[4,1024]{1,0:T(4,128)S(1)}, f32[4,1024]{1,0:T(4,128)S(1)}, u32[]{:S(2)}, u32[]{:S(2)}) %collective-permute-start.11) | collective-permute-done | bytes 16416 | tf_op jit(solution)/shard_map/ppermute | solution.py:619
  88.5 1.8 %collective-permute-start.12 = (f32[4,1024]{1,0:T(4,128)S(1)}, f32[4,1024]{1,0:T(4,128)S(1)}, u32[]{:S(2)}, u32[]{:S(2)}) collective-permute-start(f32[4,1024]{1,0:T(4,128)S(1)} %add.13), channel_id=1, source_target_pairs={{0,4},{4,0},{8,12},{12,8},{1,5},{5,1},{9,13},{13,9},{2,6},{6,2},{1... | collective-permute-start | bytes 49160 | tf_op jit(solution)/shard_map/ppermute | solution.py:619
  90.3 4.1 %shard_map.134 = bf16[128,1024]{1,0:T(8,128)(2,1)} custom-call(bf16[128,1024]{1,0:T(8,128)(2,1)} %bitcast.17, bf16[128,1024]{1,0:T(8,128)(2,1)} %bitcast.8.back_hbm, bf16[144,1536]{1,0:T(8,128)(2,1)} %get-tuple-element.81.refs_5_.d_mix_hbm, bf16[1024,1536]{1,0:T(8,128)(2,1)} %entry_hbm.7), custom_call_target="tpu_custom_call" | custom-call | flops 1000 | bytes 1000 | tf_op jit(solution)/shard_map/pallas_call | solution.py:445
  94.4 2.4 %collective-permute-done.12 = f32[4,1024]{1,0:T(4,128)S(1)} collective-permute-done((f32[4,1024]{1,0:T(4,128)S(1)}, f32[4,1024]{1,0:T(4,128)S(1)}, u32[]{:S(2)}, u32[]{:S(2)}) %collective-permute-start.12) | collective-permute-done | bytes 16416 | tf_op jit(solution)/shard_map/ppermute | solution.py:619
  96.8 3.1 %collective-permute-start.13 = (f32[4,1024]{1,0:T(4,128)S(1)}, f32[4,1024]{1,0:T(4,128)S(1)}, u32[]{:S(2)}, u32[]{:S(2)}) collective-permute-start(f32[4,1024]{1,0:T(4,128)S(1)} %add.14), channel_id=1, source_target_pairs={{0,8},{4,12},{8,0},{12,4},{1,9},{5,13},{9,1},{13,5},{2,10},{6,14},... | collective-permute-start | bytes 49160 | tf_op jit(solution)/shard_map/ppermute | solution.py:619
  99.9 2.1 %collective-permute-done.13 = f32[4,1024]{1,0:T(4,128)S(1)} collective-permute-done((f32[4,1024]{1,0:T(4,128)S(1)}, f32[4,1024]{1,0:T(4,128)S(1)}, u32[]{:S(2)}, u32[]{:S(2)}) %collective-permute-start.13) | collective-permute-done | bytes 16416 | tf_op jit(solution)/shard_map/ppermute | solution.py:619
  102.0 0.6 fusion
  102.6 0.0 all-to-all-done.2.parts_hbm
  102.6 2.0 %shard_map.137 = (bf16[8,1536]{1,0:T(8,128)(2,1)}, bf16[8,512]{1,0:T(8,128)(2,1)}, bf16[8,1536]{1,0:T(8,128)(2,1)}, bf16[8,512]{1,0:T(8,128)(2,1)}) custom-call(bf16[16,8,4096]{2,1,0:T(8,128)(2,1)} %all-to-all-done.2.parts_hbm), custom_call_target="tpu_custom_call" | custom-call | flops 1000 | bytes 1000 | tf_op jit(solution)/shard_map/pallas_call | solution.py:445
  (2 shorter events, 0.0 us)
Async XLA Ops:
  5.2 20.5 %all-to-all-start = ((bf16[16,8,2048]{2,1,0:T(8,128)(2,1)}), bf16[16,8,2048]{2,1,0:T(8,128)(2,1)}, u32[]{:S(2)}, u32[]{:S(2)}) async-start(bf16[16,8,2048]{2,1,0:T(8,128)(2,1)} %bitcast.18), calls=%async_computation | async-start | bytes 1048576 | tf_op jit(solution)/shard_map/all_to_all | solution.py:498
  15.6 2.0 %collective-permute-start = (bf16[144,1024]{1,0:T(8,128)(2,1)}, bf16[144,1024]{1,0:T(8,128)(2,1)}, u32[]{:S(2)}, u32[]{:S(2)}) collective-permute-start(bf16[144,1024]{1,0:T(8,128)(2,1)} %get-tuple-element.53.refs_1_), channel_id=1, source_target_pairs={{0,1},{1,0},{2,3},{3,2},{4,5},{5,4},{6,7},{7,6},{8,9},{9,8},{10,11... | collective-permute-start | bytes 884744 | tf_op jit(solution)/shard_map/ppermute | solution.py:529
  32.7 4.9 %collective-permute-start.1 = (bf16[128,3072]{1,0:T(8,128)(2,1)}, bf16[128,3072]{1,0:T(8,128)(2,1)}, u32[]{:S(2)}, u32[]{:S(2)}) collective-permute-start(bf16[128,3072]{1,0:T(8,128)(2,1)} %get-tuple-element.57.refs_1_), channel_id=1, source_target_pairs={{0,1},{1,0},{2,3},{3,2},{4,5},{5,4},{6,7},{7,6},{8,9},{9,8},{10,11... | collective-permute-start | bytes 2359304 | tf_op jit(solution)/shard_map/ppermute | solution.py:547
  32.8 14.4 %all-to-all-start.1 = ((bf16[16,8,1024]{2,1,0:T(8,128)(2,1)}), bf16[16,8,1024]{2,1,0:T(8,128)(2,1)}, u32[]{:S(2)}, u32[]{:S(2)}) async-start(bf16[16,8,1024]{2,1,0:T(8,128)(2,1)} %bitcast.21), calls=%async_computation.1 | async-start | bytes 524288 | tf_op jit(solution)/shard_map/all_to_all | solution.py:498
  41.4 18.3 %collective-permute-start.4 = (bf16[128,2048]{1,0:T(8,128)(2,1)}, bf16[128,2048]{1,0:T(8,128)(2,1)}, u32[]{:S(2)}, u32[]{:S(2)}) collective-permute-start(bf16[128,2048]{1,0:T(8,128)(2,1)} %get-tuple-element.72), channel_id=1, source_target_pairs={{0,16},{1,5},{2,18},{3,7},{4,20},{5,9},{6,22},{7,11},{8,24},{9,13}... | collective-permute-start | bytes 1572872 | tf_op jit(solution)/shard_map/ppermute | solution.py:565
  43.0 16.8 %collective-permute-start.5 = (bf16[128,2048]{1,0:T(8,128)(2,1)}, bf16[128,2048]{1,0:T(8,128)(2,1)}, u32[]{:S(2)}, u32[]{:S(2)}) collective-permute-start(bf16[128,2048]{1,0:T(8,128)(2,1)} %get-tuple-element.73), channel_id=1, source_target_pairs={{0,32},{1,9},{2,34},{3,11},{4,36},{5,13},{6,38},{7,15},{8,40},{9,1... | collective-permute-start | bytes 1572872 | tf_op jit(solution)/shard_map/ppermute | solution.py:565
  45.7 14.0 %collective-permute-start.6 = (bf16[128,2048]{1,0:T(8,128)(2,1)}, bf16[128,2048]{1,0:T(8,128)(2,1)}, u32[]{:S(2)}, u32[]{:S(2)}) collective-permute-start(bf16[128,2048]{1,0:T(8,128)(2,1)} %get-tuple-element.74), channel_id=1, source_target_pairs={{0,48},{1,13},{2,50},{3,15},{4,52},{5,1},{6,54},{7,3},{8,56},{9,5}... | collective-permute-start | bytes 1572872 | tf_op jit(solution)/shard_map/ppermute | solution.py:565
  53.0 2.4 %collective-permute-start.3 = (bf16[144,1536]{1,0:T(8,128)(2,1)}, bf16[144,1536]{1,0:T(8,128)(2,1)}, u32[]{:S(2)}, u32[]{:S(2)}) collective-permute-start(bf16[144,1536]{1,0:T(8,128)(2,1)} %get-tuple-element.81.refs_5_.d_mix_hbm), channel_id=1, source_target_pairs={{0,1},{1,0},{2,3},{3,2},{4,5},{5,4},{6,7},{7,6},{8,9},{9,8},{10,11... | collective-permute-start | bytes 1327112 | tf_op jit(solution)/shard_map/ppermute | solution.py:593
  53.1 2.3 %collective-permute-start.2 = (bf16[144,512]{1,0:T(8,128)(2,1)}, bf16[144,512]{1,0:T(8,128)(2,1)}, u32[]{:S(2)}, u32[]{:S(2)}) collective-permute-start(bf16[144,512]{1,0:T(8,128)(2,1)} %get-tuple-element.66), channel_id=1, source_target_pairs={{0,1},{1,0},{2,3},{3,2},{4,5},{5,4},{6,7},{7,6},{8,9},{9,8},{10,11... | collective-permute-start | bytes 442376 | tf_op jit(solution)/shard_map/ppermute | solution.py:592
  59.8 14.8 %collective-permute-start.8 = (bf16[128,2048]{1,0:T(8,128)(2,1)}, bf16[128,2048]{1,0:T(8,128)(2,1)}, u32[]{:S(2)}, u32[]{:S(2)}) collective-permute-start(bf16[128,2048]{1,0:T(8,128)(2,1)} %get-tuple-element.77), channel_id=1, source_target_pairs={{0,16},{1,5},{2,18},{3,7},{4,20},{5,9},{6,22},{7,11},{8,24},{9,13}... | collective-permute-start | bytes 1572872 | tf_op jit(solution)/shard_map/ppermute | solution.py:565
  60.7 15.6 %collective-permute-start.9 = (bf16[128,2048]{1,0:T(8,128)(2,1)}, bf16[128,2048]{1,0:T(8,128)(2,1)}, u32[]{:S(2)}, u32[]{:S(2)}) collective-permute-start(bf16[128,2048]{1,0:T(8,128)(2,1)} %get-tuple-element.78), channel_id=1, source_target_pairs={{0,32},{1,9},{2,34},{3,11},{4,36},{5,13},{6,38},{7,15},{8,40},{9,1... | collective-permute-start | bytes 1572872 | tf_op jit(solution)/shard_map/ppermute | solution.py:565
  63.3 13.8 %collective-permute-start.10 = (bf16[128,2048]{1,0:T(8,128)(2,1)}, bf16[128,2048]{1,0:T(8,128)(2,1)}, u32[]{:S(2)}, u32[]{:S(2)}) collective-permute-start(bf16[128,2048]{1,0:T(8,128)(2,1)} %get-tuple-element.79), channel_id=1, source_target_pairs={{0,48},{1,13},{2,50},{3,15},{4,52},{5,1},{6,54},{7,3},{8,56},{9,5}... | collective-permute-start | bytes 1572872 | tf_op jit(solution)/shard_map/ppermute | solution.py:565
  68.3 5.6 %collective-permute-start.7 = (f32[4,1024]{1,0:T(4,128)}, f32[4,1024]{1,0:T(4,128)S(1)}, u32[]{:S(2)}, u32[]{:S(2)}) collective-permute-start(f32[4,1024]{1,0:T(4,128)} %shard_map.133), channel_id=1, source_target_pairs={{0,2},{2,0},{1,3},{3,1},{4,6},{6,4},{5,7},{7,5},{8,10},{10,8},{9,1... | collective-permute-start | bytes 49160 | tf_op jit(solution)/shard_map/ppermute | solution.py:619
  79.9 22.8 %all-to-all-start.2 = ((bf16[16,8,4096]{2,1,0:T(8,128)(2,1)}), bf16[16,8,4096]{2,1,0:T(8,128)(2,1)}, u32[]{:S(2)}, u32[]{:S(2)}) async-start(bf16[16,8,4096]{2,1,0:T(8,128)(2,1)} %bitcast.14), calls=%async_computation.2 | async-start | bytes 2097152 | tf_op jit(solution)/shard_map/all_to_all | solution.py:651
  87.2 1.3 %collective-permute-start.11 = (f32[4,1024]{1,0:T(4,128)S(1)}, f32[4,1024]{1,0:T(4,128)S(1)}, u32[]{:S(2)}, u32[]{:S(2)}) collective-permute-start(f32[4,1024]{1,0:T(4,128)S(1)} %add.12), channel_id=1, source_target_pairs={{0,1},{1,0},{2,3},{3,2},{4,5},{5,4},{6,7},{7,6},{8,9},{9,8},{10,11... | collective-permute-start | bytes 49160 | tf_op jit(solution)/shard_map/ppermute | solution.py:619
  88.5 8.3 %collective-permute-start.12 = (f32[4,1024]{1,0:T(4,128)S(1)}, f32[4,1024]{1,0:T(4,128)S(1)}, u32[]{:S(2)}, u32[]{:S(2)}) collective-permute-start(f32[4,1024]{1,0:T(4,128)S(1)} %add.13), channel_id=1, source_target_pairs={{0,4},{4,0},{8,12},{12,8},{1,5},{5,1},{9,13},{13,9},{2,6},{6,2},{1... | collective-permute-start | bytes 49160 | tf_op jit(solution)/shard_map/ppermute | solution.py:619
  96.8 5.2 %collective-permute-start.13 = (f32[4,1024]{1,0:T(4,128)S(1)}, f32[4,1024]{1,0:T(4,128)S(1)}, u32[]{:S(2)}, u32[]{:S(2)}) collective-permute-start(f32[4,1024]{1,0:T(4,128)S(1)} %add.14), channel_id=1, source_target_pairs={{0,8},{4,12},{8,0},{12,4},{1,9},{5,13},{9,1},{13,5},{2,10},{6,14},... | collective-permute-start | bytes 49160 | tf_op jit(solution)/shard_map/ppermute | solution.py:619

commit v6 on v5

--- a/solution.py
+++ b/solution.py
@@ -117,6 +117,11 @@
         copy.start()
         return copy
 
+    def spread(self, source, target, count=2):
+        step = source.shape[0] // count
+        rows = [slice(k * step, (k + 1) * step) for k in range(count)]
+        return [self.start(source.at[r, :], target.at[r, :]) for r in rows]
+
 
 def finish(copies):
     for copy in copies:
@@ -142,15 +147,15 @@
     side = exit_.shape[1]
     first = [move.start(frames_hbm, frames), move.start(bottle_hbm, bottle)]
     columns = [slice(j * side, (j + 1) * side) for j in range(3)]
-    entries = [move.start(entry_hbm.at[:, c], entry.at[:, c]) for c in columns]
-    later = move.start(exit_hbm, exit_)
+    entries = [move.spread(entry_hbm.at[:, c], entry.at[:, c]) for c in columns]
+    later = move.spread(exit_hbm, exit_)
     grads = move.start(grad_hbm, packed.at[:, width : 2 * width])
     outs = []
     finish(first)
     fill_tokens(tokens, frames, bottle)
     low = normalize(tokens[...])[0].astype(BF)
     for c, copy in zip(columns, entries):
-        copy.wait()
+        finish(copy)
         mix[:, c] = mm(low, entry[:, c], NN).astype(BF)
     outs.append(move.start(mix, mix_hbm))
     masks = half_masks(side // HEADS)
@@ -165,7 +170,7 @@
 
     attention_forward(mix, keep, masks, save, put)
     outs.append(move.start(att, att_hbm))
-    later.wait()
+    finish(later)
     out = tokens[0:patches, :] + mm(att[0:patches, :], exit_[...], NT)
     packed[:, 0:width] = out.astype(BF)
     grads.wait()
@@ -203,8 +208,8 @@
     seqs = rows // frames
     first = move.start(moved_hbm, moved)
     columns = [slice(j * side, (j + 1) * side) for j in range(3)]
-    entries = [move.start(entry_hbm.at[:, c], entry.at[:, c]) for c in columns]
-    later = move.start(exit_hbm, exit_)
+    entries = [move.spread(entry_hbm.at[:, c], entry.at[:, c]) for c in columns]
+    later = move.spread(exit_hbm, exit_)
     core = core_ref[0]
     other, own = picker(1 - core), picker(core)
     first.wait()
@@ -214,7 +219,7 @@
     pick(cot, other, send, half + side)
     pick(cot, own, kept, half)
     for c, copy in zip(columns, entries):
-        copy.wait()
+        finish(copy)
         mix[:, c] = mm(low, entry[:, c], NN).astype(BF)
     pick(low, other, send, 0)
     pick(low, own, kept, 0)
@@ -232,7 +237,7 @@
         send[:, half + p * w : half + (p + 1) * w] = value
 
     attention_forward(mix, keep, masks, save, put)
-    later.wait()
+    finish(later)
     d_att = mm(cot, exit_[...], NN).astype(BF)
     at_mix = width + side
 
@@ -263,7 +268,7 @@
     side = exit_.shape[1]
     patches = back_hbm.shape[0]
     first = [move.start(joined_hbm, joined), move.start(back_hbm, cot.at[0:patches, :])]
-    first.append(move.start(exit_hbm, exit_))
+    first += move.spread(exit_hbm, exit_)
     second = move.start(mix_hbm, mix)
     heads = [move.start(weights_hbm.at[h], weights_buf.at[h]) for h in range(HEADS)]
     finish(first)
@@ -296,10 +301,8 @@
 ):
     move = Mover(sems)
     bots = bottle.shape[0]
-    second = [
-        move.start(entry_hbm, entry),
-        move.start(d_mix_hbm.at[d_mix_hbm.shape[0] - 16 :, :], d_mix),
-    ]
+    second = move.spread(entry_hbm, entry, 4)
+    second.append(move.start(d_mix_hbm.at[d_mix_hbm.shape[0] - 16 :, :], d_mix))
     first = [move.start(bottle_hbm, bottle), move.start(joined_hbm, joined)]
     finish(first)
     tokens[...] = jnp.zeros(tokens.shape, F32)
@@ -321,8 +324,8 @@
     first = move.start(frames_hbm, frames)
     second = [
         move.start(d_mix_hbm.at[0 : d_mix.shape[0], :], d_mix),
-        move.start(entry_hbm, entry),
         move.start(back_hbm, cot),
+        *move.spread(entry_hbm, entry, 4),
     ]
     first.wait()
     normed, inverse = normalize(frames[...].astype(F32))
@@ -381,35 +384,20 @@
     return total.astype(BF)
 
 
-def first_sum_kernel(own_hbm, a_hbm, b_hbm, c_hbm, out_hbm, parts, out, sems):
+def four_sum_kernel(right, own_hbm, a_hbm, b_hbm, c_hbm, *refs):
+    out_hbm, parts, out, sems = refs[-4:]
     move = Mover(sems)
     sources = (own_hbm, a_hbm, b_hbm, c_hbm)
-    step = out.shape[1] // 4
+    width = out.shape[1]
+    step = width // 4
     columns = [slice(j * step, (j + 1) * step) for j in range(4)]
     copies = [[move.start(r.at[:, c], parts.at[k, :, c]) for k, r in enumerate(sources)] for c in columns]
     outs = []
     for c, ready in zip(columns, copies):
         finish(ready)
         out[:, c] = add_four(parts, c)
-        outs.append(move.start(out.at[:, c], out_hbm.at[:, c]))
-    finish(outs)
-
-
-def join_kernel(own_hbm, a_hbm, b_hbm, c_hbm, other_hbm, out_hbm, parts, out, sems):
-    move = Mover(sems)
-    sources = (own_hbm, a_hbm, b_hbm, c_hbm)
-    width = parts.shape[2]
-    step = width // 4
-    columns = [slice(j * step, (j + 1) * step) for j in range(4)]
-    copies = [[move.start(r.at[:, c], parts.at[k, :, c]) for k, r in enumerate(sources)] for c in columns]
-    other = move.start(other_hbm, out.at[:, width:])
-    outs = []
-    for c, ready in zip(columns, copies):
-        finish(ready)
-        out[:, c] = add_four(parts, c)
-        outs.append(move.start(out.at[:, c], out_hbm.at[:, c]))
-    other.wait()
-    outs.append(move.start(out.at[:, width:], out_hbm.at[:, width:]))
+        at = c.start + (width if right else 0)
+        outs.append(move.start(out.at[:, c], out_hbm.at[:, at : at + step]))
     finish(outs)
 
 
@@ -441,14 +429,15 @@
 SMEM = pl.BlockSpec(memory_space=pltpu.SMEM)
 
 
-def call(kernel, outs, ins, scratch, copies, flops):
+def call(kernel, outs, ins, scratch, copies, flops, aliases=None):
     return pl.pallas_call(
         kernel,
         out_shape=tuple(jax.ShapeDtypeStruct(s, d) for s, d in outs),
         in_specs=[SMEM if a.ndim == 1 else HBM for a in ins],
         out_specs=tuple(HBM for _ in outs),
+        input_output_aliases=aliases or {},
         scratch_shapes=[pltpu.VMEM(s, d) for s, d in scratch]
-        + [pltpu.SemaphoreType.DMA((copies,))],
+        + [pltpu.SemaphoreType.DMA((copies + 4,))],
         compiler_params=pltpu.CompilerParams(vmem_limit_bytes=(64 * 1024 - 128) * 1024),
         cost_estimate=pl.CostEstimate(flops=flops, bytes_accessed=1000, transcendentals=0),
     )(*ins)
@@ -562,7 +551,7 @@
 
     def passed_on(parts):
         return [parts[0]] + [
-            lax.ppermute(parts[k], ALL, first_pairs(shape, k)) for k in range(1, 4)
+            lax.ppermute(parts[k], ALL, first_pairs(shape, k)) for k in (1, 3, 2)
         ]
 
     cot_at, mix_at = half + side, half + side + half
@@ -631,20 +620,27 @@
         5,
         1000,
     )
-    local = with_partner(with_partner(local, "c", 1), "y", 1)
-    local, delta = lax.optimization_barrier((local, delta))
-    local = with_partner(local, "y", 2)
-    (sum_t,) = call(
-        first_sum_kernel, [(share, BF)], parts_t, [((4, *share), BF), (share, BF)], 20, 1000
-    )
-
+    local = with_partner(local, "c", 1)
+    ys = shape[2]
+    sent = [local] + [
+        lax.ppermute(local, "y", [(i, (i + k) % ys) for i in range(ys)]) for k in range(1, ys)
+    ]
+    total = None
+    for j in range(ys):
+        back_by = (lax.axis_index("y") - j) % ys
+        part = sent[0]
+        for k in range(1, ys):
+            part = jnp.where(back_by == k, sent[k], part)
+        total = part if total is None else total + part
+    local = total
+    wide = (half // 4, 8 * side)
+    scratch = [((4, *share), BF), (share, BF)]
+    (half_done,) = call(
+        functools.partial(four_sum_kernel, True), [(wide, BF)], parts_t, scratch, 20, 1000
+    )
     (both,) = call(
-        join_kernel,
-        [((half // 4, 8 * side), BF)],
-        parts_s + [sum_t],
-        [((4, *share), BF), ((half // 4, 8 * side), BF)],
-        22,
-        1000,
+        functools.partial(four_sum_kernel, False), [(wide, BF)], [*parts_s, half_done], scratch,
+        20, 1000, {4: 0},
     )
     groups = second_groups(shape)
     count = len(groups[0])

time: 106 us -> 104 us (0.981)
  starting transfers between devices: 39.3 us -> 37.4 us
    ppermute x4 -> x2, starting transfers between devices: 8.06 us -> 2.77 us  [with_partner(): return local + lax.ppermute(local, axis, pairs)]
    ppermute x0 -> x3, starting transfers between devices: none -> 4.72 us  [per_device(): lax.ppermute(local, 'y', [(i, (i + k) % ys) for i in range(ys)])]
    ppermute x4 -> x2, waiting for transfers between devices: 5.68 us -> 1.47 us  [with_partner(): return local + lax.ppermute(local, axis, pairs)]
    all_to_all x1, waiting for transfers between devices: 0.01 us -> 2.97 us  [per_device(): lax.all_to_all(both.reshape(count, -1, 8 * side), ALL, 0, 0, axis_index_g...]
    ppermute x0 -> x3, waiting for transfers between devices: none -> 1.46 us  [per_device(): lax.ppermute(local, 'y', [(i, (i + k) % ys) for i in range(ys)])]
  transfers between devices with their start and end apart: 17 -> 18, of which waited for: 8 -> 10; matrix products, arithmetic and copies ran while one was open for 2% -> 1% of each run, Pallas kernels for 25% -> 26%
where the time goes in v6:
time: 104 us; the launch traced here: 103 us
  Pallas kernels  42.9 us (41%)
  starting transfers between devices  37.4 us (36%)
  waiting for transfers between devices  20.5 us (20%)
  other arithmetic  1.22 us (1%)
    pallas_call x11, Pallas kernels, call(): pl.pallas_call(kernel, out_shape=tuple((jax.ShapeDtypeStruct(s, d) for s,...  42.9 us
    all_to_all x2, starting transfers between devices, exchange(): return lax.all_to_all(blocks, FRAME, 0, 0, tiled=True).reshape(array.shape)  12.2 us
    ppermute x6, starting transfers between devices, passed_on(): lax.ppermute(parts[k], ALL, first_pairs(shape, k))  9.81 us
    all_to_all x2, waiting for transfers between devices, exchange(): return lax.all_to_all(blocks, FRAME, 0, 0, tiled=True).reshape(array.shape)  8.07 us
    all_to_all x1, starting transfers between devices, per_device(): lax.all_to_all(both.reshape(count, -1, 8 * side), ALL, 0, 0, axis_index_g...  6.76 us
    ppermute x3, starting transfers between devices, per_device(): lax.ppermute(local, 'y', [(i, (i + k) % ys) for i in range(ys)])  4.72 us
    ppermute x6, waiting for transfers between devices, passed_on(): lax.ppermute(parts[k], ALL, first_pairs(shape, k))  3.13 us
    all_to_all x1, waiting for transfers between devices, per_device(): lax.all_to_all(both.reshape(count, -1, 8 * side), ALL, 0, 0, axis_index_g...  2.97 us
  transfers between devices with their start and end apart: 18, of which 10 were waited for; matrix products, arithmetic and copies ran while one was open for 1% of the time, Pallas kernels for 26%

profile of v6, /device:TPU:0, one launch (start us, length us, event | category | flops | bytes accessed | tf_op | source)
XLA Modules:
  0.0 103.1 jit_solution(14502967965101883099)
XLA Ops:
  0.6 4.6 %shard_map.127 = (bf16[128,2048]{1,0:T(8,128)(2,1)}, bf16[144,1536]{1,0:T(8,128)(2,1)}, f32[8,144,144]{2,1,0:T(8,128)}, bf16[144,512]{1,0:T(8,128)(2,1)}) custom-call(bf16[128,1024]{1,0:T(8,128)(2,1)} %bitcast.15, bf16[4,1024]{1,0:T(4,128)(2,1)} %bitcast.22, bf16[1024,1536]{1,0:T(8,128)(2,1)} %entry_hbm.7, bf16[1024,512]{1,0:T(8,128)(2,1)} %exit_hbm.5, ...), custom_call_target="tpu_custom_call" | custom-call | flops 1000 | bytes 1000 | tf_op jit(solution)/shard_map/pallas_call | solution.py:433
  5.2 8.0 %all-to-all-start = ((bf16[16,8,2048]{2,1,0:T(8,128)(2,1)}), bf16[16,8,2048]{2,1,0:T(8,128)(2,1)}, u32[]{:S(2)}, u32[]{:S(2)}) async-start(bf16[16,8,2048]{2,1,0:T(8,128)(2,1)} %bitcast.18), calls=%async_computation | async-start | bytes 1048576 | tf_op jit(solution)/shard_map/all_to_all | solution.py:487
  13.3 2.3 %shard_map.128 = (bf16[144,1024]{1,0:T(8,128)(2,1)}, bf16[144,512]{1,0:T(8,128)(2,1)}) custom-call(s32[1]{0:T(128)} %bitcast.1.core_ref, bf16[128,1024]{1,0:T(8,128)(2,1)} %bitcast.16, bf16[4,1024]{1,0:T(4,128)(2,1)} %bitcast.23, bf16[144,512]{1,0:T(8,128)(2,1)} %get-tuple-element.50.att_hbm), custom_call_target="tpu_custom_call" | custom-call | flops 1000 | bytes 1000 | tf_op jit(solution)/shard_map/pallas_call | solution.py:433
  15.6 0.4 collective-permute-start
  16.1 1.6 %collective-permute-done.refs_2_ = bf16[144,1024]{1,0:T(8,128)(2,1)} collective-permute-done((bf16[144,1024]{1,0:T(8,128)(2,1)}, bf16[144,1024]{1,0:T(8,128)(2,1)}, u32[]{:S(2)}, u32[]{:S(2)}) %collective-permute-start) | collective-permute-done | bytes 294944 | tf_op jit(solution)/shard_map/ppermute | solution.py:518
  17.6 8.1 %all-to-all-done = bf16[16,8,2048]{2,1,0:T(8,128)(2,1)} async-done(((bf16[16,8,2048]{2,1,0:T(8,128)(2,1)}), bf16[16,8,2048]{2,1,0:T(8,128)(2,1)}, u32[]{:S(2)}, u32[]{:S(2)}) %all-to-all-start) | async-done | bytes 524320 | tf_op jit(solution)/shard_map/all_to_all | solution.py:487
  25.7 7.0 %shard_map.129 = (bf16[128,1024]{1,0:T(8,128)(2,1)}, bf16[128,3072]{1,0:T(8,128)(2,1)}, bf16[128,1024]{1,0:T(8,128)(2,1)}) custom-call(s32[1]{0:T(128)} %bitcast.1.core_ref, bf16[128,2048]{1,0:T(8,128)(2,1)} %bitcast.5.moved_hbm, bf16[1024,1536]{1,0:T(8,128)(2,1)} %entry_hbm.5, bf16[1024,512]{1,0:T(8,128)(2,1)} %exit_hbm.4), custom_call_target="tpu_custom_call" | custom-call | flops 1000 | bytes 1000 | tf_op jit(solution)/shard_map/pallas_call | solution.py:433
  32.7 0.1 collective-permute-start.1
  32.8 4.2 %all-to-all-start.1 = ((bf16[16,8,1024]{2,1,0:T(8,128)(2,1)}), bf16[16,8,1024]{2,1,0:T(8,128)(2,1)}, u32[]{:S(2)}, u32[]{:S(2)}) async-start(bf16[16,8,1024]{2,1,0:T(8,128)(2,1)} %bitcast.21), calls=%async_computation.1 | async-start | bytes 524288 | tf_op jit(solution)/shard_map/all_to_all | solution.py:487
  37.0 0.6 pad_add_fusion.place_ref
  37.6 0.0 collective-permute-done.1.refs_2_
  37.6 3.9 %shard_map.130 = (bf16[128,2048]{1,0:T(8,128)(2,1)}, bf16[128,2048]{1,0:T(8,128)(2,1)}, bf16[128,2048]{1,0:T(8,128)(2,1)}, bf16[128,2048]{1,0:T(8,128)(2,1)}) custom-call(s32[2]{0:T(128)} %pad_add_fusion.place_ref, bf16[128,1024]{1,0:T(8,128)(2,1)} %get-tuple-element.54.refs_0_, bf16[128,3072]{1,0:T(8,128)(2,1)} %get-tuple-element.55.refs_1_, ...), custom_call_target="tpu_custom_call" | custom-call | flops 1000 | bytes 1000 | tf_op jit(solution)/shard_map/pallas_call | solution.py:433
  41.5 1.5 %collective-permute-start.4 = (bf16[128,2048]{1,0:T(8,128)(2,1)}, bf16[128,2048]{1,0:T(8,128)(2,1)}, u32[]{:S(2)}, u32[]{:S(2)}) collective-permute-start(bf16[128,2048]{1,0:T(8,128)(2,1)} %get-tuple-element.70), channel_id=1, source_target_pairs={{0,16},{1,5},{2,18},{3,7},{4,20},{5,9},{6,22},{7,11},{8,24},{9,13}... | collective-permute-start | bytes 1572872 | tf_op jit(solution)/shard_map/ppermute | solution.py:554
  43.1 1.8 %collective-permute-start.5 = (bf16[128,2048]{1,0:T(8,128)(2,1)}, bf16[128,2048]{1,0:T(8,128)(2,1)}, u32[]{:S(2)}, u32[]{:S(2)}) collective-permute-start(bf16[128,2048]{1,0:T(8,128)(2,1)} %get-tuple-element.71), channel_id=1, source_target_pairs={{0,48},{1,13},{2,50},{3,15},{4,52},{5,1},{6,54},{7,3},{8,56},{9,5}... | collective-permute-start | bytes 1572872 | tf_op jit(solution)/shard_map/ppermute | solution.py:554
  44.9 1.8 %collective-permute-start.6 = (bf16[128,2048]{1,0:T(8,128)(2,1)}, bf16[128,2048]{1,0:T(8,128)(2,1)}, u32[]{:S(2)}, u32[]{:S(2)}) collective-permute-start(bf16[128,2048]{1,0:T(8,128)(2,1)} %get-tuple-element.72), channel_id=1, source_target_pairs={{0,32},{1,9},{2,34},{3,11},{4,36},{5,13},{6,38},{7,15},{8,40},{9,1... | collective-permute-start | bytes 1572872 | tf_op jit(solution)/shard_map/ppermute | solution.py:554
  46.7 0.0 all-to-all-done.1
  46.7 5.8 %shard_map.131 = (bf16[144,512]{1,0:T(8,128)(2,1)}, bf16[144,512]{1,0:T(8,128)(2,1)}, bf16[144,1536]{1,0:T(8,128)(2,1)}) custom-call(s32[1]{0:T(128)} %bitcast.1.core_ref, bf16[128,1024]{1,0:T(8,128)(2,1)} %bitcast.7.back_hbm, bf16[4,1024]{1,0:T(4,128)(2,1)} %bitcast.25, bf16[144,1536]{1,0:T(8,128)(2,1)} %get-tuple-element.58.mix_hbm, ...), custom_call_target="tpu_custom_call" | custom-call | flops 1000 | bytes 1000 | tf_op jit(solution)/shard_map/pallas_call | solution.py:433
  52.5 0.1 collective-permute-start.3
  52.6 0.5 collective-permute-start.2
  53.1 1.8 %collective-permute-done.2.refs_4_ = bf16[144,512]{1,0:T(8,128)(2,1)} collective-permute-done((bf16[144,512]{1,0:T(8,128)(2,1)}, bf16[144,512]{1,0:T(8,128)(2,1)}, u32[]{:S(2)}, u32[]{:S(2)}) %collective-permute-start.2) | collective-permute-done | bytes 147488 | tf_op jit(solution)/shard_map/ppermute | solution.py:581
  54.9 0.0 collective-permute-done.3.refs_6_
  54.9 4.4 %shard_map.132 = (bf16[128,2048]{1,0:T(8,128)(2,1)}, bf16[128,2048]{1,0:T(8,128)(2,1)}, bf16[128,2048]{1,0:T(8,128)(2,1)}, bf16[128,2048]{1,0:T(8,128)(2,1)}) custom-call(s32[2]{0:T(128)} %pad_add_fusion.place_ref, bf16[144,512]{1,0:T(8,128)(2,1)} %get-tuple-element.61.refs_0_, bf16[144,1024]{1,0:T(8,128)(2,1)} %get-tuple-element.51.refs_1_, ...), custom_call_target="tpu_custom_call" | custom-call | flops 1000 | bytes 1000 | tf_op jit(solution)/shard_map/pallas_call | solution.py:433
  59.3 0.0 collective-permute-done.4.a_hbm
  59.3 0.0 collective-permute-done.5.b_hbm
  59.3 0.0 collective-permute-done.6.c_hbm
  59.3 1.1 %collective-permute-start.8 = (bf16[128,2048]{1,0:T(8,128)(2,1)}, bf16[128,2048]{1,0:T(8,128)(2,1)}, u32[]{:S(2)}, u32[]{:S(2)}) collective-permute-start(bf16[128,2048]{1,0:T(8,128)(2,1)} %get-tuple-element.75), channel_id=1, source_target_pairs={{0,16},{1,5},{2,18},{3,7},{4,20},{5,9},{6,22},{7,11},{8,24},{9,13}... | collective-permute-start | bytes 1572872 | tf_op jit(solution)/shard_map/ppermute | solution.py:554
  60.5 2.2 %collective-permute-start.9 = (bf16[128,2048]{1,0:T(8,128)(2,1)}, bf16[128,2048]{1,0:T(8,128)(2,1)}, u32[]{:S(2)}, u32[]{:S(2)}) collective-permute-start(bf16[128,2048]{1,0:T(8,128)(2,1)} %get-tuple-element.76), channel_id=1, source_target_pairs={{0,48},{1,13},{2,50},{3,15},{4,52},{5,1},{6,54},{7,3},{8,56},{9,5}... | collective-permute-start | bytes 1572872 | tf_op jit(solution)/shard_map/ppermute | solution.py:554
  62.6 1.4 %collective-permute-start.10 = (bf16[128,2048]{1,0:T(8,128)(2,1)}, bf16[128,2048]{1,0:T(8,128)(2,1)}, u32[]{:S(2)}, u32[]{:S(2)}) collective-permute-start(bf16[128,2048]{1,0:T(8,128)(2,1)} %get-tuple-element.77), channel_id=1, source_target_pairs={{0,32},{1,9},{2,34},{3,11},{4,36},{5,13},{6,38},{7,15},{8,40},{9,1... | collective-permute-start | bytes 1572872 | tf_op jit(solution)/shard_map/ppermute | solution.py:554
  64.0 3.6 %shard_map.133 = f32[4,1024]{1,0:T(4,128)} custom-call(bf16[4,1024]{1,0:T(4,128)(2,1)} %bitcast.24, bf16[4,1024]{1,0:T(4,128)(2,1)} %bitcast.26, bf16[144,1536]{1,0:T(8,128)(2,1)} %get-tuple-element.78.refs_5_.d_mix_hbm, bf16[1024,1536]{1,0:T(8,128)(2,1)} %entry_hbm.7), custom_call_target="tpu_custom_call" | custom-call | flops 1000 | bytes 1000 | tf_op jit(solution)/shard_map/pallas_call | solution.py:433
  67.6 0.0 copy-start
  67.6 2.7 %collective-permute-start.7 = (f32[4,1024]{1,0:T(4,128)}, f32[4,1024]{1,0:T(4,128)S(1)}, u32[]{:S(2)}, u32[]{:S(2)}) collective-permute-start(f32[4,1024]{1,0:T(4,128)} %shard_map.133), channel_id=1, source_target_pairs={{0,2},{2,0},{1,3},{3,1},{4,6},{6,4},{5,7},{7,5},{8,10},{10,8},{9,1... | collective-permute-start | bytes 49160 | tf_op jit(solution)/shard_map/ppermute | solution.py:608
  70.3 2.5 %shard_map.135.refs_0_ = bf16[128,4096]{1,0:T(8,128)(2,1)} custom-call(bf16[128,2048]{1,0:T(8,128)(2,1)} %get-tuple-element.84.own_hbm, bf16[128,2048]{1,0:T(8,128)(2,1)} %collective-permute-done.4.a_hbm, bf16[128,2048]{1,0:T(8,128)(2,1)} %collective-permute-done.5.b_hbm, bf16[128,2048]{1,0:T(8,128)(2,1)} %collective-permute-done.6.c_hbm), custom_call_target="tpu_custom_call" | custom-call | flops 1000 | bytes 1000 | tf_op jit(solution)/shard_map/pallas_call | solution.py:433
  72.8 0.3 collective-permute-done.7
  73.1 0.0 copy-done
  73.1 0.0 collective-permute-done.8.a_hbm
  73.1 2.1 %collective-permute-done.9.b_hbm = bf16[128,2048]{1,0:T(8,128)(2,1)} collective-permute-done((bf16[128,2048]{1,0:T(8,128)(2,1)}, bf16[128,2048]{1,0:T(8,128)(2,1)}, u32[]{:S(2)}, u32[]{:S(2)}) %collective-permute-start.9) | collective-permute-done | bytes 524320 | tf_op jit(solution)/shard_map/ppermute | solution.py:554
  75.3 1.0 collective-permute-done.10.c_hbm
  76.3 2.6 %shard_map.136 = bf16[128,4096]{1,0:T(8,128)(2,1)} custom-call(bf16[128,2048]{1,0:T(8,128)(2,1)} %get-tuple-element.80.own_hbm, bf16[128,2048]{1,0:T(8,128)(2,1)} %collective-permute-done.8.a_hbm, bf16[128,2048]{1,0:T(8,128)(2,1)} %collective-permute-done.9.b_hbm, bf16[128,2048]{1,0:T(8,128)(2,1)} %collective-permute-done.10.c_hbm, ...), custom_call_target="tpu_custom_call", output_to_operand_aliasing={{}: (4, {})} | custom-call | flops 1000 | bytes 1000 | tf_op jit(solution)/shard_map/pallas_call | solution.py:433
  78.9 6.8 %all-to-all-start.2 = ((bf16[16,8,4096]{2,1,0:T(8,128)(2,1)}), bf16[16,8,4096]{2,1,0:T(8,128)(2,1)}, u32[]{:S(2)}, u32[]{:S(2)}) async-start(bf16[16,8,4096]{2,1,0:T(8,128)(2,1)} %bitcast.14), calls=%async_computation.2 | async-start | bytes 2097152 | tf_op jit(solution)/shard_map/all_to_all | solution.py:647
  85.6 0.1 collective-permute-start.11
  85.7 1.2 %collective-permute-done.11 = f32[4,1024]{1,0:T(4,128)S(1)} collective-permute-done((f32[4,1024]{1,0:T(4,128)S(1)}, f32[4,1024]{1,0:T(4,128)S(1)}, u32[]{:S(2)}, u32[]{:S(2)}) %collective-permute-start.11) | collective-permute-done | bytes 16416 | tf_op jit(solution)/shard_map/ppermute | solution.py:608
  86.9 3.0 %collective-permute-start.12 = (f32[4,1024]{1,0:T(4,128)S(1)}, f32[4,1024]{1,0:T(4,128)S(1)}, u32[]{:S(2)}, u32[]{:S(2)}) collective-permute-start(f32[4,1024]{1,0:T(4,128)S(1)} %add.33), channel_id=1, source_target_pairs={{0,12},{4,0},{8,4},{12,8},{1,13},{5,1},{9,5},{13,9},{2,14},{6,2},{... | collective-permute-start | bytes 49160 | tf_op jit(solution)/shard_map/ppermute | solution.py:626
  89.9 0.9 collective-permute-start.13
  90.8 0.9 collective-permute-start.14
  91.6 4.2 %shard_map.134 = bf16[128,1024]{1,0:T(8,128)(2,1)} custom-call(bf16[128,1024]{1,0:T(8,128)(2,1)} %bitcast.17, bf16[128,1024]{1,0:T(8,128)(2,1)} %bitcast.7.back_hbm, bf16[144,1536]{1,0:T(8,128)(2,1)} %get-tuple-element.78.refs_5_.d_mix_hbm, bf16[1024,1536]{1,0:T(8,128)(2,1)} %entry_hbm.7), custom_call_target="tpu_custom_call" | custom-call | flops 1000 | bytes 1000 | tf_op jit(solution)/shard_map/pallas_call | solution.py:433
  95.8 0.0 collective-permute-done.12
  95.8 1.4 %collective-permute-done.13 = f32[4,1024]{1,0:T(4,128)S(1)} collective-permute-done((f32[4,1024]{1,0:T(4,128)S(1)}, f32[4,1024]{1,0:T(4,128)S(1)}, u32[]{:S(2)}, u32[]{:S(2)}) %collective-permute-start.13) | collective-permute-done | bytes 16416 | tf_op jit(solution)/shard_map/ppermute | solution.py:626
  97.2 0.1 collective-permute-done.14
  97.3 0.6 fusion
  97.9 3.0 %all-to-all-done.2.parts_hbm = bf16[16,8,4096]{2,1,0:T(8,128)(2,1)} async-done(((bf16[16,8,4096]{2,1,0:T(8,128)(2,1)}), bf16[16,8,4096]{2,1,0:T(8,128)(2,1)}, u32[]{:S(2)}, u32[]{:S(2)}) %all-to-all-start.2) | async-done | bytes 1048608 | tf_op jit(solution)/shard_map/all_to_all | solution.py:647
  100.9 2.0 %shard_map.137 = (bf16[8,1536]{1,0:T(8,128)(2,1)}, bf16[8,512]{1,0:T(8,128)(2,1)}, bf16[8,1536]{1,0:T(8,128)(2,1)}, bf16[8,512]{1,0:T(8,128)(2,1)}) custom-call(bf16[16,8,4096]{2,1,0:T(8,128)(2,1)} %all-to-all-done.2.parts_hbm), custom_call_target="tpu_custom_call" | custom-call | flops 1000 | bytes 1000 | tf_op jit(solution)/shard_map/pallas_call | solution.py:433
  (2 shorter events, 0.0 us)
Async XLA Ops:
  5.2 20.5 %all-to-all-start = ((bf16[16,8,2048]{2,1,0:T(8,128)(2,1)}), bf16[16,8,2048]{2,1,0:T(8,128)(2,1)}, u32[]{:S(2)}, u32[]{:S(2)}) async-start(bf16[16,8,2048]{2,1,0:T(8,128)(2,1)} %bitcast.18), calls=%async_computation | async-start | bytes 1048576 | tf_op jit(solution)/shard_map/all_to_all | solution.py:487
  15.6 2.0 %collective-permute-start = (bf16[144,1024]{1,0:T(8,128)(2,1)}, bf16[144,1024]{1,0:T(8,128)(2,1)}, u32[]{:S(2)}, u32[]{:S(2)}) collective-permute-start(bf16[144,1024]{1,0:T(8,128)(2,1)} %get-tuple-element.51.refs_1_), channel_id=1, source_target_pairs={{0,1},{1,0},{2,3},{3,2},{4,5},{5,4},{6,7},{7,6},{8,9},{9,8},{10,11... | collective-permute-start | bytes 884744 | tf_op jit(solution)/shard_map/ppermute | solution.py:518
  32.7 4.9 %collective-permute-start.1 = (bf16[128,3072]{1,0:T(8,128)(2,1)}, bf16[128,3072]{1,0:T(8,128)(2,1)}, u32[]{:S(2)}, u32[]{:S(2)}) collective-permute-start(bf16[128,3072]{1,0:T(8,128)(2,1)} %get-tuple-element.55.refs_1_), channel_id=1, source_target_pairs={{0,1},{1,0},{2,3},{3,2},{4,5},{5,4},{6,7},{7,6},{8,9},{9,8},{10,11... | collective-permute-start | bytes 2359304 | tf_op jit(solution)/shard_map/ppermute | solution.py:536
  32.8 13.8 %all-to-all-start.1 = ((bf16[16,8,1024]{2,1,0:T(8,128)(2,1)}), bf16[16,8,1024]{2,1,0:T(8,128)(2,1)}, u32[]{:S(2)}, u32[]{:S(2)}) async-start(bf16[16,8,1024]{2,1,0:T(8,128)(2,1)} %bitcast.21), calls=%async_computation.1 | async-start | bytes 524288 | tf_op jit(solution)/shard_map/all_to_all | solution.py:487
  41.5 17.7 %collective-permute-start.4 = (bf16[128,2048]{1,0:T(8,128)(2,1)}, bf16[128,2048]{1,0:T(8,128)(2,1)}, u32[]{:S(2)}, u32[]{:S(2)}) collective-permute-start(bf16[128,2048]{1,0:T(8,128)(2,1)} %get-tuple-element.70), channel_id=1, source_target_pairs={{0,16},{1,5},{2,18},{3,7},{4,20},{5,9},{6,22},{7,11},{8,24},{9,13}... | collective-permute-start | bytes 1572872 | tf_op jit(solution)/shard_map/ppermute | solution.py:554
  43.1 16.2 %collective-permute-start.5 = (bf16[128,2048]{1,0:T(8,128)(2,1)}, bf16[128,2048]{1,0:T(8,128)(2,1)}, u32[]{:S(2)}, u32[]{:S(2)}) collective-permute-start(bf16[128,2048]{1,0:T(8,128)(2,1)} %get-tuple-element.71), channel_id=1, source_target_pairs={{0,48},{1,13},{2,50},{3,15},{4,52},{5,1},{6,54},{7,3},{8,56},{9,5}... | collective-permute-start | bytes 1572872 | tf_op jit(solution)/shard_map/ppermute | solution.py:554
  44.9 14.4 %collective-permute-start.6 = (bf16[128,2048]{1,0:T(8,128)(2,1)}, bf16[128,2048]{1,0:T(8,128)(2,1)}, u32[]{:S(2)}, u32[]{:S(2)}) collective-permute-start(bf16[128,2048]{1,0:T(8,128)(2,1)} %get-tuple-element.72), channel_id=1, source_target_pairs={{0,32},{1,9},{2,34},{3,11},{4,36},{5,13},{6,38},{7,15},{8,40},{9,1... | collective-permute-start | bytes 1572872 | tf_op jit(solution)/shard_map/ppermute | solution.py:554
  52.5 2.4 %collective-permute-start.3 = (bf16[144,1536]{1,0:T(8,128)(2,1)}, bf16[144,1536]{1,0:T(8,128)(2,1)}, u32[]{:S(2)}, u32[]{:S(2)}) collective-permute-start(bf16[144,1536]{1,0:T(8,128)(2,1)} %get-tuple-element.78.refs_5_.d_mix_hbm), channel_id=1, source_target_pairs={{0,1},{1,0},{2,3},{3,2},{4,5},{5,4},{6,7},{7,6},{8,9},{9,8},{10,11... | collective-permute-start | bytes 1327112 | tf_op jit(solution)/shard_map/ppermute | solution.py:582
  52.6 2.3 %collective-permute-start.2 = (bf16[144,512]{1,0:T(8,128)(2,1)}, bf16[144,512]{1,0:T(8,128)(2,1)}, u32[]{:S(2)}, u32[]{:S(2)}) collective-permute-start(bf16[144,512]{1,0:T(8,128)(2,1)} %get-tuple-element.64), channel_id=1, source_target_pairs={{0,1},{1,0},{2,3},{3,2},{4,5},{5,4},{6,7},{7,6},{8,9},{9,8},{10,11... | collective-permute-start | bytes 442376 | tf_op jit(solution)/shard_map/ppermute | solution.py:581
  59.3 13.8 %collective-permute-start.8 = (bf16[128,2048]{1,0:T(8,128)(2,1)}, bf16[128,2048]{1,0:T(8,128)(2,1)}, u32[]{:S(2)}, u32[]{:S(2)}) collective-permute-start(bf16[128,2048]{1,0:T(8,128)(2,1)} %get-tuple-element.75), channel_id=1, source_target_pairs={{0,16},{1,5},{2,18},{3,7},{4,20},{5,9},{6,22},{7,11},{8,24},{9,13}... | collective-permute-start | bytes 1572872 | tf_op jit(solution)/shard_map/ppermute | solution.py:554
  60.5 14.8 %collective-permute-start.9 = (bf16[128,2048]{1,0:T(8,128)(2,1)}, bf16[128,2048]{1,0:T(8,128)(2,1)}, u32[]{:S(2)}, u32[]{:S(2)}) collective-permute-start(bf16[128,2048]{1,0:T(8,128)(2,1)} %get-tuple-element.76), channel_id=1, source_target_pairs={{0,48},{1,13},{2,50},{3,15},{4,52},{5,1},{6,54},{7,3},{8,56},{9,5}... | collective-permute-start | bytes 1572872 | tf_op jit(solution)/shard_map/ppermute | solution.py:554
  62.6 13.7 %collective-permute-start.10 = (bf16[128,2048]{1,0:T(8,128)(2,1)}, bf16[128,2048]{1,0:T(8,128)(2,1)}, u32[]{:S(2)}, u32[]{:S(2)}) collective-permute-start(bf16[128,2048]{1,0:T(8,128)(2,1)} %get-tuple-element.77), channel_id=1, source_target_pairs={{0,32},{1,9},{2,34},{3,11},{4,36},{5,13},{6,38},{7,15},{8,40},{9,1... | collective-permute-start | bytes 1572872 | tf_op jit(solution)/shard_map/ppermute | solution.py:554
  67.6 5.5 %copy-start = (f32[4,1024]{1,0:T(4,128)S(1)}, f32[4,1024]{1,0:T(4,128)}, u32[]{:S(2)}) copy-start(f32[4,1024]{1,0:T(4,128)} %shard_map.133) | copy-start | bytes 49156
  67.6 5.5 %collective-permute-start.7 = (f32[4,1024]{1,0:T(4,128)}, f32[4,1024]{1,0:T(4,128)S(1)}, u32[]{:S(2)}, u32[]{:S(2)}) collective-permute-start(f32[4,1024]{1,0:T(4,128)} %shard_map.133), channel_id=1, source_target_pairs={{0,2},{2,0},{1,3},{3,1},{4,6},{6,4},{5,7},{7,5},{8,10},{10,8},{9,1... | collective-permute-start | bytes 49160 | tf_op jit(solution)/shard_map/ppermute | solution.py:608
  78.9 22.0 %all-to-all-start.2 = ((bf16[16,8,4096]{2,1,0:T(8,128)(2,1)}), bf16[16,8,4096]{2,1,0:T(8,128)(2,1)}, u32[]{:S(2)}, u32[]{:S(2)}) async-start(bf16[16,8,4096]{2,1,0:T(8,128)(2,1)} %bitcast.14), calls=%async_computation.2 | async-start | bytes 2097152 | tf_op jit(solution)/shard_map/all_to_all | solution.py:647
  85.6 1.3 %collective-permute-start.11 = (f32[4,1024]{1,0:T(4,128)S(1)}, f32[4,1024]{1,0:T(4,128)S(1)}, u32[]{:S(2)}, u32[]{:S(2)}) collective-permute-start(f32[4,1024]{1,0:T(4,128)S(1)} %add.31), channel_id=1, source_target_pairs={{0,1},{1,0},{2,3},{3,2},{4,5},{5,4},{6,7},{7,6},{8,9},{9,8},{10,11... | collective-permute-start | bytes 49160 | tf_op jit(solution)/shard_map/ppermute | solution.py:608
  86.9 8.9 %collective-permute-start.12 = (f32[4,1024]{1,0:T(4,128)S(1)}, f32[4,1024]{1,0:T(4,128)S(1)}, u32[]{:S(2)}, u32[]{:S(2)}) collective-permute-start(f32[4,1024]{1,0:T(4,128)S(1)} %add.33), channel_id=1, source_target_pairs={{0,12},{4,0},{8,4},{12,8},{1,13},{5,1},{9,5},{13,9},{2,14},{6,2},{... | collective-permute-start | bytes 49160 | tf_op jit(solution)/shard_map/ppermute | solution.py:626
  89.9 7.3 %collective-permute-start.13 = (f32[4,1024]{1,0:T(4,128)S(1)}, f32[4,1024]{1,0:T(4,128)S(1)}, u32[]{:S(2)}, u32[]{:S(2)}) collective-permute-start(f32[4,1024]{1,0:T(4,128)S(1)} %add.33), channel_id=1, source_target_pairs={{0,8},{4,12},{8,0},{12,4},{1,9},{5,13},{9,1},{13,5},{2,10},{6,14},... | collective-permute-start | bytes 49160 | tf_op jit(solution)/shard_map/ppermute | solution.py:626
  90.8 6.5 %collective-permute-start.14 = (f32[4,1024]{1,0:T(4,128)S(1)}, f32[4,1024]{1,0:T(4,128)S(1)}, u32[]{:S(2)}, u32[]{:S(2)}) collective-permute-start(f32[4,1024]{1,0:T(4,128)S(1)} %add.33), channel_id=1, source_target_pairs={{0,4},{4,8},{8,12},{12,0},{1,5},{5,9},{9,13},{13,1},{2,6},{6,10},{... | collective-permute-start | bytes 49160 | tf_op jit(solution)/shard_map/ppermute | solution.py:626

commit v7 on v6

--- a/solution.py
+++ b/solution.py
@@ -38,51 +38,49 @@
     return low.astype(BF), (1.0 - low).astype(BF)
 
 
+def head_pairs(mix_ref):
+    side = mix_ref.shape[1] // 3
+    width = 2 * (side // HEADS)
+
+    def columns(part, p):
+        return mix_ref[:, part * side + p * width : part * side + (p + 1) * width]
+
+    return side, width, 1.0 / math.sqrt(width // 2), columns
+
+
 def attention_forward(mix_ref, keep, masks, save, put):
-    width = 2 * (mix_ref.shape[1] // 3 // HEADS)
-    side = mix_ref.shape[1] // 3
-    factor = 1.0 / math.sqrt(width // 2)
+    _, width, factor, columns = head_pairs(mix_ref)
+    heads = [(p, h) for p in range(HEADS // 2) for h in range(2)]
+    scores = [mm(columns(1, p) * masks[h], columns(0, p), NT) * factor for p, h in heads]
+    scores = [jnp.where(keep, s, -jnp.inf) for s in scores]
+    tops = [jnp.max(s, axis=0, keepdims=True) for s in scores]
+    expons = [jnp.exp(s - t) for s, t in zip(scores, tops)]
+    sums = [1.0 / jnp.sum(e, axis=0, keepdims=True) for e in expons]
+    weights = [e * r for e, r in zip(expons, sums)]
+    for k, w in enumerate(weights):
+        save(k, w)
+    parts = [mm(w.astype(BF), columns(2, p) * masks[h], TN) for w, (p, h) in zip(weights, heads)]
     for p in range(HEADS // 2):
-        q2 = mix_ref[:, p * width : (p + 1) * width]
-        k2 = mix_ref[:, side + p * width : side + (p + 1) * width]
-        v2 = mix_ref[:, 2 * side + p * width : 2 * side + (p + 1) * width]
-        total = None
-        for h in range(2):
-            scores = mm(k2 * masks[h], q2, NT) * factor
-            scores = jnp.where(keep, scores, -jnp.inf)
-            expon = jnp.exp(scores - jnp.max(scores, axis=0, keepdims=True))
-            weights = expon * (1.0 / jnp.sum(expon, axis=0, keepdims=True))
-            save(2 * p + h, weights)
-            part = mm(weights.astype(BF), v2 * masks[h], TN)
-            total = part if total is None else total + part
-        put(p, width, total.astype(BF))
+        put(p, width, (parts[2 * p] + parts[2 * p + 1]).astype(BF))
 
 
 def attention_backward(mix_ref, load, d_att, masks, put):
-    width = 2 * (mix_ref.shape[1] // 3 // HEADS)
-    side = mix_ref.shape[1] // 3
-    factor = 1.0 / math.sqrt(width // 2)
-    for p in range(HEADS // 2):
-        q2 = mix_ref[:, p * width : (p + 1) * width]
-        k2 = mix_ref[:, side + p * width : side + (p + 1) * width]
-        v2 = mix_ref[:, 2 * side + p * width : 2 * side + (p + 1) * width]
-        d2 = d_att[:, p * width : (p + 1) * width]
-        dq = dk = dv = None
-        for h in range(2):
-            dh = d2 * masks[h]
-            weights = load(2 * p + h)
-            grad = mm(v2, dh, NT)
-            centre = jnp.sum(weights * grad, axis=0, keepdims=True)
-            ds = (weights * (grad - centre) * factor).astype(BF)
-            a = mm(ds, k2 * masks[h], TN)
-            b = mm(ds, q2 * masks[h], NN)
-            c = mm(weights.astype(BF), dh, NN)
-            dq = a if dq is None else dq + a
-            dk = b if dk is None else dk + b
-            dv = c if dv is None else dv + c
-        put(p * width, width, dq.astype(BF))
-        put(side + p * width, width, dk.astype(BF))
-        put(2 * side + p * width, width, dv.astype(BF))
+    side, width, factor, columns = head_pairs(mix_ref)
+    heads = [(p, h) for p in range(HEADS // 2) for h in range(2)]
+    d_heads = [d_att[:, p * width : (p + 1) * width] * masks[h] for p, h in heads]
+    grads = [mm(columns(2, p), d, NT) for d, (p, _) in zip(d_heads, heads)]
+    scores_grads = []
+    for k, grad in enumerate(grads):
+        weights = load(k)
+        centre = jnp.sum(weights * grad, axis=0, keepdims=True)
+        scores_grads.append((weights * (grad - centre) * factor).astype(BF))
+    dv = [mm(load(k, True).astype(BF), d, NN) for k, d in enumerate(d_heads)]
+    dk = [mm(g, columns(0, p) * masks[h], NN) for g, (p, h) in zip(scores_grads, heads)]
+    dq = [mm(g, columns(1, p) * masks[h], TN) for g, (p, h) in zip(scores_grads, heads)]
+    for part, each in enumerate((dq, dk, dv)):
+        for p in range(HEADS // 2):
+            value = each[2 * p] + each[2 * p + 1]
+            put(part * side + p * width, width, value.astype(BF))
 
 
 def inputs_gradient(c, normed, inverse, d_normed):
@@ -244,7 +242,7 @@
     def put_grad(at, w, value):
         send[:, at_mix + at : at_mix + at + w] = value
 
-    attention_backward(mix, lambda h: weights_buf[h], d_att, masks, put_grad)
+    attention_backward(mix, lambda h, again=False: weights_buf[h], d_att, masks, put_grad)
     outs.append(move.start(send, send_hbm))
     d_normed = mm(send[:, at_mix:], entry[...], NT)
     back[...] = inputs_gradient(cot, normed, inverse, d_normed).astype(BF)
@@ -283,8 +281,9 @@
     masks = half_masks(side // HEADS)
     second.wait()
 
-    def load(h):
-        heads[h].wait()
+    def load(h, again=False):
+        if not again:
+            heads[h].wait()
         return weights_buf[h]
 
     def put_grad(at, w, value):

time: 104 us -> 102 us (0.981)
  Pallas kernels: 42.9 us -> 39.7 us
  waiting for transfers between devices: 20.5 us -> 21.6 us
    pallas_call x11, Pallas kernels: 42.9 us -> 39.7 us  [call(): pl.pallas_call(kernel, out_shape=tuple((jax.ShapeDtypeStruct(s, d) for s,...]
    ppermute x6, waiting for transfers between devices: 3.13 us -> 5.02 us  [passed_on(): lax.ppermute(parts[k], ALL, first_pairs(shape, k))]
  transfers between devices with their start and end apart: 18 -> 18, of which waited for: 10 -> 10; matrix products, arithmetic and copies ran while one was open for 1% -> 1% of each run, Pallas kernels for 26% -> 25%
where the time goes in v7:
time: 102 us; the launch traced here: 101 us
  Pallas kernels  39.7 us (39%)
  starting transfers between devices  37.6 us (37%)
  waiting for transfers between devices  21.6 us (21%)
  other arithmetic  1.22 us (1%)
    pallas_call x11, Pallas kernels, call(): pl.pallas_call(kernel, out_shape=tuple((jax.ShapeDtypeStruct(s, d) for s,...  39.7 us
    all_to_all x2, starting transfers between devices, exchange(): return lax.all_to_all(blocks, FRAME, 0, 0, tiled=True).reshape(array.shape)  12.2 us
    ppermute x6, starting transfers between devices, passed_on(): lax.ppermute(parts[k], ALL, first_pairs(shape, k))  8.85 us
    all_to_all x2, waiting for transfers between devices, exchange(): return lax.all_to_all(blocks, FRAME, 0, 0, tiled=True).reshape(array.shape)  8.06 us
    all_to_all x1, starting transfers between devices, per_device(): lax.all_to_all(both.reshape(count, -1, 8 * side), ALL, 0, 0, axis_index_g...  7.3 us
    ppermute x6, waiting for transfers between devices, passed_on(): lax.ppermute(parts[k], ALL, first_pairs(shape, k))  5.02 us
    ppermute x3, starting transfers between devices, per_device(): lax.ppermute(local, 'y', [(i, (i + k) % ys) for i in range(ys)])  4.72 us
    ppermute x2, starting transfers between devices, with_partner(): return local + lax.ppermute(local, axis, pairs)  3.41 us
  transfers between devices with their start and end apart: 18, of which 10 were waited for; matrix products, arithmetic and copies ran while one was open for 1% of the time, Pallas kernels for 25%

profile of v7, /device:TPU:0, one launch (start us, length us, event | category | flops | bytes accessed | tf_op | source)
XLA Modules:
  0.0 101.1 jit_solution(2738586318478484094)
XLA Ops:
  0.6 4.6 %shard_map.127 = (bf16[128,2048]{1,0:T(8,128)(2,1)}, bf16[144,1536]{1,0:T(8,128)(2,1)}, f32[8,144,144]{2,1,0:T(8,128)}, bf16[144,512]{1,0:T(8,128)(2,1)}) custom-call(bf16[128,1024]{1,0:T(8,128)(2,1)} %bitcast.15, bf16[4,1024]{1,0:T(4,128)(2,1)} %bitcast.22, bf16[1024,1536]{1,0:T(8,128)(2,1)} %entry_hbm.7, bf16[1024,512]{1,0:T(8,128)(2,1)} %exit_hbm.5, ...), custom_call_target="tpu_custom_call" | custom-call | flops 1000 | bytes 1000 | tf_op jit(solution)/shard_map/pallas_call | solution.py:432
  5.2 8.0 %all-to-all-start = ((bf16[16,8,2048]{2,1,0:T(8,128)(2,1)}), bf16[16,8,2048]{2,1,0:T(8,128)(2,1)}, u32[]{:S(2)}, u32[]{:S(2)}) async-start(bf16[16,8,2048]{2,1,0:T(8,128)(2,1)} %bitcast.18), calls=%async_computation | async-start | bytes 1048576 | tf_op jit(solution)/shard_map/all_to_all | solution.py:486
  13.3 2.3 %shard_map.128 = (bf16[144,1024]{1,0:T(8,128)(2,1)}, bf16[144,512]{1,0:T(8,128)(2,1)}) custom-call(s32[1]{0:T(128)} %bitcast.1.core_ref, bf16[128,1024]{1,0:T(8,128)(2,1)} %bitcast.16, bf16[4,1024]{1,0:T(4,128)(2,1)} %bitcast.23, bf16[144,512]{1,0:T(8,128)(2,1)} %get-tuple-element.50.att_hbm), custom_call_target="tpu_custom_call" | custom-call | flops 1000 | bytes 1000 | tf_op jit(solution)/shard_map/pallas_call | solution.py:432
  15.6 0.4 collective-permute-start
  16.0 1.6 %collective-permute-done.refs_2_ = bf16[144,1024]{1,0:T(8,128)(2,1)} collective-permute-done((bf16[144,1024]{1,0:T(8,128)(2,1)}, bf16[144,1024]{1,0:T(8,128)(2,1)}, u32[]{:S(2)}, u32[]{:S(2)}) %collective-permute-start) | collective-permute-done | bytes 294944 | tf_op jit(solution)/shard_map/ppermute | solution.py:517
  17.6 8.1 %all-to-all-done = bf16[16,8,2048]{2,1,0:T(8,128)(2,1)} async-done(((bf16[16,8,2048]{2,1,0:T(8,128)(2,1)}), bf16[16,8,2048]{2,1,0:T(8,128)(2,1)}, u32[]{:S(2)}, u32[]{:S(2)}) %all-to-all-start) | async-done | bytes 524320 | tf_op jit(solution)/shard_map/all_to_all | solution.py:486
  25.7 5.6 %shard_map.129 = (bf16[128,1024]{1,0:T(8,128)(2,1)}, bf16[128,3072]{1,0:T(8,128)(2,1)}, bf16[128,1024]{1,0:T(8,128)(2,1)}) custom-call(s32[1]{0:T(128)} %bitcast.1.core_ref, bf16[128,2048]{1,0:T(8,128)(2,1)} %bitcast.5.moved_hbm, bf16[1024,1536]{1,0:T(8,128)(2,1)} %entry_hbm.5, bf16[1024,512]{1,0:T(8,128)(2,1)} %exit_hbm.4), custom_call_target="tpu_custom_call" | custom-call | flops 1000 | bytes 1000 | tf_op jit(solution)/shard_map/pallas_call | solution.py:432
  31.3 0.1 collective-permute-start.1
  31.4 4.2 %all-to-all-start.1 = ((bf16[16,8,1024]{2,1,0:T(8,128)(2,1)}), bf16[16,8,1024]{2,1,0:T(8,128)(2,1)}, u32[]{:S(2)}, u32[]{:S(2)}) async-start(bf16[16,8,1024]{2,1,0:T(8,128)(2,1)} %bitcast.21), calls=%async_computation.1 | async-start | bytes 524288 | tf_op jit(solution)/shard_map/all_to_all | solution.py:486
  35.6 0.6 pad_add_fusion.place_ref
  36.2 0.0 collective-permute-done.1.refs_2_
  36.2 3.9 %shard_map.130 = (bf16[128,2048]{1,0:T(8,128)(2,1)}, bf16[128,2048]{1,0:T(8,128)(2,1)}, bf16[128,2048]{1,0:T(8,128)(2,1)}, bf16[128,2048]{1,0:T(8,128)(2,1)}) custom-call(s32[2]{0:T(128)} %pad_add_fusion.place_ref, bf16[128,1024]{1,0:T(8,128)(2,1)} %get-tuple-element.54.refs_0_, bf16[128,3072]{1,0:T(8,128)(2,1)} %get-tuple-element.55.refs_1_, ...), custom_call_target="tpu_custom_call" | custom-call | flops 1000 | bytes 1000 | tf_op jit(solution)/shard_map/pallas_call | solution.py:432
  40.1 1.5 %collective-permute-start.4 = (bf16[128,2048]{1,0:T(8,128)(2,1)}, bf16[128,2048]{1,0:T(8,128)(2,1)}, u32[]{:S(2)}, u32[]{:S(2)}) collective-permute-start(bf16[128,2048]{1,0:T(8,128)(2,1)} %get-tuple-element.70), channel_id=1, source_target_pairs={{0,16},{1,5},{2,18},{3,7},{4,20},{5,9},{6,22},{7,11},{8,24},{9,13}... | collective-permute-start | bytes 1572872 | tf_op jit(solution)/shard_map/ppermute | solution.py:553
  41.7 1.8 %collective-permute-start.5 = (bf16[128,2048]{1,0:T(8,128)(2,1)}, bf16[128,2048]{1,0:T(8,128)(2,1)}, u32[]{:S(2)}, u32[]{:S(2)}) collective-permute-start(bf16[128,2048]{1,0:T(8,128)(2,1)} %get-tuple-element.71), channel_id=1, source_target_pairs={{0,48},{1,13},{2,50},{3,15},{4,52},{5,1},{6,54},{7,3},{8,56},{9,5}... | collective-permute-start | bytes 1572872 | tf_op jit(solution)/shard_map/ppermute | solution.py:553
  43.4 1.8 %collective-permute-start.6 = (bf16[128,2048]{1,0:T(8,128)(2,1)}, bf16[128,2048]{1,0:T(8,128)(2,1)}, u32[]{:S(2)}, u32[]{:S(2)}) collective-permute-start(bf16[128,2048]{1,0:T(8,128)(2,1)} %get-tuple-element.72), channel_id=1, source_target_pairs={{0,32},{1,9},{2,34},{3,11},{4,36},{5,13},{6,38},{7,15},{8,40},{9,1... | collective-permute-start | bytes 1572872 | tf_op jit(solution)/shard_map/ppermute | solution.py:553
  45.2 0.0 all-to-all-done.1
  45.2 4.0 %shard_map.131 = (bf16[144,512]{1,0:T(8,128)(2,1)}, bf16[144,512]{1,0:T(8,128)(2,1)}, bf16[144,1536]{1,0:T(8,128)(2,1)}) custom-call(s32[1]{0:T(128)} %bitcast.1.core_ref, bf16[128,1024]{1,0:T(8,128)(2,1)} %bitcast.7.back_hbm, bf16[4,1024]{1,0:T(4,128)(2,1)} %bitcast.25, bf16[144,1536]{1,0:T(8,128)(2,1)} %get-tuple-element.58.mix_hbm, ...), custom_call_target="tpu_custom_call" | custom-call | flops 1000 | bytes 1000 | tf_op jit(solution)/shard_map/pallas_call | solution.py:432
  49.2 0.1 collective-permute-start.3
  49.3 0.5 collective-permute-start.2
  49.8 1.8 %collective-permute-done.2.refs_4_ = bf16[144,512]{1,0:T(8,128)(2,1)} collective-permute-done((bf16[144,512]{1,0:T(8,128)(2,1)}, bf16[144,512]{1,0:T(8,128)(2,1)}, u32[]{:S(2)}, u32[]{:S(2)}) %collective-permute-start.2) | collective-permute-done | bytes 147488 | tf_op jit(solution)/shard_map/ppermute | solution.py:580
  51.7 0.0 collective-permute-done.3.refs_6_
  51.7 4.4 %shard_map.132 = (bf16[128,2048]{1,0:T(8,128)(2,1)}, bf16[128,2048]{1,0:T(8,128)(2,1)}, bf16[128,2048]{1,0:T(8,128)(2,1)}, bf16[128,2048]{1,0:T(8,128)(2,1)}) custom-call(s32[2]{0:T(128)} %pad_add_fusion.place_ref, bf16[144,512]{1,0:T(8,128)(2,1)} %get-tuple-element.61.refs_0_, bf16[144,1024]{1,0:T(8,128)(2,1)} %get-tuple-element.51.refs_1_, ...), custom_call_target="tpu_custom_call" | custom-call | flops 1000 | bytes 1000 | tf_op jit(solution)/shard_map/pallas_call | solution.py:432
  56.0 0.0 collective-permute-done.4.a_hbm
  56.0 0.0 collective-permute-done.5.b_hbm
  56.1 1.4 %collective-permute-done.6.c_hbm = bf16[128,2048]{1,0:T(8,128)(2,1)} collective-permute-done((bf16[128,2048]{1,0:T(8,128)(2,1)}, bf16[128,2048]{1,0:T(8,128)(2,1)}, u32[]{:S(2)}, u32[]{:S(2)}) %collective-permute-start.6) | collective-permute-done | bytes 524320 | tf_op jit(solution)/shard_map/ppermute | solution.py:553
  57.5 1.4 %collective-permute-start.8 = (bf16[128,2048]{1,0:T(8,128)(2,1)}, bf16[128,2048]{1,0:T(8,128)(2,1)}, u32[]{:S(2)}, u32[]{:S(2)}) collective-permute-start(bf16[128,2048]{1,0:T(8,128)(2,1)} %get-tuple-element.75), channel_id=1, source_target_pairs={{0,16},{1,5},{2,18},{3,7},{4,20},{5,9},{6,22},{7,11},{8,24},{9,13}... | collective-permute-start | bytes 1572872 | tf_op jit(solution)/shard_map/ppermute | solution.py:553
  58.9 1.8 %collective-permute-start.9 = (bf16[128,2048]{1,0:T(8,128)(2,1)}, bf16[128,2048]{1,0:T(8,128)(2,1)}, u32[]{:S(2)}, u32[]{:S(2)}) collective-permute-start(bf16[128,2048]{1,0:T(8,128)(2,1)} %get-tuple-element.76), channel_id=1, source_target_pairs={{0,48},{1,13},{2,50},{3,15},{4,52},{5,1},{6,54},{7,3},{8,56},{9,5}... | collective-permute-start | bytes 1572872 | tf_op jit(solution)/shard_map/ppermute | solution.py:553
  60.7 0.5 collective-permute-start.10
  61.2 3.6 %shard_map.133 = f32[4,1024]{1,0:T(4,128)} custom-call(bf16[4,1024]{1,0:T(4,128)(2,1)} %bitcast.24, bf16[4,1024]{1,0:T(4,128)(2,1)} %bitcast.26, bf16[144,1536]{1,0:T(8,128)(2,1)} %get-tuple-element.78.refs_5_.d_mix_hbm, bf16[1024,1536]{1,0:T(8,128)(2,1)} %entry_hbm.7), custom_call_target="tpu_custom_call" | custom-call | flops 1000 | bytes 1000 | tf_op jit(solution)/shard_map/pallas_call | solution.py:432
  64.8 0.0 copy-start
  64.8 3.3 %collective-permute-start.7 = (f32[4,1024]{1,0:T(4,128)}, f32[4,1024]{1,0:T(4,128)S(1)}, u32[]{:S(2)}, u32[]{:S(2)}) collective-permute-start(f32[4,1024]{1,0:T(4,128)} %shard_map.133), channel_id=1, source_target_pairs={{0,2},{2,0},{1,3},{3,1},{4,6},{6,4},{5,7},{7,5},{8,10},{10,8},{9,1... | collective-permute-start | bytes 49160 | tf_op jit(solution)/shard_map/ppermute | solution.py:607
  68.1 2.5 %shard_map.135.refs_0_ = bf16[128,4096]{1,0:T(8,128)(2,1)} custom-call(bf16[128,2048]{1,0:T(8,128)(2,1)} %get-tuple-element.84.own_hbm, bf16[128,2048]{1,0:T(8,128)(2,1)} %collective-permute-done.4.a_hbm, bf16[128,2048]{1,0:T(8,128)(2,1)} %collective-permute-done.5.b_hbm, bf16[128,2048]{1,0:T(8,128)(2,1)} %collective-permute-done.6.c_hbm), custom_call_target="tpu_custom_call" | custom-call | flops 1000 | bytes 1000 | tf_op jit(solution)/shard_map/pallas_call | solution.py:432
  70.7 0.0 collective-permute-done.7
  70.7 0.0 copy-done
  70.7 0.0 collective-permute-done.8.a_hbm
  70.7 2.7 %collective-permute-done.9.b_hbm = bf16[128,2048]{1,0:T(8,128)(2,1)} collective-permute-done((bf16[128,2048]{1,0:T(8,128)(2,1)}, bf16[128,2048]{1,0:T(8,128)(2,1)}, u32[]{:S(2)}, u32[]{:S(2)}) %collective-permute-start.9) | collective-permute-done | bytes 524320 | tf_op jit(solution)/shard_map/ppermute | solution.py:553
  73.4 0.9 collective-permute-done.10.c_hbm
  74.3 2.6 %shard_map.136 = bf16[128,4096]{1,0:T(8,128)(2,1)} custom-call(bf16[128,2048]{1,0:T(8,128)(2,1)} %get-tuple-element.80.own_hbm, bf16[128,2048]{1,0:T(8,128)(2,1)} %collective-permute-done.8.a_hbm, bf16[128,2048]{1,0:T(8,128)(2,1)} %collective-permute-done.9.b_hbm, bf16[128,2048]{1,0:T(8,128)(2,1)} %collective-permute-done.10.c_hbm, ...), custom_call_target="tpu_custom_call", output_to_operand_aliasing={{}: (4, {})} | custom-call | flops 1000 | bytes 1000 | tf_op jit(solution)/shard_map/pallas_call | solution.py:432
  76.9 7.3 %all-to-all-start.2 = ((bf16[16,8,4096]{2,1,0:T(8,128)(2,1)}), bf16[16,8,4096]{2,1,0:T(8,128)(2,1)}, u32[]{:S(2)}, u32[]{:S(2)}) async-start(bf16[16,8,4096]{2,1,0:T(8,128)(2,1)} %bitcast.14), calls=%async_computation.2 | async-start | bytes 2097152 | tf_op jit(solution)/shard_map/all_to_all | solution.py:646
  84.2 0.1 collective-permute-start.11
  84.3 1.2 %collective-permute-done.11 = f32[4,1024]{1,0:T(4,128)S(1)} collective-permute-done((f32[4,1024]{1,0:T(4,128)S(1)}, f32[4,1024]{1,0:T(4,128)S(1)}, u32[]{:S(2)}, u32[]{:S(2)}) %collective-permute-start.11) | collective-permute-done | bytes 16416 | tf_op jit(solution)/shard_map/ppermute | solution.py:607
  85.5 3.0 %collective-permute-start.12 = (f32[4,1024]{1,0:T(4,128)S(1)}, f32[4,1024]{1,0:T(4,128)S(1)}, u32[]{:S(2)}, u32[]{:S(2)}) collective-permute-start(f32[4,1024]{1,0:T(4,128)S(1)} %add.33), channel_id=1, source_target_pairs={{0,12},{4,0},{8,4},{12,8},{1,13},{5,1},{9,5},{13,9},{2,14},{6,2},{... | collective-permute-start | bytes 49160 | tf_op jit(solution)/shard_map/ppermute | solution.py:625
  88.5 0.9 collective-permute-start.13
  89.3 0.9 collective-permute-start.14
  90.2 4.2 %shard_map.134 = bf16[128,1024]{1,0:T(8,128)(2,1)} custom-call(bf16[128,1024]{1,0:T(8,128)(2,1)} %bitcast.17, bf16[128,1024]{1,0:T(8,128)(2,1)} %bitcast.7.back_hbm, bf16[144,1536]{1,0:T(8,128)(2,1)} %get-tuple-element.78.refs_5_.d_mix_hbm, bf16[1024,1536]{1,0:T(8,128)(2,1)} %entry_hbm.7), custom_call_target="tpu_custom_call" | custom-call | flops 1000 | bytes 1000 | tf_op jit(solution)/shard_map/pallas_call | solution.py:432
  94.4 0.0 collective-permute-done.12
  94.4 1.2 %collective-permute-done.13 = f32[4,1024]{1,0:T(4,128)S(1)} collective-permute-done((f32[4,1024]{1,0:T(4,128)S(1)}, f32[4,1024]{1,0:T(4,128)S(1)}, u32[]{:S(2)}, u32[]{:S(2)}) %collective-permute-start.13) | collective-permute-done | bytes 16416 | tf_op jit(solution)/shard_map/ppermute | solution.py:625
  95.6 0.1 collective-permute-done.14
  95.7 0.6 fusion
  96.3 2.6 %all-to-all-done.2.parts_hbm = bf16[16,8,4096]{2,1,0:T(8,128)(2,1)} async-done(((bf16[16,8,4096]{2,1,0:T(8,128)(2,1)}), bf16[16,8,4096]{2,1,0:T(8,128)(2,1)}, u32[]{:S(2)}, u32[]{:S(2)}) %all-to-all-start.2) | async-done | bytes 1048608 | tf_op jit(solution)/shard_map/all_to_all | solution.py:646
  98.9 2.0 %shard_map.137 = (bf16[8,1536]{1,0:T(8,128)(2,1)}, bf16[8,512]{1,0:T(8,128)(2,1)}, bf16[8,1536]{1,0:T(8,128)(2,1)}, bf16[8,512]{1,0:T(8,128)(2,1)}) custom-call(bf16[16,8,4096]{2,1,0:T(8,128)(2,1)} %all-to-all-done.2.parts_hbm), custom_call_target="tpu_custom_call" | custom-call | flops 1000 | bytes 1000 | tf_op jit(solution)/shard_map/pallas_call | solution.py:432
  (2 shorter events, 0.0 us)
Async XLA Ops:
  5.2 20.5 %all-to-all-start = ((bf16[16,8,2048]{2,1,0:T(8,128)(2,1)}), bf16[16,8,2048]{2,1,0:T(8,128)(2,1)}, u32[]{:S(2)}, u32[]{:S(2)}) async-start(bf16[16,8,2048]{2,1,0:T(8,128)(2,1)} %bitcast.18), calls=%async_computation | async-start | bytes 1048576 | tf_op jit(solution)/shard_map/all_to_all | solution.py:486
  15.6 2.0 %collective-permute-start = (bf16[144,1024]{1,0:T(8,128)(2,1)}, bf16[144,1024]{1,0:T(8,128)(2,1)}, u32[]{:S(2)}, u32[]{:S(2)}) collective-permute-start(bf16[144,1024]{1,0:T(8,128)(2,1)} %get-tuple-element.51.refs_1_), channel_id=1, source_target_pairs={{0,1},{1,0},{2,3},{3,2},{4,5},{5,4},{6,7},{7,6},{8,9},{9,8},{10,11... | collective-permute-start | bytes 884744 | tf_op jit(solution)/shard_map/ppermute | solution.py:517
  31.3 4.9 %collective-permute-start.1 = (bf16[128,3072]{1,0:T(8,128)(2,1)}, bf16[128,3072]{1,0:T(8,128)(2,1)}, u32[]{:S(2)}, u32[]{:S(2)}) collective-permute-start(bf16[128,3072]{1,0:T(8,128)(2,1)} %get-tuple-element.55.refs_1_), channel_id=1, source_target_pairs={{0,1},{1,0},{2,3},{3,2},{4,5},{5,4},{6,7},{7,6},{8,9},{9,8},{10,11... | collective-permute-start | bytes 2359304 | tf_op jit(solution)/shard_map/ppermute | solution.py:535
  31.4 13.8 %all-to-all-start.1 = ((bf16[16,8,1024]{2,1,0:T(8,128)(2,1)}), bf16[16,8,1024]{2,1,0:T(8,128)(2,1)}, u32[]{:S(2)}, u32[]{:S(2)}) async-start(bf16[16,8,1024]{2,1,0:T(8,128)(2,1)} %bitcast.21), calls=%async_computation.1 | async-start | bytes 524288 | tf_op jit(solution)/shard_map/all_to_all | solution.py:486
  40.1 15.9 %collective-permute-start.4 = (bf16[128,2048]{1,0:T(8,128)(2,1)}, bf16[128,2048]{1,0:T(8,128)(2,1)}, u32[]{:S(2)}, u32[]{:S(2)}) collective-permute-start(bf16[128,2048]{1,0:T(8,128)(2,1)} %get-tuple-element.70), channel_id=1, source_target_pairs={{0,16},{1,5},{2,18},{3,7},{4,20},{5,9},{6,22},{7,11},{8,24},{9,13}... | collective-permute-start | bytes 1572872 | tf_op jit(solution)/shard_map/ppermute | solution.py:553
  41.7 14.4 %collective-permute-start.5 = (bf16[128,2048]{1,0:T(8,128)(2,1)}, bf16[128,2048]{1,0:T(8,128)(2,1)}, u32[]{:S(2)}, u32[]{:S(2)}) collective-permute-start(bf16[128,2048]{1,0:T(8,128)(2,1)} %get-tuple-element.71), channel_id=1, source_target_pairs={{0,48},{1,13},{2,50},{3,15},{4,52},{5,1},{6,54},{7,3},{8,56},{9,5}... | collective-permute-start | bytes 1572872 | tf_op jit(solution)/shard_map/ppermute | solution.py:553
  43.4 14.1 %collective-permute-start.6 = (bf16[128,2048]{1,0:T(8,128)(2,1)}, bf16[128,2048]{1,0:T(8,128)(2,1)}, u32[]{:S(2)}, u32[]{:S(2)}) collective-permute-start(bf16[128,2048]{1,0:T(8,128)(2,1)} %get-tuple-element.72), channel_id=1, source_target_pairs={{0,32},{1,9},{2,34},{3,11},{4,36},{5,13},{6,38},{7,15},{8,40},{9,1... | collective-permute-start | bytes 1572872 | tf_op jit(solution)/shard_map/ppermute | solution.py:553
  49.2 2.4 %collective-permute-start.3 = (bf16[144,1536]{1,0:T(8,128)(2,1)}, bf16[144,1536]{1,0:T(8,128)(2,1)}, u32[]{:S(2)}, u32[]{:S(2)}) collective-permute-start(bf16[144,1536]{1,0:T(8,128)(2,1)} %get-tuple-element.78.refs_5_.d_mix_hbm), channel_id=1, source_target_pairs={{0,1},{1,0},{2,3},{3,2},{4,5},{5,4},{6,7},{7,6},{8,9},{9,8},{10,11... | collective-permute-start | bytes 1327112 | tf_op jit(solution)/shard_map/ppermute | solution.py:581
  49.3 2.3 %collective-permute-start.2 = (bf16[144,512]{1,0:T(8,128)(2,1)}, bf16[144,512]{1,0:T(8,128)(2,1)}, u32[]{:S(2)}, u32[]{:S(2)}) collective-permute-start(bf16[144,512]{1,0:T(8,128)(2,1)} %get-tuple-element.64), channel_id=1, source_target_pairs={{0,1},{1,0},{2,3},{3,2},{4,5},{5,4},{6,7},{7,6},{8,9},{9,8},{10,11... | collective-permute-start | bytes 442376 | tf_op jit(solution)/shard_map/ppermute | solution.py:580
  57.5 13.2 %collective-permute-start.8 = (bf16[128,2048]{1,0:T(8,128)(2,1)}, bf16[128,2048]{1,0:T(8,128)(2,1)}, u32[]{:S(2)}, u32[]{:S(2)}) collective-permute-start(bf16[128,2048]{1,0:T(8,128)(2,1)} %get-tuple-element.75), channel_id=1, source_target_pairs={{0,16},{1,5},{2,18},{3,7},{4,20},{5,9},{6,22},{7,11},{8,24},{9,13}... | collective-permute-start | bytes 1572872 | tf_op jit(solution)/shard_map/ppermute | solution.py:553
  58.9 14.5 %collective-permute-start.9 = (bf16[128,2048]{1,0:T(8,128)(2,1)}, bf16[128,2048]{1,0:T(8,128)(2,1)}, u32[]{:S(2)}, u32[]{:S(2)}) collective-permute-start(bf16[128,2048]{1,0:T(8,128)(2,1)} %get-tuple-element.76), channel_id=1, source_target_pairs={{0,48},{1,13},{2,50},{3,15},{4,52},{5,1},{6,54},{7,3},{8,56},{9,5}... | collective-permute-start | bytes 1572872 | tf_op jit(solution)/shard_map/ppermute | solution.py:553
  60.7 13.6 %collective-permute-start.10 = (bf16[128,2048]{1,0:T(8,128)(2,1)}, bf16[128,2048]{1,0:T(8,128)(2,1)}, u32[]{:S(2)}, u32[]{:S(2)}) collective-permute-start(bf16[128,2048]{1,0:T(8,128)(2,1)} %get-tuple-element.77), channel_id=1, source_target_pairs={{0,32},{1,9},{2,34},{3,11},{4,36},{5,13},{6,38},{7,15},{8,40},{9,1... | collective-permute-start | bytes 1572872 | tf_op jit(solution)/shard_map/ppermute | solution.py:553
  64.8 5.9 %copy-start = (f32[4,1024]{1,0:T(4,128)S(1)}, f32[4,1024]{1,0:T(4,128)}, u32[]{:S(2)}) copy-start(f32[4,1024]{1,0:T(4,128)} %shard_map.133) | copy-start | bytes 49156
  64.8 5.9 %collective-permute-start.7 = (f32[4,1024]{1,0:T(4,128)}, f32[4,1024]{1,0:T(4,128)S(1)}, u32[]{:S(2)}, u32[]{:S(2)}) collective-permute-start(f32[4,1024]{1,0:T(4,128)} %shard_map.133), channel_id=1, source_target_pairs={{0,2},{2,0},{1,3},{3,1},{4,6},{6,4},{5,7},{7,5},{8,10},{10,8},{9,1... | collective-permute-start | bytes 49160 | tf_op jit(solution)/shard_map/ppermute | solution.py:607
  76.9 22.0 %all-to-all-start.2 = ((bf16[16,8,4096]{2,1,0:T(8,128)(2,1)}), bf16[16,8,4096]{2,1,0:T(8,128)(2,1)}, u32[]{:S(2)}, u32[]{:S(2)}) async-start(bf16[16,8,4096]{2,1,0:T(8,128)(2,1)} %bitcast.14), calls=%async_computation.2 | async-start | bytes 2097152 | tf_op jit(solution)/shard_map/all_to_all | solution.py:646
  84.2 1.3 %collective-permute-start.11 = (f32[4,1024]{1,0:T(4,128)S(1)}, f32[4,1024]{1,0:T(4,128)S(1)}, u32[]{:S(2)}, u32[]{:S(2)}) collective-permute-start(f32[4,1024]{1,0:T(4,128)S(1)} %add.31), channel_id=1, source_target_pairs={{0,1},{1,0},{2,3},{3,2},{4,5},{5,4},{6,7},{7,6},{8,9},{9,8},{10,11... | collective-permute-start | bytes 49160 | tf_op jit(solution)/shard_map/ppermute | solution.py:607
  85.5 8.9 %collective-permute-start.12 = (f32[4,1024]{1,0:T(4,128)S(1)}, f32[4,1024]{1,0:T(4,128)S(1)}, u32[]{:S(2)}, u32[]{:S(2)}) collective-permute-start(f32[4,1024]{1,0:T(4,128)S(1)} %add.33), channel_id=1, source_target_pairs={{0,12},{4,0},{8,4},{12,8},{1,13},{5,1},{9,5},{13,9},{2,14},{6,2},{... | collective-permute-start | bytes 49160 | tf_op jit(solution)/shard_map/ppermute | solution.py:625
  88.5 7.1 %collective-permute-start.13 = (f32[4,1024]{1,0:T(4,128)S(1)}, f32[4,1024]{1,0:T(4,128)S(1)}, u32[]{:S(2)}, u32[]{:S(2)}) collective-permute-start(f32[4,1024]{1,0:T(4,128)S(1)} %add.33), channel_id=1, source_target_pairs={{0,8},{4,12},{8,0},{12,4},{1,9},{5,13},{9,1},{13,5},{2,10},{6,14},... | collective-permute-start | bytes 49160 | tf_op jit(solution)/shard_map/ppermute | solution.py:625
  89.3 6.4 %collective-permute-start.14 = (f32[4,1024]{1,0:T(4,128)S(1)}, f32[4,1024]{1,0:T(4,128)S(1)}, u32[]{:S(2)}, u32[]{:S(2)}) collective-permute-start(f32[4,1024]{1,0:T(4,128)S(1)} %add.33), channel_id=1, source_target_pairs={{0,4},{4,8},{8,12},{12,0},{1,5},{5,9},{9,13},{13,1},{2,6},{6,10},{... | collective-permute-start | bytes 49160 | tf_op jit(solution)/shard_map/ppermute | solution.py:625

commit v8 on v7

--- a/solution.py
+++ b/solution.py
@@ -146,10 +146,10 @@
     first = [move.start(frames_hbm, frames), move.start(bottle_hbm, bottle)]
     columns = [slice(j * side, (j + 1) * side) for j in range(3)]
     entries = [move.spread(entry_hbm.at[:, c], entry.at[:, c]) for c in columns]
+    outs = []
+    finish(first)
     later = move.spread(exit_hbm, exit_)
     grads = move.start(grad_hbm, packed.at[:, width : 2 * width])
-    outs = []
-    finish(first)
     fill_tokens(tokens, frames, bottle)
     low = normalize(tokens[...])[0].astype(BF)
     for c, copy in zip(columns, entries):
@@ -207,10 +207,10 @@
     first = move.start(moved_hbm, moved)
     columns = [slice(j * side, (j + 1) * side) for j in range(3)]
     entries = [move.spread(entry_hbm.at[:, c], entry.at[:, c]) for c in columns]
-    later = move.spread(exit_hbm, exit_)
     core = core_ref[0]
     other, own = picker(1 - core), picker(core)
     first.wait()
+    later = move.spread(exit_hbm, exit_)
     cot = moved[:, width : 2 * width]
     normed, inverse = normalize(moved[:, 0:width].astype(F32))
     low = normed.astype(BF)
@@ -370,9 +370,9 @@
     finish(ready[0] + ready[1])
     put(3 * side, mm(left_c[...], right_a[...], TN).astype(BF))
     finish(ready[2] + ready[3])
-    product = mm(left_n[...], right_m[...], TN).astype(BF)
+    turned = left_n[...].T
     for j in range(3):
-        put(j * side, product[:, j * side : (j + 1) * side])
+        put(j * side, mm(turned, right_m[:, j * side : (j + 1) * side], NN).astype(BF))
     finish(outs)
 
 

time: 102 us -> 102 us (level)
  no operation moved by 1% of the time
where the time goes in v8:
time: 102 us; the launch traced here: 101 us
  Pallas kernels  39.7 us (39%)
  starting transfers between devices  37.6 us (37%)
  waiting for transfers between devices  21.6 us (21%)
  other arithmetic  1.22 us (1%)
    pallas_call x11, Pallas kernels, call(): pl.pallas_call(kernel, out_shape=tuple((jax.ShapeDtypeStruct(s, d) for s,...  39.7 us
    all_to_all x2, starting transfers between devices, exchange(): return lax.all_to_all(blocks, FRAME, 0, 0, tiled=True).reshape(array.shape)  12.2 us
    ppermute x6, starting transfers between devices, passed_on(): lax.ppermute(parts[k], ALL, first_pairs(shape, k))  8.85 us
    all_to_all x2, waiting for transfers between devices, exchange(): return lax.all_to_all(blocks, FRAME, 0, 0, tiled=True).reshape(array.shape)  8.06 us
    all_to_all x1, starting transfers between devices, per_device(): lax.all_to_all(both.reshape(count, -1, 8 * side), ALL, 0, 0, axis_index_g...  7.3 us
    ppermute x6, waiting for transfers between devices, passed_on(): lax.ppermute(parts[k], ALL, first_pairs(shape, k))  5.02 us
    ppermute x3, starting transfers between devices, per_device(): lax.ppermute(local, 'y', [(i, (i + k) % ys) for i in range(ys)])  4.72 us
    ppermute x2, starting transfers between devices, with_partner(): return local + lax.ppermute(local, axis, pairs)  3.41 us
  transfers between devices with their start and end apart: 18, of which 10 were waited for; matrix products, arithmetic and copies ran while one was open for 1% of the time, Pallas kernels for 25%

profile of v8, /device:TPU:0, one launch (start us, length us, event | category | flops | bytes accessed | tf_op | source)
XLA Modules:
  0.0 101.1 jit_solution(17127518198299199207)
XLA Ops:
  0.6 4.6 %shard_map.127 = (bf16[128,2048]{1,0:T(8,128)(2,1)}, bf16[144,1536]{1,0:T(8,128)(2,1)}, f32[8,144,144]{2,1,0:T(8,128)}, bf16[144,512]{1,0:T(8,128)(2,1)}) custom-call(bf16[128,1024]{1,0:T(8,128)(2,1)} %bitcast.15, bf16[4,1024]{1,0:T(4,128)(2,1)} %bitcast.22, bf16[1024,1536]{1,0:T(8,128)(2,1)} %entry_hbm.7, bf16[1024,512]{1,0:T(8,128)(2,1)} %exit_hbm.5, ...), custom_call_target="tpu_custom_call" | custom-call | flops 1000 | bytes 1000 | tf_op jit(solution)/shard_map/pallas_call | solution.py:432
  5.2 8.0 %all-to-all-start = ((bf16[16,8,2048]{2,1,0:T(8,128)(2,1)}), bf16[16,8,2048]{2,1,0:T(8,128)(2,1)}, u32[]{:S(2)}, u32[]{:S(2)}) async-start(bf16[16,8,2048]{2,1,0:T(8,128)(2,1)} %bitcast.18), calls=%async_computation | async-start | bytes 1048576 | tf_op jit(solution)/shard_map/all_to_all | solution.py:486
  13.3 2.3 %shard_map.128 = (bf16[144,1024]{1,0:T(8,128)(2,1)}, bf16[144,512]{1,0:T(8,128)(2,1)}) custom-call(s32[1]{0:T(128)} %bitcast.1.core_ref, bf16[128,1024]{1,0:T(8,128)(2,1)} %bitcast.16, bf16[4,1024]{1,0:T(4,128)(2,1)} %bitcast.23, bf16[144,512]{1,0:T(8,128)(2,1)} %get-tuple-element.50.att_hbm), custom_call_target="tpu_custom_call" | custom-call | flops 1000 | bytes 1000 | tf_op jit(solution)/shard_map/pallas_call | solution.py:432
  15.6 0.4 collective-permute-start
  16.0 1.6 %collective-permute-done.refs_2_ = bf16[144,1024]{1,0:T(8,128)(2,1)} collective-permute-done((bf16[144,1024]{1,0:T(8,128)(2,1)}, bf16[144,1024]{1,0:T(8,128)(2,1)}, u32[]{:S(2)}, u32[]{:S(2)}) %collective-permute-start) | collective-permute-done | bytes 294944 | tf_op jit(solution)/shard_map/ppermute | solution.py:517
  17.6 8.1 %all-to-all-done = bf16[16,8,2048]{2,1,0:T(8,128)(2,1)} async-done(((bf16[16,8,2048]{2,1,0:T(8,128)(2,1)}), bf16[16,8,2048]{2,1,0:T(8,128)(2,1)}, u32[]{:S(2)}, u32[]{:S(2)}) %all-to-all-start) | async-done | bytes 524320 | tf_op jit(solution)/shard_map/all_to_all | solution.py:486
  25.7 5.6 %shard_map.129 = (bf16[128,1024]{1,0:T(8,128)(2,1)}, bf16[128,3072]{1,0:T(8,128)(2,1)}, bf16[128,1024]{1,0:T(8,128)(2,1)}) custom-call(s32[1]{0:T(128)} %bitcast.1.core_ref, bf16[128,2048]{1,0:T(8,128)(2,1)} %bitcast.5.moved_hbm, bf16[1024,1536]{1,0:T(8,128)(2,1)} %entry_hbm.5, bf16[1024,512]{1,0:T(8,128)(2,1)} %exit_hbm.4), custom_call_target="tpu_custom_call" | custom-call | flops 1000 | bytes 1000 | tf_op jit(solution)/shard_map/pallas_call | solution.py:432
  31.3 0.1 collective-permute-start.1
  31.4 4.2 %all-to-all-start.1 = ((bf16[16,8,1024]{2,1,0:T(8,128)(2,1)}), bf16[16,8,1024]{2,1,0:T(8,128)(2,1)}, u32[]{:S(2)}, u32[]{:S(2)}) async-start(bf16[16,8,1024]{2,1,0:T(8,128)(2,1)} %bitcast.21), calls=%async_computation.1 | async-start | bytes 524288 | tf_op jit(solution)/shard_map/all_to_all | solution.py:486
  35.6 0.6 pad_add_fusion.place_ref
  36.2 0.0 collective-permute-done.1.refs_2_
  36.2 3.9 %shard_map.130 = (bf16[128,2048]{1,0:T(8,128)(2,1)}, bf16[128,2048]{1,0:T(8,128)(2,1)}, bf16[128,2048]{1,0:T(8,128)(2,1)}, bf16[128,2048]{1,0:T(8,128)(2,1)}) custom-call(s32[2]{0:T(128)} %pad_add_fusion.place_ref, bf16[128,1024]{1,0:T(8,128)(2,1)} %get-tuple-element.54.refs_0_, bf16[128,3072]{1,0:T(8,128)(2,1)} %get-tuple-element.55.refs_1_, ...), custom_call_target="tpu_custom_call" | custom-call | flops 1000 | bytes 1000 | tf_op jit(solution)/shard_map/pallas_call | solution.py:432
  40.1 1.5 %collective-permute-start.4 = (bf16[128,2048]{1,0:T(8,128)(2,1)}, bf16[128,2048]{1,0:T(8,128)(2,1)}, u32[]{:S(2)}, u32[]{:S(2)}) collective-permute-start(bf16[128,2048]{1,0:T(8,128)(2,1)} %get-tuple-element.70), channel_id=1, source_target_pairs={{0,16},{1,5},{2,18},{3,7},{4,20},{5,9},{6,22},{7,11},{8,24},{9,13}... | collective-permute-start | bytes 1572872 | tf_op jit(solution)/shard_map/ppermute | solution.py:553
  41.7 1.8 %collective-permute-start.5 = (bf16[128,2048]{1,0:T(8,128)(2,1)}, bf16[128,2048]{1,0:T(8,128)(2,1)}, u32[]{:S(2)}, u32[]{:S(2)}) collective-permute-start(bf16[128,2048]{1,0:T(8,128)(2,1)} %get-tuple-element.71), channel_id=1, source_target_pairs={{0,48},{1,13},{2,50},{3,15},{4,52},{5,1},{6,54},{7,3},{8,56},{9,5}... | collective-permute-start | bytes 1572872 | tf_op jit(solution)/shard_map/ppermute | solution.py:553
  43.4 1.8 %collective-permute-start.6 = (bf16[128,2048]{1,0:T(8,128)(2,1)}, bf16[128,2048]{1,0:T(8,128)(2,1)}, u32[]{:S(2)}, u32[]{:S(2)}) collective-permute-start(bf16[128,2048]{1,0:T(8,128)(2,1)} %get-tuple-element.72), channel_id=1, source_target_pairs={{0,32},{1,9},{2,34},{3,11},{4,36},{5,13},{6,38},{7,15},{8,40},{9,1... | collective-permute-start | bytes 1572872 | tf_op jit(solution)/shard_map/ppermute | solution.py:553
  45.2 0.0 all-to-all-done.1
  45.2 4.0 %shard_map.131 = (bf16[144,512]{1,0:T(8,128)(2,1)}, bf16[144,512]{1,0:T(8,128)(2,1)}, bf16[144,1536]{1,0:T(8,128)(2,1)}) custom-call(s32[1]{0:T(128)} %bitcast.1.core_ref, bf16[128,1024]{1,0:T(8,128)(2,1)} %bitcast.7.back_hbm, bf16[4,1024]{1,0:T(4,128)(2,1)} %bitcast.25, bf16[144,1536]{1,0:T(8,128)(2,1)} %get-tuple-element.58.mix_hbm, ...), custom_call_target="tpu_custom_call" | custom-call | flops 1000 | bytes 1000 | tf_op jit(solution)/shard_map/pallas_call | solution.py:432
  49.2 0.1 collective-permute-start.3
  49.3 0.5 collective-permute-start.2
  49.8 1.8 %collective-permute-done.2.refs_4_ = bf16[144,512]{1,0:T(8,128)(2,1)} collective-permute-done((bf16[144,512]{1,0:T(8,128)(2,1)}, bf16[144,512]{1,0:T(8,128)(2,1)}, u32[]{:S(2)}, u32[]{:S(2)}) %collective-permute-start.2) | collective-permute-done | bytes 147488 | tf_op jit(solution)/shard_map/ppermute | solution.py:580
  51.7 0.0 collective-permute-done.3.refs_6_
  51.7 4.4 %shard_map.132 = (bf16[128,2048]{1,0:T(8,128)(2,1)}, bf16[128,2048]{1,0:T(8,128)(2,1)}, bf16[128,2048]{1,0:T(8,128)(2,1)}, bf16[128,2048]{1,0:T(8,128)(2,1)}) custom-call(s32[2]{0:T(128)} %pad_add_fusion.place_ref, bf16[144,512]{1,0:T(8,128)(2,1)} %get-tuple-element.61.refs_0_, bf16[144,1024]{1,0:T(8,128)(2,1)} %get-tuple-element.51.refs_1_, ...), custom_call_target="tpu_custom_call" | custom-call | flops 1000 | bytes 1000 | tf_op jit(solution)/shard_map/pallas_call | solution.py:432
  56.0 0.0 collective-permute-done.4.a_hbm
  56.0 0.1 collective-permute-done.5.b_hbm
  56.1 1.4 %collective-permute-done.6.c_hbm = bf16[128,2048]{1,0:T(8,128)(2,1)} collective-permute-done((bf16[128,2048]{1,0:T(8,128)(2,1)}, bf16[128,2048]{1,0:T(8,128)(2,1)}, u32[]{:S(2)}, u32[]{:S(2)}) %collective-permute-start.6) | collective-permute-done | bytes 524320 | tf_op jit(solution)/shard_map/ppermute | solution.py:553
  57.5 1.4 %collective-permute-start.8 = (bf16[128,2048]{1,0:T(8,128)(2,1)}, bf16[128,2048]{1,0:T(8,128)(2,1)}, u32[]{:S(2)}, u32[]{:S(2)}) collective-permute-start(bf16[128,2048]{1,0:T(8,128)(2,1)} %get-tuple-element.75), channel_id=1, source_target_pairs={{0,16},{1,5},{2,18},{3,7},{4,20},{5,9},{6,22},{7,11},{8,24},{9,13}... | collective-permute-start | bytes 1572872 | tf_op jit(solution)/shard_map/ppermute | solution.py:553
  58.9 1.8 %collective-permute-start.9 = (bf16[128,2048]{1,0:T(8,128)(2,1)}, bf16[128,2048]{1,0:T(8,128)(2,1)}, u32[]{:S(2)}, u32[]{:S(2)}) collective-permute-start(bf16[128,2048]{1,0:T(8,128)(2,1)} %get-tuple-element.76), channel_id=1, source_target_pairs={{0,48},{1,13},{2,50},{3,15},{4,52},{5,1},{6,54},{7,3},{8,56},{9,5}... | collective-permute-start | bytes 1572872 | tf_op jit(solution)/shard_map/ppermute | solution.py:553
  60.7 0.5 collective-permute-start.10
  61.2 3.6 %shard_map.133 = f32[4,1024]{1,0:T(4,128)} custom-call(bf16[4,1024]{1,0:T(4,128)(2,1)} %bitcast.24, bf16[4,1024]{1,0:T(4,128)(2,1)} %bitcast.26, bf16[144,1536]{1,0:T(8,128)(2,1)} %get-tuple-element.78.refs_5_.d_mix_hbm, bf16[1024,1536]{1,0:T(8,128)(2,1)} %entry_hbm.7), custom_call_target="tpu_custom_call" | custom-call | flops 1000 | bytes 1000 | tf_op jit(solution)/shard_map/pallas_call | solution.py:432
  64.8 0.0 copy-start
  64.8 3.3 %collective-permute-start.7 = (f32[4,1024]{1,0:T(4,128)}, f32[4,1024]{1,0:T(4,128)S(1)}, u32[]{:S(2)}, u32[]{:S(2)}) collective-permute-start(f32[4,1024]{1,0:T(4,128)} %shard_map.133), channel_id=1, source_target_pairs={{0,2},{2,0},{1,3},{3,1},{4,6},{6,4},{5,7},{7,5},{8,10},{10,8},{9,1... | collective-permute-start | bytes 49160 | tf_op jit(solution)/shard_map/ppermute | solution.py:607
  68.1 2.5 %shard_map.135.refs_0_ = bf16[128,4096]{1,0:T(8,128)(2,1)} custom-call(bf16[128,2048]{1,0:T(8,128)(2,1)} %get-tuple-element.84.own_hbm, bf16[128,2048]{1,0:T(8,128)(2,1)} %collective-permute-done.4.a_hbm, bf16[128,2048]{1,0:T(8,128)(2,1)} %collective-permute-done.5.b_hbm, bf16[128,2048]{1,0:T(8,128)(2,1)} %collective-permute-done.6.c_hbm), custom_call_target="tpu_custom_call" | custom-call | flops 1000 | bytes 1000 | tf_op jit(solution)/shard_map/pallas_call | solution.py:432
  70.7 0.0 collective-permute-done.7
  70.7 0.0 copy-done
  70.7 0.0 collective-permute-done.8.a_hbm
  70.7 2.7 %collective-permute-done.9.b_hbm = bf16[128,2048]{1,0:T(8,128)(2,1)} collective-permute-done((bf16[128,2048]{1,0:T(8,128)(2,1)}, bf16[128,2048]{1,0:T(8,128)(2,1)}, u32[]{:S(2)}, u32[]{:S(2)}) %collective-permute-start.9) | collective-permute-done | bytes 524320 | tf_op jit(solution)/shard_map/ppermute | solution.py:553
  73.4 0.9 collective-permute-done.10.c_hbm
  74.3 2.6 %shard_map.136 = bf16[128,4096]{1,0:T(8,128)(2,1)} custom-call(bf16[128,2048]{1,0:T(8,128)(2,1)} %get-tuple-element.80.own_hbm, bf16[128,2048]{1,0:T(8,128)(2,1)} %collective-permute-done.8.a_hbm, bf16[128,2048]{1,0:T(8,128)(2,1)} %collective-permute-done.9.b_hbm, bf16[128,2048]{1,0:T(8,128)(2,1)} %collective-permute-done.10.c_hbm, ...), custom_call_target="tpu_custom_call", output_to_operand_aliasing={{}: (4, {})} | custom-call | flops 1000 | bytes 1000 | tf_op jit(solution)/shard_map/pallas_call | solution.py:432
  76.9 7.3 %all-to-all-start.2 = ((bf16[16,8,4096]{2,1,0:T(8,128)(2,1)}), bf16[16,8,4096]{2,1,0:T(8,128)(2,1)}, u32[]{:S(2)}, u32[]{:S(2)}) async-start(bf16[16,8,4096]{2,1,0:T(8,128)(2,1)} %bitcast.14), calls=%async_computation.2 | async-start | bytes 2097152 | tf_op jit(solution)/shard_map/all_to_all | solution.py:646
  84.2 0.1 collective-permute-start.11
  84.3 1.2 %collective-permute-done.11 = f32[4,1024]{1,0:T(4,128)S(1)} collective-permute-done((f32[4,1024]{1,0:T(4,128)S(1)}, f32[4,1024]{1,0:T(4,128)S(1)}, u32[]{:S(2)}, u32[]{:S(2)}) %collective-permute-start.11) | collective-permute-done | bytes 16416 | tf_op jit(solution)/shard_map/ppermute | solution.py:607
  85.5 3.0 %collective-permute-start.12 = (f32[4,1024]{1,0:T(4,128)S(1)}, f32[4,1024]{1,0:T(4,128)S(1)}, u32[]{:S(2)}, u32[]{:S(2)}) collective-permute-start(f32[4,1024]{1,0:T(4,128)S(1)} %add.33), channel_id=1, source_target_pairs={{0,12},{4,0},{8,4},{12,8},{1,13},{5,1},{9,5},{13,9},{2,14},{6,2},{... | collective-permute-start | bytes 49160 | tf_op jit(solution)/shard_map/ppermute | solution.py:625
  88.5 0.9 collective-permute-start.13
  89.3 0.9 collective-permute-start.14
  90.2 4.2 %shard_map.134 = bf16[128,1024]{1,0:T(8,128)(2,1)} custom-call(bf16[128,1024]{1,0:T(8,128)(2,1)} %bitcast.17, bf16[128,1024]{1,0:T(8,128)(2,1)} %bitcast.7.back_hbm, bf16[144,1536]{1,0:T(8,128)(2,1)} %get-tuple-element.78.refs_5_.d_mix_hbm, bf16[1024,1536]{1,0:T(8,128)(2,1)} %entry_hbm.7), custom_call_target="tpu_custom_call" | custom-call | flops 1000 | bytes 1000 | tf_op jit(solution)/shard_map/pallas_call | solution.py:432
  94.4 0.0 collective-permute-done.12
  94.4 1.2 %collective-permute-done.13 = f32[4,1024]{1,0:T(4,128)S(1)} collective-permute-done((f32[4,1024]{1,0:T(4,128)S(1)}, f32[4,1024]{1,0:T(4,128)S(1)}, u32[]{:S(2)}, u32[]{:S(2)}) %collective-permute-start.13) | collective-permute-done | bytes 16416 | tf_op jit(solution)/shard_map/ppermute | solution.py:625
  95.6 0.1 collective-permute-done.14
  95.7 0.6 fusion
  96.3 2.6 %all-to-all-done.2.parts_hbm = bf16[16,8,4096]{2,1,0:T(8,128)(2,1)} async-done(((bf16[16,8,4096]{2,1,0:T(8,128)(2,1)}), bf16[16,8,4096]{2,1,0:T(8,128)(2,1)}, u32[]{:S(2)}, u32[]{:S(2)}) %all-to-all-start.2) | async-done | bytes 1048608 | tf_op jit(solution)/shard_map/all_to_all | solution.py:646
  98.9 2.0 %shard_map.137 = (bf16[8,1536]{1,0:T(8,128)(2,1)}, bf16[8,512]{1,0:T(8,128)(2,1)}, bf16[8,1536]{1,0:T(8,128)(2,1)}, bf16[8,512]{1,0:T(8,128)(2,1)}) custom-call(bf16[16,8,4096]{2,1,0:T(8,128)(2,1)} %all-to-all-done.2.parts_hbm), custom_call_target="tpu_custom_call" | custom-call | flops 1000 | bytes 1000 | tf_op jit(solution)/shard_map/pallas_call | solution.py:432
  (2 shorter events, 0.0 us)
Async XLA Ops:
  5.2 20.5 %all-to-all-start = ((bf16[16,8,2048]{2,1,0:T(8,128)(2,1)}), bf16[16,8,2048]{2,1,0:T(8,128)(2,1)}, u32[]{:S(2)}, u32[]{:S(2)}) async-start(bf16[16,8,2048]{2,1,0:T(8,128)(2,1)} %bitcast.18), calls=%async_computation | async-start | bytes 1048576 | tf_op jit(solution)/shard_map/all_to_all | solution.py:486
  15.6 2.0 %collective-permute-start = (bf16[144,1024]{1,0:T(8,128)(2,1)}, bf16[144,1024]{1,0:T(8,128)(2,1)}, u32[]{:S(2)}, u32[]{:S(2)}) collective-permute-start(bf16[144,1024]{1,0:T(8,128)(2,1)} %get-tuple-element.51.refs_1_), channel_id=1, source_target_pairs={{0,1},{1,0},{2,3},{3,2},{4,5},{5,4},{6,7},{7,6},{8,9},{9,8},{10,11... | collective-permute-start | bytes 884744 | tf_op jit(solution)/shard_map/ppermute | solution.py:517
  31.3 4.9 %collective-permute-start.1 = (bf16[128,3072]{1,0:T(8,128)(2,1)}, bf16[128,3072]{1,0:T(8,128)(2,1)}, u32[]{:S(2)}, u32[]{:S(2)}) collective-permute-start(bf16[128,3072]{1,0:T(8,128)(2,1)} %get-tuple-element.55.refs_1_), channel_id=1, source_target_pairs={{0,1},{1,0},{2,3},{3,2},{4,5},{5,4},{6,7},{7,6},{8,9},{9,8},{10,11... | collective-permute-start | bytes 2359304 | tf_op jit(solution)/shard_map/ppermute | solution.py:535
  31.4 13.8 %all-to-all-start.1 = ((bf16[16,8,1024]{2,1,0:T(8,128)(2,1)}), bf16[16,8,1024]{2,1,0:T(8,128)(2,1)}, u32[]{:S(2)}, u32[]{:S(2)}) async-start(bf16[16,8,1024]{2,1,0:T(8,128)(2,1)} %bitcast.21), calls=%async_computation.1 | async-start | bytes 524288 | tf_op jit(solution)/shard_map/all_to_all | solution.py:486
  40.1 15.9 %collective-permute-start.4 = (bf16[128,2048]{1,0:T(8,128)(2,1)}, bf16[128,2048]{1,0:T(8,128)(2,1)}, u32[]{:S(2)}, u32[]{:S(2)}) collective-permute-start(bf16[128,2048]{1,0:T(8,128)(2,1)} %get-tuple-element.70), channel_id=1, source_target_pairs={{0,16},{1,5},{2,18},{3,7},{4,20},{5,9},{6,22},{7,11},{8,24},{9,13}... | collective-permute-start | bytes 1572872 | tf_op jit(solution)/shard_map/ppermute | solution.py:553
  41.7 14.4 %collective-permute-start.5 = (bf16[128,2048]{1,0:T(8,128)(2,1)}, bf16[128,2048]{1,0:T(8,128)(2,1)}, u32[]{:S(2)}, u32[]{:S(2)}) collective-permute-start(bf16[128,2048]{1,0:T(8,128)(2,1)} %get-tuple-element.71), channel_id=1, source_target_pairs={{0,48},{1,13},{2,50},{3,15},{4,52},{5,1},{6,54},{7,3},{8,56},{9,5}... | collective-permute-start | bytes 1572872 | tf_op jit(solution)/shard_map/ppermute | solution.py:553
  43.4 14.0 %collective-permute-start.6 = (bf16[128,2048]{1,0:T(8,128)(2,1)}, bf16[128,2048]{1,0:T(8,128)(2,1)}, u32[]{:S(2)}, u32[]{:S(2)}) collective-permute-start(bf16[128,2048]{1,0:T(8,128)(2,1)} %get-tuple-element.72), channel_id=1, source_target_pairs={{0,32},{1,9},{2,34},{3,11},{4,36},{5,13},{6,38},{7,15},{8,40},{9,1... | collective-permute-start | bytes 1572872 | tf_op jit(solution)/shard_map/ppermute | solution.py:553
  49.2 2.4 %collective-permute-start.3 = (bf16[144,1536]{1,0:T(8,128)(2,1)}, bf16[144,1536]{1,0:T(8,128)(2,1)}, u32[]{:S(2)}, u32[]{:S(2)}) collective-permute-start(bf16[144,1536]{1,0:T(8,128)(2,1)} %get-tuple-element.78.refs_5_.d_mix_hbm), channel_id=1, source_target_pairs={{0,1},{1,0},{2,3},{3,2},{4,5},{5,4},{6,7},{7,6},{8,9},{9,8},{10,11... | collective-permute-start | bytes 1327112 | tf_op jit(solution)/shard_map/ppermute | solution.py:581
  49.3 2.3 %collective-permute-start.2 = (bf16[144,512]{1,0:T(8,128)(2,1)}, bf16[144,512]{1,0:T(8,128)(2,1)}, u32[]{:S(2)}, u32[]{:S(2)}) collective-permute-start(bf16[144,512]{1,0:T(8,128)(2,1)} %get-tuple-element.64), channel_id=1, source_target_pairs={{0,1},{1,0},{2,3},{3,2},{4,5},{5,4},{6,7},{7,6},{8,9},{9,8},{10,11... | collective-permute-start | bytes 442376 | tf_op jit(solution)/shard_map/ppermute | solution.py:580
  57.5 13.2 %collective-permute-start.8 = (bf16[128,2048]{1,0:T(8,128)(2,1)}, bf16[128,2048]{1,0:T(8,128)(2,1)}, u32[]{:S(2)}, u32[]{:S(2)}) collective-permute-start(bf16[128,2048]{1,0:T(8,128)(2,1)} %get-tuple-element.75), channel_id=1, source_target_pairs={{0,16},{1,5},{2,18},{3,7},{4,20},{5,9},{6,22},{7,11},{8,24},{9,13}... | collective-permute-start | bytes 1572872 | tf_op jit(solution)/shard_map/ppermute | solution.py:553
  58.9 14.5 %collective-permute-start.9 = (bf16[128,2048]{1,0:T(8,128)(2,1)}, bf16[128,2048]{1,0:T(8,128)(2,1)}, u32[]{:S(2)}, u32[]{:S(2)}) collective-permute-start(bf16[128,2048]{1,0:T(8,128)(2,1)} %get-tuple-element.76), channel_id=1, source_target_pairs={{0,48},{1,13},{2,50},{3,15},{4,52},{5,1},{6,54},{7,3},{8,56},{9,5}... | collective-permute-start | bytes 1572872 | tf_op jit(solution)/shard_map/ppermute | solution.py:553
  60.7 13.6 %collective-permute-start.10 = (bf16[128,2048]{1,0:T(8,128)(2,1)}, bf16[128,2048]{1,0:T(8,128)(2,1)}, u32[]{:S(2)}, u32[]{:S(2)}) collective-permute-start(bf16[128,2048]{1,0:T(8,128)(2,1)} %get-tuple-element.77), channel_id=1, source_target_pairs={{0,32},{1,9},{2,34},{3,11},{4,36},{5,13},{6,38},{7,15},{8,40},{9,1... | collective-permute-start | bytes 1572872 | tf_op jit(solution)/shard_map/ppermute | solution.py:553
  64.8 5.9 %copy-start = (f32[4,1024]{1,0:T(4,128)S(1)}, f32[4,1024]{1,0:T(4,128)}, u32[]{:S(2)}) copy-start(f32[4,1024]{1,0:T(4,128)} %shard_map.133) | copy-start | bytes 49156
  64.8 5.9 %collective-permute-start.7 = (f32[4,1024]{1,0:T(4,128)}, f32[4,1024]{1,0:T(4,128)S(1)}, u32[]{:S(2)}, u32[]{:S(2)}) collective-permute-start(f32[4,1024]{1,0:T(4,128)} %shard_map.133), channel_id=1, source_target_pairs={{0,2},{2,0},{1,3},{3,1},{4,6},{6,4},{5,7},{7,5},{8,10},{10,8},{9,1... | collective-permute-start | bytes 49160 | tf_op jit(solution)/shard_map/ppermute | solution.py:607
  76.9 22.0 %all-to-all-start.2 = ((bf16[16,8,4096]{2,1,0:T(8,128)(2,1)}), bf16[16,8,4096]{2,1,0:T(8,128)(2,1)}, u32[]{:S(2)}, u32[]{:S(2)}) async-start(bf16[16,8,4096]{2,1,0:T(8,128)(2,1)} %bitcast.14), calls=%async_computation.2 | async-start | bytes 2097152 | tf_op jit(solution)/shard_map/all_to_all | solution.py:646
  84.2 1.3 %collective-permute-start.11 = (f32[4,1024]{1,0:T(4,128)S(1)}, f32[4,1024]{1,0:T(4,128)S(1)}, u32[]{:S(2)}, u32[]{:S(2)}) collective-permute-start(f32[4,1024]{1,0:T(4,128)S(1)} %add.31), channel_id=1, source_target_pairs={{0,1},{1,0},{2,3},{3,2},{4,5},{5,4},{6,7},{7,6},{8,9},{9,8},{10,11... | collective-permute-start | bytes 49160 | tf_op jit(solution)/shard_map/ppermute | solution.py:607
  85.5 8.9 %collective-permute-start.12 = (f32[4,1024]{1,0:T(4,128)S(1)}, f32[4,1024]{1,0:T(4,128)S(1)}, u32[]{:S(2)}, u32[]{:S(2)}) collective-permute-start(f32[4,1024]{1,0:T(4,128)S(1)} %add.33), channel_id=1, source_target_pairs={{0,12},{4,0},{8,4},{12,8},{1,13},{5,1},{9,5},{13,9},{2,14},{6,2},{... | collective-permute-start | bytes 49160 | tf_op jit(solution)/shard_map/ppermute | solution.py:625
  88.5 7.1 %collective-permute-start.13 = (f32[4,1024]{1,0:T(4,128)S(1)}, f32[4,1024]{1,0:T(4,128)S(1)}, u32[]{:S(2)}, u32[]{:S(2)}) collective-permute-start(f32[4,1024]{1,0:T(4,128)S(1)} %add.33), channel_id=1, source_target_pairs={{0,8},{4,12},{8,0},{12,4},{1,9},{5,13},{9,1},{13,5},{2,10},{6,14},... | collective-permute-start | bytes 49160 | tf_op jit(solution)/shard_map/ppermute | solution.py:625
  89.3 6.4 %collective-permute-start.14 = (f32[4,1024]{1,0:T(4,128)S(1)}, f32[4,1024]{1,0:T(4,128)S(1)}, u32[]{:S(2)}, u32[]{:S(2)}) collective-permute-start(f32[4,1024]{1,0:T(4,128)S(1)} %add.33), channel_id=1, source_target_pairs={{0,4},{4,8},{8,12},{12,0},{1,5},{5,9},{9,13},{13,1},{2,6},{6,10},{... | collective-permute-start | bytes 49160 | tf_op jit(solution)/shard_map/ppermute | solution.py:625

commit v9 on v8

--- a/solution.py
+++ b/solution.py
@@ -376,27 +376,23 @@
     finish(outs)
 
 
-def add_four(parts, columns):
-    total = parts[0, :, columns].astype(F32)
-    for k in range(1, 4):
-        total = total + parts[k, :, columns].astype(F32)
-    return total.astype(BF)
-
-
 def four_sum_kernel(right, own_hbm, a_hbm, b_hbm, c_hbm, *refs):
     out_hbm, parts, out, sems = refs[-4:]
     move = Mover(sems)
     sources = (own_hbm, a_hbm, b_hbm, c_hbm)
-    width = out.shape[1]
-    step = width // 4
-    columns = [slice(j * step, (j + 1) * step) for j in range(4)]
-    copies = [[move.start(r.at[:, c], parts.at[k, :, c]) for k, r in enumerate(sources)] for c in columns]
+    count, width = out.shape
+    step = count // 4
+    rows = [slice(j * step, (j + 1) * step) for j in range(4)]
+    copies = [[move.start(s.at[r, :], parts.at[k, r, :]) for k, s in enumerate(sources)] for r in rows]
+    at = width if right else 0
     outs = []
-    for c, ready in zip(columns, copies):
+    for r, ready in zip(rows, copies):
         finish(ready)
-        out[:, c] = add_four(parts, c)
-        at = c.start + (width if right else 0)
-        outs.append(move.start(out.at[:, c], out_hbm.at[:, at : at + step]))
+        total = parts[0, r, :].astype(F32)
+        for k in range(1, 4):
+            total = total + parts[k, r, :].astype(F32)
+        out[r, :] = total.astype(BF)
+        outs.append(move.start(out.at[r, :], out_hbm.at[r, at : at + width]))
     finish(outs)
 
 

time: 102 us -> 102 us (level)
  no operation moved by 1% of the time
where the time goes in v9:
time: 102 us; the launch traced here: 101 us
  Pallas kernels  39.6 us (39%)
  starting transfers between devices  37.6 us (37%)
  waiting for transfers between devices  21.6 us (21%)
  other arithmetic  1.22 us (1%)
    pallas_call x11, Pallas kernels, call(): pl.pallas_call(kernel, out_shape=tuple((jax.ShapeDtypeStruct(s, d) for s,...  39.6 us
    all_to_all x2, starting transfers between devices, exchange(): return lax.all_to_all(blocks, FRAME, 0, 0, tiled=True).reshape(array.shape)  12.2 us
    ppermute x6, starting transfers between devices, passed_on(): lax.ppermute(parts[k], ALL, first_pairs(shape, k))  8.85 us
    all_to_all x2, waiting for transfers between devices, exchange(): return lax.all_to_all(blocks, FRAME, 0, 0, tiled=True).reshape(array.shape)  8.06 us
    all_to_all x1, starting transfers between devices, per_device(): lax.all_to_all(both.reshape(count, -1, 8 * side), ALL, 0, 0, axis_index_g...  7.3 us
    ppermute x6, waiting for transfers between devices, passed_on(): lax.ppermute(parts[k], ALL, first_pairs(shape, k))  5.03 us
    ppermute x3, starting transfers between devices, per_device(): lax.ppermute(local, 'y', [(i, (i + k) % ys) for i in range(ys)])  4.72 us
    ppermute x2, starting transfers between devices, with_partner(): return local + lax.ppermute(local, axis, pairs)  3.41 us
  transfers between devices with their start and end apart: 18, of which 10 were waited for; matrix products, arithmetic and copies ran while one was open for 1% of the time, Pallas kernels for 25%

profile of v9, /device:TPU:0, one launch (start us, length us, event | category | flops | bytes accessed | tf_op | source)
XLA Modules:
  0.0 101.1 jit_solution(9889667452567953158)
XLA Ops:
  0.6 4.6 %shard_map.127 = (bf16[128,2048]{1,0:T(8,128)(2,1)}, bf16[144,1536]{1,0:T(8,128)(2,1)}, f32[8,144,144]{2,1,0:T(8,128)}, bf16[144,512]{1,0:T(8,128)(2,1)}) custom-call(bf16[128,1024]{1,0:T(8,128)(2,1)} %bitcast.15, bf16[4,1024]{1,0:T(4,128)(2,1)} %bitcast.22, bf16[1024,1536]{1,0:T(8,128)(2,1)} %entry_hbm.7, bf16[1024,512]{1,0:T(8,128)(2,1)} %exit_hbm.5, ...), custom_call_target="tpu_custom_call" | custom-call | flops 1000 | bytes 1000 | tf_op jit(solution)/shard_map/pallas_call | solution.py:428
  5.2 8.0 %all-to-all-start = ((bf16[16,8,2048]{2,1,0:T(8,128)(2,1)}), bf16[16,8,2048]{2,1,0:T(8,128)(2,1)}, u32[]{:S(2)}, u32[]{:S(2)}) async-start(bf16[16,8,2048]{2,1,0:T(8,128)(2,1)} %bitcast.18), calls=%async_computation | async-start | bytes 1048576 | tf_op jit(solution)/shard_map/all_to_all | solution.py:482
  13.3 2.3 %shard_map.128 = (bf16[144,1024]{1,0:T(8,128)(2,1)}, bf16[144,512]{1,0:T(8,128)(2,1)}) custom-call(s32[1]{0:T(128)} %bitcast.1.core_ref, bf16[128,1024]{1,0:T(8,128)(2,1)} %bitcast.16, bf16[4,1024]{1,0:T(4,128)(2,1)} %bitcast.23, bf16[144,512]{1,0:T(8,128)(2,1)} %get-tuple-element.50.att_hbm), custom_call_target="tpu_custom_call" | custom-call | flops 1000 | bytes 1000 | tf_op jit(solution)/shard_map/pallas_call | solution.py:428
  15.6 0.4 collective-permute-start
  16.0 1.6 %collective-permute-done.refs_2_ = bf16[144,1024]{1,0:T(8,128)(2,1)} collective-permute-done((bf16[144,1024]{1,0:T(8,128)(2,1)}, bf16[144,1024]{1,0:T(8,128)(2,1)}, u32[]{:S(2)}, u32[]{:S(2)}) %collective-permute-start) | collective-permute-done | bytes 294944 | tf_op jit(solution)/shard_map/ppermute | solution.py:513
  17.6 8.1 %all-to-all-done = bf16[16,8,2048]{2,1,0:T(8,128)(2,1)} async-done(((bf16[16,8,2048]{2,1,0:T(8,128)(2,1)}), bf16[16,8,2048]{2,1,0:T(8,128)(2,1)}, u32[]{:S(2)}, u32[]{:S(2)}) %all-to-all-start) | async-done | bytes 524320 | tf_op jit(solution)/shard_map/all_to_all | solution.py:482
  25.7 5.6 %shard_map.129 = (bf16[128,1024]{1,0:T(8,128)(2,1)}, bf16[128,3072]{1,0:T(8,128)(2,1)}, bf16[128,1024]{1,0:T(8,128)(2,1)}) custom-call(s32[1]{0:T(128)} %bitcast.1.core_ref, bf16[128,2048]{1,0:T(8,128)(2,1)} %bitcast.5.moved_hbm, bf16[1024,1536]{1,0:T(8,128)(2,1)} %entry_hbm.5, bf16[1024,512]{1,0:T(8,128)(2,1)} %exit_hbm.4), custom_call_target="tpu_custom_call" | custom-call | flops 1000 | bytes 1000 | tf_op jit(solution)/shard_map/pallas_call | solution.py:428
  31.3 0.1 collective-permute-start.1
  31.4 4.2 %all-to-all-start.1 = ((bf16[16,8,1024]{2,1,0:T(8,128)(2,1)}), bf16[16,8,1024]{2,1,0:T(8,128)(2,1)}, u32[]{:S(2)}, u32[]{:S(2)}) async-start(bf16[16,8,1024]{2,1,0:T(8,128)(2,1)} %bitcast.21), calls=%async_computation.1 | async-start | bytes 524288 | tf_op jit(solution)/shard_map/all_to_all | solution.py:482
  35.6 0.6 pad_add_fusion.place_ref
  36.2 0.0 collective-permute-done.1.refs_2_
  36.2 3.9 %shard_map.130 = (bf16[128,2048]{1,0:T(8,128)(2,1)}, bf16[128,2048]{1,0:T(8,128)(2,1)}, bf16[128,2048]{1,0:T(8,128)(2,1)}, bf16[128,2048]{1,0:T(8,128)(2,1)}) custom-call(s32[2]{0:T(128)} %pad_add_fusion.place_ref, bf16[128,1024]{1,0:T(8,128)(2,1)} %get-tuple-element.54.refs_0_, bf16[128,3072]{1,0:T(8,128)(2,1)} %get-tuple-element.55.refs_1_, ...), custom_call_target="tpu_custom_call" | custom-call | flops 1000 | bytes 1000 | tf_op jit(solution)/shard_map/pallas_call | solution.py:428
  40.1 1.5 %collective-permute-start.4 = (bf16[128,2048]{1,0:T(8,128)(2,1)}, bf16[128,2048]{1,0:T(8,128)(2,1)}, u32[]{:S(2)}, u32[]{:S(2)}) collective-permute-start(bf16[128,2048]{1,0:T(8,128)(2,1)} %get-tuple-element.70), channel_id=1, source_target_pairs={{0,16},{1,5},{2,18},{3,7},{4,20},{5,9},{6,22},{7,11},{8,24},{9,13}... | collective-permute-start | bytes 1572872 | tf_op jit(solution)/shard_map/ppermute | solution.py:549
  41.7 1.8 %collective-permute-start.5 = (bf16[128,2048]{1,0:T(8,128)(2,1)}, bf16[128,2048]{1,0:T(8,128)(2,1)}, u32[]{:S(2)}, u32[]{:S(2)}) collective-permute-start(bf16[128,2048]{1,0:T(8,128)(2,1)} %get-tuple-element.71), channel_id=1, source_target_pairs={{0,48},{1,13},{2,50},{3,15},{4,52},{5,1},{6,54},{7,3},{8,56},{9,5}... | collective-permute-start | bytes 1572872 | tf_op jit(solution)/shard_map/ppermute | solution.py:549
  43.4 1.8 %collective-permute-start.6 = (bf16[128,2048]{1,0:T(8,128)(2,1)}, bf16[128,2048]{1,0:T(8,128)(2,1)}, u32[]{:S(2)}, u32[]{:S(2)}) collective-permute-start(bf16[128,2048]{1,0:T(8,128)(2,1)} %get-tuple-element.72), channel_id=1, source_target_pairs={{0,32},{1,9},{2,34},{3,11},{4,36},{5,13},{6,38},{7,15},{8,40},{9,1... | collective-permute-start | bytes 1572872 | tf_op jit(solution)/shard_map/ppermute | solution.py:549
  45.2 0.0 all-to-all-done.1
  45.2 4.0 %shard_map.131 = (bf16[144,512]{1,0:T(8,128)(2,1)}, bf16[144,512]{1,0:T(8,128)(2,1)}, bf16[144,1536]{1,0:T(8,128)(2,1)}) custom-call(s32[1]{0:T(128)} %bitcast.1.core_ref, bf16[128,1024]{1,0:T(8,128)(2,1)} %bitcast.7.back_hbm, bf16[4,1024]{1,0:T(4,128)(2,1)} %bitcast.25, bf16[144,1536]{1,0:T(8,128)(2,1)} %get-tuple-element.58.mix_hbm, ...), custom_call_target="tpu_custom_call" | custom-call | flops 1000 | bytes 1000 | tf_op jit(solution)/shard_map/pallas_call | solution.py:428
  49.2 0.1 collective-permute-start.3
  49.3 0.5 collective-permute-start.2
  49.8 1.8 %collective-permute-done.2.refs_4_ = bf16[144,512]{1,0:T(8,128)(2,1)} collective-permute-done((bf16[144,512]{1,0:T(8,128)(2,1)}, bf16[144,512]{1,0:T(8,128)(2,1)}, u32[]{:S(2)}, u32[]{:S(2)}) %collective-permute-start.2) | collective-permute-done | bytes 147488 | tf_op jit(solution)/shard_map/ppermute | solution.py:576
  51.7 0.0 collective-permute-done.3.refs_6_
  51.7 4.4 %shard_map.132 = (bf16[128,2048]{1,0:T(8,128)(2,1)}, bf16[128,2048]{1,0:T(8,128)(2,1)}, bf16[128,2048]{1,0:T(8,128)(2,1)}, bf16[128,2048]{1,0:T(8,128)(2,1)}) custom-call(s32[2]{0:T(128)} %pad_add_fusion.place_ref, bf16[144,512]{1,0:T(8,128)(2,1)} %get-tuple-element.61.refs_0_, bf16[144,1024]{1,0:T(8,128)(2,1)} %get-tuple-element.51.refs_1_, ...), custom_call_target="tpu_custom_call" | custom-call | flops 1000 | bytes 1000 | tf_op jit(solution)/shard_map/pallas_call | solution.py:428
  56.0 0.0 collective-permute-done.4.a_hbm
  56.0 0.1 collective-permute-done.5.b_hbm
  56.1 1.4 %collective-permute-done.6.c_hbm = bf16[128,2048]{1,0:T(8,128)(2,1)} collective-permute-done((bf16[128,2048]{1,0:T(8,128)(2,1)}, bf16[128,2048]{1,0:T(8,128)(2,1)}, u32[]{:S(2)}, u32[]{:S(2)}) %collective-permute-start.6) | collective-permute-done | bytes 524320 | tf_op jit(solution)/shard_map/ppermute | solution.py:549
  57.5 1.4 %collective-permute-start.8 = (bf16[128,2048]{1,0:T(8,128)(2,1)}, bf16[128,2048]{1,0:T(8,128)(2,1)}, u32[]{:S(2)}, u32[]{:S(2)}) collective-permute-start(bf16[128,2048]{1,0:T(8,128)(2,1)} %get-tuple-element.75), channel_id=1, source_target_pairs={{0,16},{1,5},{2,18},{3,7},{4,20},{5,9},{6,22},{7,11},{8,24},{9,13}... | collective-permute-start | bytes 1572872 | tf_op jit(solution)/shard_map/ppermute | solution.py:549
  58.9 1.8 %collective-permute-start.9 = (bf16[128,2048]{1,0:T(8,128)(2,1)}, bf16[128,2048]{1,0:T(8,128)(2,1)}, u32[]{:S(2)}, u32[]{:S(2)}) collective-permute-start(bf16[128,2048]{1,0:T(8,128)(2,1)} %get-tuple-element.76), channel_id=1, source_target_pairs={{0,48},{1,13},{2,50},{3,15},{4,52},{5,1},{6,54},{7,3},{8,56},{9,5}... | collective-permute-start | bytes 1572872 | tf_op jit(solution)/shard_map/ppermute | solution.py:549
  60.7 0.5 collective-permute-start.10
  61.2 3.6 %shard_map.133 = f32[4,1024]{1,0:T(4,128)} custom-call(bf16[4,1024]{1,0:T(4,128)(2,1)} %bitcast.24, bf16[4,1024]{1,0:T(4,128)(2,1)} %bitcast.26, bf16[144,1536]{1,0:T(8,128)(2,1)} %get-tuple-element.78.refs_5_.d_mix_hbm, bf16[1024,1536]{1,0:T(8,128)(2,1)} %entry_hbm.7), custom_call_target="tpu_custom_call" | custom-call | flops 1000 | bytes 1000 | tf_op jit(solution)/shard_map/pallas_call | solution.py:428
  64.8 0.0 copy-start
  64.8 3.3 %collective-permute-start.7 = (f32[4,1024]{1,0:T(4,128)}, f32[4,1024]{1,0:T(4,128)S(1)}, u32[]{:S(2)}, u32[]{:S(2)}) collective-permute-start(f32[4,1024]{1,0:T(4,128)} %shard_map.133), channel_id=1, source_target_pairs={{0,2},{2,0},{1,3},{3,1},{4,6},{6,4},{5,7},{7,5},{8,10},{10,8},{9,1... | collective-permute-start | bytes 49160 | tf_op jit(solution)/shard_map/ppermute | solution.py:603
  68.1 2.5 %shard_map.135.refs_0_ = bf16[128,4096]{1,0:T(8,128)(2,1)} custom-call(bf16[128,2048]{1,0:T(8,128)(2,1)} %get-tuple-element.84.own_hbm, bf16[128,2048]{1,0:T(8,128)(2,1)} %collective-permute-done.4.a_hbm, bf16[128,2048]{1,0:T(8,128)(2,1)} %collective-permute-done.5.b_hbm, bf16[128,2048]{1,0:T(8,128)(2,1)} %collective-permute-done.6.c_hbm), custom_call_target="tpu_custom_call" | custom-call | flops 1000 | bytes 1000 | tf_op jit(solution)/shard_map/pallas_call | solution.py:428
  70.7 0.0 collective-permute-done.7
  70.7 0.0 copy-done
  70.7 0.0 collective-permute-done.8.a_hbm
  70.7 2.7 %collective-permute-done.9.b_hbm = bf16[128,2048]{1,0:T(8,128)(2,1)} collective-permute-done((bf16[128,2048]{1,0:T(8,128)(2,1)}, bf16[128,2048]{1,0:T(8,128)(2,1)}, u32[]{:S(2)}, u32[]{:S(2)}) %collective-permute-start.9) | collective-permute-done | bytes 524320 | tf_op jit(solution)/shard_map/ppermute | solution.py:549
  73.4 0.9 collective-permute-done.10.c_hbm
  74.3 2.5 %shard_map.136 = bf16[128,4096]{1,0:T(8,128)(2,1)} custom-call(bf16[128,2048]{1,0:T(8,128)(2,1)} %get-tuple-element.80.own_hbm, bf16[128,2048]{1,0:T(8,128)(2,1)} %collective-permute-done.8.a_hbm, bf16[128,2048]{1,0:T(8,128)(2,1)} %collective-permute-done.9.b_hbm, bf16[128,2048]{1,0:T(8,128)(2,1)} %collective-permute-done.10.c_hbm, ...), custom_call_target="tpu_custom_call", output_to_operand_aliasing={{}: (4, {})} | custom-call | flops 1000 | bytes 1000 | tf_op jit(solution)/shard_map/pallas_call | solution.py:428
  76.8 7.3 %all-to-all-start.2 = ((bf16[16,8,4096]{2,1,0:T(8,128)(2,1)}), bf16[16,8,4096]{2,1,0:T(8,128)(2,1)}, u32[]{:S(2)}, u32[]{:S(2)}) async-start(bf16[16,8,4096]{2,1,0:T(8,128)(2,1)} %bitcast.14), calls=%async_computation.2 | async-start | bytes 2097152 | tf_op jit(solution)/shard_map/all_to_all | solution.py:642
  84.1 0.1 collective-permute-start.11
  84.2 1.2 %collective-permute-done.11 = f32[4,1024]{1,0:T(4,128)S(1)} collective-permute-done((f32[4,1024]{1,0:T(4,128)S(1)}, f32[4,1024]{1,0:T(4,128)S(1)}, u32[]{:S(2)}, u32[]{:S(2)}) %collective-permute-start.11) | collective-permute-done | bytes 16416 | tf_op jit(solution)/shard_map/ppermute | solution.py:603
  85.4 3.0 %collective-permute-start.12 = (f32[4,1024]{1,0:T(4,128)S(1)}, f32[4,1024]{1,0:T(4,128)S(1)}, u32[]{:S(2)}, u32[]{:S(2)}) collective-permute-start(f32[4,1024]{1,0:T(4,128)S(1)} %add.33), channel_id=1, source_target_pairs={{0,12},{4,0},{8,4},{12,8},{1,13},{5,1},{9,5},{13,9},{2,14},{6,2},{... | collective-permute-start | bytes 49160 | tf_op jit(solution)/shard_map/ppermute | solution.py:621
  88.4 0.9 collective-permute-start.13
  89.3 0.9 collective-permute-start.14
  90.1 4.2 %shard_map.134 = bf16[128,1024]{1,0:T(8,128)(2,1)} custom-call(bf16[128,1024]{1,0:T(8,128)(2,1)} %bitcast.17, bf16[128,1024]{1,0:T(8,128)(2,1)} %bitcast.7.back_hbm, bf16[144,1536]{1,0:T(8,128)(2,1)} %get-tuple-element.78.refs_5_.d_mix_hbm, bf16[1024,1536]{1,0:T(8,128)(2,1)} %entry_hbm.7), custom_call_target="tpu_custom_call" | custom-call | flops 1000 | bytes 1000 | tf_op jit(solution)/shard_map/pallas_call | solution.py:428
  94.3 0.0 collective-permute-done.12
  94.3 1.2 %collective-permute-done.13 = f32[4,1024]{1,0:T(4,128)S(1)} collective-permute-done((f32[4,1024]{1,0:T(4,128)S(1)}, f32[4,1024]{1,0:T(4,128)S(1)}, u32[]{:S(2)}, u32[]{:S(2)}) %collective-permute-start.13) | collective-permute-done | bytes 16416 | tf_op jit(solution)/shard_map/ppermute | solution.py:621
  95.6 0.1 collective-permute-done.14
  95.6 0.6 fusion
  96.3 2.6 %all-to-all-done.2.parts_hbm = bf16[16,8,4096]{2,1,0:T(8,128)(2,1)} async-done(((bf16[16,8,4096]{2,1,0:T(8,128)(2,1)}), bf16[16,8,4096]{2,1,0:T(8,128)(2,1)}, u32[]{:S(2)}, u32[]{:S(2)}) %all-to-all-start.2) | async-done | bytes 1048608 | tf_op jit(solution)/shard_map/all_to_all | solution.py:642
  98.9 2.0 %shard_map.137 = (bf16[8,1536]{1,0:T(8,128)(2,1)}, bf16[8,512]{1,0:T(8,128)(2,1)}, bf16[8,1536]{1,0:T(8,128)(2,1)}, bf16[8,512]{1,0:T(8,128)(2,1)}) custom-call(bf16[16,8,4096]{2,1,0:T(8,128)(2,1)} %all-to-all-done.2.parts_hbm), custom_call_target="tpu_custom_call" | custom-call | flops 1000 | bytes 1000 | tf_op jit(solution)/shard_map/pallas_call | solution.py:428
  (2 shorter events, 0.0 us)
Async XLA Ops:
  5.2 20.5 %all-to-all-start = ((bf16[16,8,2048]{2,1,0:T(8,128)(2,1)}), bf16[16,8,2048]{2,1,0:T(8,128)(2,1)}, u32[]{:S(2)}, u32[]{:S(2)}) async-start(bf16[16,8,2048]{2,1,0:T(8,128)(2,1)} %bitcast.18), calls=%async_computation | async-start | bytes 1048576 | tf_op jit(solution)/shard_map/all_to_all | solution.py:482
  15.6 2.0 %collective-permute-start = (bf16[144,1024]{1,0:T(8,128)(2,1)}, bf16[144,1024]{1,0:T(8,128)(2,1)}, u32[]{:S(2)}, u32[]{:S(2)}) collective-permute-start(bf16[144,1024]{1,0:T(8,128)(2,1)} %get-tuple-element.51.refs_1_), channel_id=1, source_target_pairs={{0,1},{1,0},{2,3},{3,2},{4,5},{5,4},{6,7},{7,6},{8,9},{9,8},{10,11... | collective-permute-start | bytes 884744 | tf_op jit(solution)/shard_map/ppermute | solution.py:513
  31.3 4.9 %collective-permute-start.1 = (bf16[128,3072]{1,0:T(8,128)(2,1)}, bf16[128,3072]{1,0:T(8,128)(2,1)}, u32[]{:S(2)}, u32[]{:S(2)}) collective-permute-start(bf16[128,3072]{1,0:T(8,128)(2,1)} %get-tuple-element.55.refs_1_), channel_id=1, source_target_pairs={{0,1},{1,0},{2,3},{3,2},{4,5},{5,4},{6,7},{7,6},{8,9},{9,8},{10,11... | collective-permute-start | bytes 2359304 | tf_op jit(solution)/shard_map/ppermute | solution.py:531
  31.4 13.8 %all-to-all-start.1 = ((bf16[16,8,1024]{2,1,0:T(8,128)(2,1)}), bf16[16,8,1024]{2,1,0:T(8,128)(2,1)}, u32[]{:S(2)}, u32[]{:S(2)}) async-start(bf16[16,8,1024]{2,1,0:T(8,128)(2,1)} %bitcast.21), calls=%async_computation.1 | async-start | bytes 524288 | tf_op jit(solution)/shard_map/all_to_all | solution.py:482
  40.1 15.9 %collective-permute-start.4 = (bf16[128,2048]{1,0:T(8,128)(2,1)}, bf16[128,2048]{1,0:T(8,128)(2,1)}, u32[]{:S(2)}, u32[]{:S(2)}) collective-permute-start(bf16[128,2048]{1,0:T(8,128)(2,1)} %get-tuple-element.70), channel_id=1, source_target_pairs={{0,16},{1,5},{2,18},{3,7},{4,20},{5,9},{6,22},{7,11},{8,24},{9,13}... | collective-permute-start | bytes 1572872 | tf_op jit(solution)/shard_map/ppermute | solution.py:549
  41.7 14.4 %collective-permute-start.5 = (bf16[128,2048]{1,0:T(8,128)(2,1)}, bf16[128,2048]{1,0:T(8,128)(2,1)}, u32[]{:S(2)}, u32[]{:S(2)}) collective-permute-start(bf16[128,2048]{1,0:T(8,128)(2,1)} %get-tuple-element.71), channel_id=1, source_target_pairs={{0,48},{1,13},{2,50},{3,15},{4,52},{5,1},{6,54},{7,3},{8,56},{9,5}... | collective-permute-start | bytes 1572872 | tf_op jit(solution)/shard_map/ppermute | solution.py:549
  43.4 14.0 %collective-permute-start.6 = (bf16[128,2048]{1,0:T(8,128)(2,1)}, bf16[128,2048]{1,0:T(8,128)(2,1)}, u32[]{:S(2)}, u32[]{:S(2)}) collective-permute-start(bf16[128,2048]{1,0:T(8,128)(2,1)} %get-tuple-element.72), channel_id=1, source_target_pairs={{0,32},{1,9},{2,34},{3,11},{4,36},{5,13},{6,38},{7,15},{8,40},{9,1... | collective-permute-start | bytes 1572872 | tf_op jit(solution)/shard_map/ppermute | solution.py:549
  49.2 2.4 %collective-permute-start.3 = (bf16[144,1536]{1,0:T(8,128)(2,1)}, bf16[144,1536]{1,0:T(8,128)(2,1)}, u32[]{:S(2)}, u32[]{:S(2)}) collective-permute-start(bf16[144,1536]{1,0:T(8,128)(2,1)} %get-tuple-element.78.refs_5_.d_mix_hbm), channel_id=1, source_target_pairs={{0,1},{1,0},{2,3},{3,2},{4,5},{5,4},{6,7},{7,6},{8,9},{9,8},{10,11... | collective-permute-start | bytes 1327112 | tf_op jit(solution)/shard_map/ppermute | solution.py:577
  49.3 2.3 %collective-permute-start.2 = (bf16[144,512]{1,0:T(8,128)(2,1)}, bf16[144,512]{1,0:T(8,128)(2,1)}, u32[]{:S(2)}, u32[]{:S(2)}) collective-permute-start(bf16[144,512]{1,0:T(8,128)(2,1)} %get-tuple-element.64), channel_id=1, source_target_pairs={{0,1},{1,0},{2,3},{3,2},{4,5},{5,4},{6,7},{7,6},{8,9},{9,8},{10,11... | collective-permute-start | bytes 442376 | tf_op jit(solution)/shard_map/ppermute | solution.py:576
  57.5 13.2 %collective-permute-start.8 = (bf16[128,2048]{1,0:T(8,128)(2,1)}, bf16[128,2048]{1,0:T(8,128)(2,1)}, u32[]{:S(2)}, u32[]{:S(2)}) collective-permute-start(bf16[128,2048]{1,0:T(8,128)(2,1)} %get-tuple-element.75), channel_id=1, source_target_pairs={{0,16},{1,5},{2,18},{3,7},{4,20},{5,9},{6,22},{7,11},{8,24},{9,13}... | collective-permute-start | bytes 1572872 | tf_op jit(solution)/shard_map/ppermute | solution.py:549
  58.9 14.5 %collective-permute-start.9 = (bf16[128,2048]{1,0:T(8,128)(2,1)}, bf16[128,2048]{1,0:T(8,128)(2,1)}, u32[]{:S(2)}, u32[]{:S(2)}) collective-permute-start(bf16[128,2048]{1,0:T(8,128)(2,1)} %get-tuple-element.76), channel_id=1, source_target_pairs={{0,48},{1,13},{2,50},{3,15},{4,52},{5,1},{6,54},{7,3},{8,56},{9,5}... | collective-permute-start | bytes 1572872 | tf_op jit(solution)/shard_map/ppermute | solution.py:549
  60.7 13.6 %collective-permute-start.10 = (bf16[128,2048]{1,0:T(8,128)(2,1)}, bf16[128,2048]{1,0:T(8,128)(2,1)}, u32[]{:S(2)}, u32[]{:S(2)}) collective-permute-start(bf16[128,2048]{1,0:T(8,128)(2,1)} %get-tuple-element.77), channel_id=1, source_target_pairs={{0,32},{1,9},{2,34},{3,11},{4,36},{5,13},{6,38},{7,15},{8,40},{9,1... | collective-permute-start | bytes 1572872 | tf_op jit(solution)/shard_map/ppermute | solution.py:549
  64.8 5.9 %copy-start = (f32[4,1024]{1,0:T(4,128)S(1)}, f32[4,1024]{1,0:T(4,128)}, u32[]{:S(2)}) copy-start(f32[4,1024]{1,0:T(4,128)} %shard_map.133) | copy-start | bytes 49156
  64.8 5.9 %collective-permute-start.7 = (f32[4,1024]{1,0:T(4,128)}, f32[4,1024]{1,0:T(4,128)S(1)}, u32[]{:S(2)}, u32[]{:S(2)}) collective-permute-start(f32[4,1024]{1,0:T(4,128)} %shard_map.133), channel_id=1, source_target_pairs={{0,2},{2,0},{1,3},{3,1},{4,6},{6,4},{5,7},{7,5},{8,10},{10,8},{9,1... | collective-permute-start | bytes 49160 | tf_op jit(solution)/shard_map/ppermute | solution.py:603
  76.8 22.0 %all-to-all-start.2 = ((bf16[16,8,4096]{2,1,0:T(8,128)(2,1)}), bf16[16,8,4096]{2,1,0:T(8,128)(2,1)}, u32[]{:S(2)}, u32[]{:S(2)}) async-start(bf16[16,8,4096]{2,1,0:T(8,128)(2,1)} %bitcast.14), calls=%async_computation.2 | async-start | bytes 2097152 | tf_op jit(solution)/shard_map/all_to_all | solution.py:642
  84.1 1.3 %collective-permute-start.11 = (f32[4,1024]{1,0:T(4,128)S(1)}, f32[4,1024]{1,0:T(4,128)S(1)}, u32[]{:S(2)}, u32[]{:S(2)}) collective-permute-start(f32[4,1024]{1,0:T(4,128)S(1)} %add.31), channel_id=1, source_target_pairs={{0,1},{1,0},{2,3},{3,2},{4,5},{5,4},{6,7},{7,6},{8,9},{9,8},{10,11... | collective-permute-start | bytes 49160 | tf_op jit(solution)/shard_map/ppermute | solution.py:603
  85.4 8.9 %collective-permute-start.12 = (f32[4,1024]{1,0:T(4,128)S(1)}, f32[4,1024]{1,0:T(4,128)S(1)}, u32[]{:S(2)}, u32[]{:S(2)}) collective-permute-start(f32[4,1024]{1,0:T(4,128)S(1)} %add.33), channel_id=1, source_target_pairs={{0,12},{4,0},{8,4},{12,8},{1,13},{5,1},{9,5},{13,9},{2,14},{6,2},{... | collective-permute-start | bytes 49160 | tf_op jit(solution)/shard_map/ppermute | solution.py:621
  88.4 7.1 %collective-permute-start.13 = (f32[4,1024]{1,0:T(4,128)S(1)}, f32[4,1024]{1,0:T(4,128)S(1)}, u32[]{:S(2)}, u32[]{:S(2)}) collective-permute-start(f32[4,1024]{1,0:T(4,128)S(1)} %add.33), channel_id=1, source_target_pairs={{0,8},{4,12},{8,0},{12,4},{1,9},{5,13},{9,1},{13,5},{2,10},{6,14},... | collective-permute-start | bytes 49160 | tf_op jit(solution)/shard_map/ppermute | solution.py:621
  89.3 6.4 %collective-permute-start.14 = (f32[4,1024]{1,0:T(4,128)S(1)}, f32[4,1024]{1,0:T(4,128)S(1)}, u32[]{:S(2)}, u32[]{:S(2)}) collective-permute-start(f32[4,1024]{1,0:T(4,128)S(1)} %add.33), channel_id=1, source_target_pairs={{0,4},{4,8},{8,12},{12,0},{1,5},{5,9},{9,13},{13,1},{2,6},{6,10},{... | collective-permute-start | bytes 49160 | tf_op jit(solution)/shard_map/ppermute | solution.py:621
